TPU v7x, 256 devices: a whole 4x4x8 slice. The times are simulated.
256 devices in a mesh: seq: 32 (over z, x), exp: 8 (over y, core).
Axes of the slice: x: 4, y: 4, z: 8, core: 2. Of those that a mesh axis runs over, the one named last changes fastest.
Arguments:
- x_resid: bfloat16 [16384, 2048], P(('seq', 'exp')), may hold values from -36 to 36
- queries: bfloat16 [16384, 2048], P('seq', 'exp'), may hold values from -6 to 6
- key_proj: bfloat16 [16384, 2048], P('seq', 'exp'), may hold values from -6 to 6
- val_proj: bfloat16 [16384, 2048], P('seq', 'exp'), may hold values from -6 to 6
- w_out: bfloat16 [2048, 2048], P('exp'), may hold values from -0.125 to 0.125
- norm_gain: float32 [2048], replicated, may hold values from 0.1 to 1.9
- w_gate: bfloat16 [8, 2048, 1408], P('exp', 'seq'), may hold values from -0.125 to 0.125
- w_up: bfloat16 [8, 2048, 1408], P('exp', 'seq'), may hold values from -0.125 to 0.125
- w_down: bfloat16 [8, 1408, 2048], P('exp', None, 'seq'), may hold values from -0.15625 to 0.15625
- routes: int32 [16384, 2], P(('seq', 'exp')), may hold values from 0 to 7, all different within a row; in each aligned block of 64 rows (0 to 63, 64 to 127, ...) at most 18 rows name the same one
- gate_prob: float32 [16384, 2], P(('seq', 'exp')), may hold values from 0.05 to 0.6
- grad_out: bfloat16 [16384, 2048], P(('seq', 'exp')), may hold values from -6 to 6
Outputs:
- layer_out: bfloat16 [16384, 2048], P(('seq', 'exp'))
- grad_in: bfloat16 [16384, 2048], P(('seq', 'exp'))
- grad_gate: float32 [16384, 2], P(('seq', 'exp'))
Inputs may be any that keep to these rules, and one draw needn't show every extreme that they name: `routes`: in each aligned block of 64 tokens (the tokens of one device) no expert is named by more than 18 rows, a bound that some block reaches; a token's two experts differ.
All inputs are finite; a program needn't handle non-finite values.
Results may differ from a plain program's by a relative error of at most 0.024.
Values may be sent and summed in bfloat16 or wider, within the bound.
No kernel may reach another device: no remote copies, remote signals or barrier semaphores. Data moves between devices by JAX's collectives and lax.ppermute only.
A program may use at most 128 MiB of HBM per device.

v0:
```python
import functools
import math

import jax
import jax.numpy as jnp
from jax import lax
from jax.experimental import pallas as pl
from jax.experimental.pallas import tpu as pltpu
from jax.sharding import PartitionSpec as P

HD = 128
W = 2048
CAP = 18
SLOT = 24
BACK = 40
NZ = 8
NX = 4
NY = 4
norm_eps = 1e-06
F32 = jnp.float32
BF16 = jnp.bfloat16
VMEM = pl.BlockSpec(memory_space=pltpu.VMEM)
SMEM = pl.BlockSpec(memory_space=pltpu.SMEM)
HBM = pl.BlockSpec(memory_space=pltpu.HBM)


def params(mib):
    return pltpu.CompilerParams(vmem_limit_bytes=mib * 2**20)


def nt(a, b):
    return lax.dot_general(a, b, (((1,), (1,)), ((), ())), preferred_element_type=F32)


def nn(a, b):
    return jnp.dot(a, b, preferred_element_type=F32)


def shift_zx(block, dz, dx):
    route = [(s, ((s // NX + dz) % NZ) * NX + (s % NX + dx) % NX) for s in range(NZ * NX)]
    return lax.ppermute(block, "seq", route)


def along_z(block, d):
    return shift_zx(block, d, 0)


def along_x(block, d):
    return shift_zx(block, 0, d)


def along_y(block, d):
    return lax.ppermute(block, "exp", [(i, (i + 2 * d) % (2 * NY)) for i in range(2 * NY)])


def swap_core(block):
    return lax.ppermute(block, "exp", [(i, i ^ 1) for i in range(2 * NY)])


def after(value, *earlier):
    return lax.optimization_barrier((value, earlier))[0]


def opposite(ahead, behind, cut, move):
    return [move(ahead[:cut], 1), move(behind[cut:], -1)]


def to_earlier(own):
    x = lax.axis_index("seq") % NX
    above = along_z(own, 1)
    return above, (
        jnp.where(x == NX - 1, above, own),
        jnp.where(x < 2, own, above),
        jnp.where(x == 0, own, above),
    )


def earlier_shards(above, loads):
    return [along_x(loads[0], 1), along_x(loads[1], 2), along_x(loads[2], -1), above]


def attention_kernel(where, q, k0, k1, k2, k3, k4, v0, v1, v2, v3, v4, out):
    keys, vals = (k0, k1, k2, k3, k4), (v0, v1, v2, v3, v4)
    rows, span = 128, k0.shape[0]
    scale = 1.0 / math.sqrt(HD)
    seq = where[0]

    def block(i, _):
        at = pl.multiple_of(i * rows, rows)
        qpos = at + lax.broadcasted_iota(jnp.int32, (rows, span), 0)
        kpos = lax.broadcasted_iota(jnp.int32, (rows, span), 1)
        for h in range(out.shape[1] // HD):
            cols = slice(h * HD, (h + 1) * HD)
            queries = q[pl.ds(at, rows), cols]
            scores = []
            for d in range(5):
                s = nt(queries, keys[d][:, cols]) * scale
                if d == 0:
                    s = jnp.where(kpos <= qpos, s, -jnp.inf)
                elif d == 4:
                    s = jnp.where((kpos > qpos) & (seq >= d), s, -jnp.inf)
                else:
                    s = jnp.where(seq >= d, s, -jnp.inf)
                scores.append(s)
            top = scores[0]
            for s in scores[1:]:
                top = jnp.maximum(top, s)
            top = jnp.max(top, axis=-1, keepdims=True)
            mixed = jnp.zeros((rows, HD), F32)
            total = jnp.zeros((rows, span), F32)
            for d in range(5):
                e = jnp.exp(scores[d] - top)
                total = total + e
                mixed = mixed + nn(e.astype(BF16), vals[d][:, cols])
            out[pl.ds(at, rows), cols] = (mixed / jnp.sum(total, axis=-1, keepdims=True)).astype(BF16)
        return 0

    lax.fori_loop(0, q.shape[0] // rows, block, 0)


def attention(where, q, keys, vals):
    return pl.pallas_call(
        attention_kernel,
        out_shape=jax.ShapeDtypeStruct(q.shape, BF16),
        in_specs=[SMEM] + [VMEM] * 11,
        out_specs=VMEM,
        compiler_params=params(24),
        cost_estimate=pl.CostEstimate(flops=4 * 512 * 2560 * 256, bytes_accessed=6 * 2**20, transcendentals=512 * 2560 * 2),
    )(where, q, *keys, *vals)


def gather_rows(rows, earlier):
    count = rows.shape[0]
    plane = jnp.concatenate([rows, along_x(rows, 1), along_x(rows, 2), along_x(rows, -1)], axis=0)
    plane = after(plane, earlier)
    pieces = [(plane, 0)]
    ahead, behind = plane, plane
    for dz in (1, 2, 3):
        ahead, behind = along_z(ahead, 1), along_z(behind, -1)
        pieces += [(ahead, dz), (behind, NZ - dz)]
    listed = [[(dx * count, dz, dx) for dx in range(NX)] for _, dz in pieces]
    far = opposite(ahead, behind, NX // 2 * count, along_z)
    listed += [[(dx % 2 * count, NZ // 2, dx) for dx in pair] for pair in ((0, 1), (2, 3))]
    return [p for p, _ in pieces] + far, listed


def project_kernel(where, own, sib, w_own, w_sib, out):
    for d in range(NY):
        y = lax.rem(where[0] + d, NY)
        out[d] = (nn(own[y], w_own[...]) + nn(sib[y], w_sib[...])).astype(BF16)


def project(where, own, sib, w_own, w_sib):
    return pl.pallas_call(
        project_kernel,
        out_shape=jax.ShapeDtypeStruct((NY, own.shape[1], w_own.shape[1]), BF16),
        in_specs=[pl.BlockSpec(memory_space=pltpu.SMEM)] + [VMEM] * 4,
        out_specs=VMEM,
        compiler_params=params(24),
        cost_estimate=pl.CostEstimate(flops=2 * 256 * 512 * 2048, bytes_accessed=6 * 2**20, transcendentals=0),
    )(where, own, sib, w_own, w_sib)


def slots_of(target_rows, slots, tokens):
    at = lax.broadcasted_iota(jnp.int32, (slots, tokens), 0)
    hit = (at == target_rows[0:1, :]) | (at == target_rows[1:2, :])
    return jnp.where(hit, 1.0, 0.0).astype(BF16)


def norm_kernel(x, p0, p1, p2, p3, gain, target_rows, hidden, send):
    total = p0[...].astype(F32) + p1[...].astype(F32) + p2[...].astype(F32) + p3[...].astype(F32)
    state = (x[...].astype(F32) + total).astype(BF16)
    hidden[...] = state
    wide = state.astype(F32)
    rstd = lax.rsqrt(jnp.mean(wide * wide, axis=-1, keepdims=True) + norm_eps)
    moe_in = (wide * rstd * gain[...]).astype(BF16)
    place = slots_of(target_rows, send.shape[0], x.shape[0])
    send[...] = nn(place, moe_in).astype(BF16)


def norm_dispatch(x, parts, gain, target_rows, slots):
    tokens, width = x.shape
    return pl.pallas_call(
        norm_kernel,
        out_shape=(
            jax.ShapeDtypeStruct((tokens, width), BF16),
            jax.ShapeDtypeStruct((slots, width), BF16),
        ),
        in_specs=[VMEM] * 7,
        out_specs=(VMEM, VMEM),
        compiler_params=params(24),
        cost_estimate=pl.CostEstimate(flops=2 * slots * tokens * width, bytes_accessed=3 * 2**20, transcendentals=0),
    )(x, *parts, gain, target_rows)


def scatter_kernel(rows, target_rows, send):
    place = slots_of(target_rows, send.shape[0], rows.shape[0])
    send[...] = nn(place, rows[...]).astype(BF16)


def scatter_rows(rows, target_rows, slots):
    return pl.pallas_call(
        scatter_kernel,
        out_shape=jax.ShapeDtypeStruct((slots, rows.shape[1]), BF16),
        in_specs=[VMEM] * 2,
        out_specs=VMEM,
        compiler_params=params(16),
        cost_estimate=pl.CostEstimate(flops=2 * slots * 64 * 2048, bytes_accessed=2**20, transcendentals=0),
    )(rows, target_rows)


def down_kernel(runs, where, rows_grad, *refs):
    pieces, (wd, back, sem) = refs[: len(runs)], refs[len(runs) :]
    seq = where[0]
    z, x = seq // NX, lax.rem(seq, NX)
    part = wd.shape[0] // (NZ * NX)
    for piece, listed in zip(pieces, runs):
        for first, dz, dx in listed:
            source = lax.rem(z + NZ - dz, NZ) * NX + lax.rem(x + NX - dx, NX)
            row = pl.multiple_of(source * part, part)
            pltpu.make_async_copy(piece.at[pl.ds(first, part)], wd.at[pl.ds(row, part)], sem).start()
    pltpu.make_async_copy(wd, wd, sem).wait()
    span = 256
    for k in range(wd.shape[0] // span):
        cols = pl.ds(k * span, span)
        term = nn(rows_grad[:, cols], wd[cols, :])
        back[...] = term if k == 0 else back[...] + term


def down_part(where, rows_grad, pieces, runs):
    rows, width = rows_grad.shape
    hidden = pieces[0].shape[1]
    return pl.pallas_call(
        functools.partial(down_kernel, runs),
        out_shape=(jax.ShapeDtypeStruct((width, hidden), BF16), jax.ShapeDtypeStruct((rows, hidden), F32)),
        in_specs=[SMEM, VMEM] + [HBM] * len(pieces),
        out_specs=(VMEM, VMEM),
        scratch_shapes=[pltpu.SemaphoreType.DMA(())],
        compiler_params=params(16),
        cost_estimate=pl.CostEstimate(flops=2 * rows * width * hidden, bytes_accessed=7 * 2**20, transcendentals=0),
    )(where, rows_grad, *pieces)


def expert_kernel(rows_in, down, ba, chunk, both, wg, wu, wd, ga, ua, hid, gpg, gpu, sems, down_sem):
    shards = chunk.shape[0]
    part = chunk.shape[1] // 2
    mats = (wg, wu)
    group = 4
    steps = shards // group
    span = group * part

    def start(s, _):
        row = pl.multiple_of(s * part, part)
        for m in range(2):
            pltpu.make_async_copy(
                chunk.at[s, pl.ds(m * part, part)], mats[m].at[pl.ds(row, part)], sems.at[m, s // group]
            ).start()
        return 0

    lax.fori_loop(0, shards, start, 0)
    fetch = pltpu.make_async_copy(down, wd, down_sem)
    fetch.start()
    for k in range(steps):
        cols = pl.ds(k * span, span)
        for m, acc in ((0, ga), (1, ua)):
            view = mats[m].at[cols]
            pltpu.make_async_copy(view, view, sems.at[m, k]).wait()
            term = nn(rows_in[:, cols], mats[m][cols, :])
            acc[...] = term if k == 0 else acc[...] + term

    def point(i, _):
        r = pl.ds(pl.multiple_of(i * 16, 16), 16)
        gate, up, grad = ga[r, :], ua[r, :], ba[r, :]
        sigma = jax.nn.sigmoid(gate)
        act = gate * sigma
        hid[r, :] = (act * up).astype(BF16)
        gpg[r, :] = (grad * up * sigma * (1.0 + gate * (1.0 - sigma))).astype(BF16)
        gpu[r, :] = (grad * act).astype(BF16)
        return 0

    lax.fori_loop(0, hid.shape[0] // 16, point, 0)
    fetch.wait()
    sources = 2 * NY

    def finish(k, _):
        cols = pl.ds(pl.multiple_of(k * span, span), span)
        out = nt(hid[...], wd[cols, :]).reshape(sources, SLOT, span)
        back = (nt(gpg[...], wg[cols, :]) + nt(gpu[...], wu[cols, :])).reshape(sources, SLOT, span)
        rest = jnp.zeros((sources, BACK - 2 * CAP, span), F32)
        joined = jnp.concatenate([out[:, :CAP], back[:, :CAP], rest], axis=1)
        both[:, cols] = joined.reshape(sources * BACK, span).astype(BF16)
        return 0

    lax.fori_loop(0, steps, finish, 0)


def experts(rows_in, wd, back, chunk):
    rows, width = rows_in.shape
    shards, hidden = chunk.shape[0], chunk.shape[2]
    return pl.pallas_call(
        expert_kernel,
        out_shape=jax.ShapeDtypeStruct((2 * NY * BACK, width), BF16),
        in_specs=[VMEM, HBM, VMEM, HBM],
        out_specs=VMEM,
        scratch_shapes=[pltpu.VMEM((width, hidden), BF16)] * 3
        + [pltpu.VMEM((rows, hidden), F32)] * 2
        + [pltpu.VMEM((rows, hidden), BF16)] * 3
        + [pltpu.SemaphoreType.DMA((2, shards // 4)), pltpu.SemaphoreType.DMA(())],
        compiler_params=params(50),
        cost_estimate=pl.CostEstimate(
            flops=10 * rows * width * hidden, bytes_accessed=14 * 2**20, transcendentals=rows * hidden
        ),
    )(rows_in, wd, back, chunk)


def combine_kernel(hidden, grad_out, rows, target, prob, gain, layer_out, grad_in, grad_gate):
    tokens = hidden.shape[0]
    at = lax.broadcasted_iota(jnp.int32, (tokens, rows.shape[0]), 1)

    def picked(c, offset):
        place = jnp.where(at == target[:, c : c + 1] + offset, 1.0, 0.0).astype(BF16)
        return nn(place, rows[...])

    wide = hidden[...].astype(F32)
    grad = grad_out[...].astype(F32)
    out0, out1 = picked(0, 0), picked(1, 0)
    p0, p1 = prob[:, 0:1], prob[:, 1:2]
    layer_out[...] = (wide + (p0 * out0 + p1 * out1)).astype(BF16)
    grad_gate[:, 0:1] = jnp.sum(grad * out0, axis=-1, keepdims=True)
    grad_gate[:, 1:2] = jnp.sum(grad * out1, axis=-1, keepdims=True)
    moe_grad = p0 * picked(0, CAP) + p1 * picked(1, CAP)
    rstd = lax.rsqrt(jnp.mean(wide * wide, axis=-1, keepdims=True) + norm_eps)
    normed = wide * rstd
    scaled = moe_grad * gain[...]
    mean = jnp.mean(scaled * normed, axis=-1, keepdims=True)
    grad_in[...] = (grad + rstd * (scaled - normed * mean)).astype(BF16)


def combine(hidden, grad_out, rows, target, prob, gain):
    tokens, width = hidden.shape
    made = jax.ShapeDtypeStruct((tokens, width), BF16)
    return pl.pallas_call(
        combine_kernel,
        out_shape=(made, made, jax.ShapeDtypeStruct((tokens, 2), F32)),
        in_specs=[VMEM] * 6,
        out_specs=(VMEM,) * 3,
        compiler_params=params(24),
        cost_estimate=pl.CostEstimate(flops=2**28, bytes_accessed=3 * 2**20, transcendentals=0),
    )(hidden, grad_out, rows, target, prob, gain)


def per_device(
    x_resid, queries, key_proj, val_proj, w_out, norm_gain, w_gate, w_up, w_down, routes, gate_prob, grad_out
):
    tok_dev, width = x_resid.shape
    me_seq, me_exp = lax.axis_index("seq"), lax.axis_index("exp")
    where = jnp.stack([me_seq, me_exp // 2, me_exp % 2]).astype(jnp.int32)
    core, y = me_exp % 2, me_exp // 2
    chunk = lax.all_gather(jnp.concatenate([w_gate[0], w_up[0]], axis=0), "seq", axis=0)
    (k_above, k_loads), (v_above, v_loads) = to_earlier(key_proj), to_earlier(val_proj)
    keys = [key_proj] + earlier_shards(k_above, k_loads)
    vals = [val_proj] + earlier_shards(v_above, v_loads)
    downs, runs = gather_rows(w_down[0].T, (k_above, v_above))
    w_sib = swap_core(after(w_out, keys))

    flat = routes.reshape(-1)
    order = jnp.arange(flat.shape[0], dtype=jnp.int32)
    same = (flat[:, None] == flat[None, :]) & (order[None, :] < order[:, None])
    rank = jnp.sum(same.astype(jnp.int32), axis=1)
    target_rows = (flat * SLOT + rank).reshape(tok_dev, 2).T
    returned = (flat * BACK + rank).reshape(tok_dev, 2)
    sources = 2 * NY
    slots = sources * SLOT
    gain = norm_gain[None, :]

    def exchange(rows):
        split = rows.reshape(sources, rows.shape[0] // sources, rows.shape[1])
        return lax.all_to_all(split, "exp", split_axis=0, concat_axis=0, tiled=True)

    recv_grad = exchange(scatter_rows(after(grad_out, keys), target_rows, slots)).reshape(slots, width)
    attn = attention(where, queries, keys, vals)
    owners = attn.reshape(NY, 2, tok_dev, attn.shape[1])
    mine = lax.dynamic_index_in_dim(owners, core, 1, keepdims=False)
    theirs = swap_core(lax.dynamic_index_in_dim(owners, 1 - core, 1, keepdims=False))
    partial = project(y[None].astype(jnp.int32), mine, theirs, w_out, w_sib)
    parts = [partial[0]] + [along_y(partial[d], d) for d in (1, 2, 3)]
    hidden, send_in = norm_dispatch(x_resid, parts, gain, target_rows, slots)
    recv_in = exchange(send_in).reshape(slots, width)
    both = experts(recv_in, *down_part(where, recv_grad, downs, runs), chunk)
    rows = exchange(both).reshape(sources * BACK, width)
    return combine(hidden, grad_out, rows, returned, gate_prob, gain)


def solution(mesh):
    tokens = P(("seq", "exp"), None)
    heads = P("seq", "exp")
    placed = (
        tokens,
        heads,
        heads,
        heads,
        P("exp", None),
        P(),
        P("exp", "seq", None),
        P("exp", "seq", None),
        P("exp", None, "seq"),
        tokens,
        tokens,
        tokens,
    )
    return jax.shard_map(
        per_device, mesh=mesh, in_specs=placed, out_specs=(tokens, tokens, tokens), check_vma=False
    )
```

profile of v0, /device:TPU:2, one launch (start us, length us, event | category | flops | bytes accessed | tf_op | source)
XLA Modules:
  0.0 209.3 jit_solution(17898250285214249542)
XLA Ops:
  7.2 1.8 pad_maximum_fusion.1
  9.1 2.0 collective-permute-start
  11.6 2.4 %collective-permute-start.14 = (bf16[64,1408]{1,0:T(8,128)(2,1)}, bf16[64,1408]{1,0:T(8,128)(2,1)S(1)}, u32[]{:S(2)}, u32[]{:S(2)}) collective-permute-start(bf16[64,1408]{1,0:T(8,128)(2,1)} %bitcast.44), channel_id=1, source_target_pairs={{0,16},{8,24},{16,0},{24,8},{32,48},{40,56},{48,32},{56,40},{64,80... | collective-permute-start | bytes 540680 | tf_op jit(solution)/shard_map/ppermute | solution.py:41
  14.0 1.8 collective-permute-start.13
  15.8 1.9 collective-permute-start.4
  17.8 4.6 %collective-permute-done.k4 = bf16[512,256]{1,0:T(8,128)(2,1)S(1)} collective-permute-done((bf16[512,256]{1,0:T(8,128)(2,1)}, bf16[512,256]{1,0:T(8,128)(2,1)S(1)}, u32[]{:S(2)}, u32[]{:S(2)}) %collective-permute-start) | collective-permute-done | bytes 262176 | tf_op jit(solution)/shard_map/ppermute | solution.py:41
  22.4 1.0 broadcast_select_fusion.1
  23.4 1.6 collective-permute-start.1
  25.0 1.1 collective-permute-start.2
  26.1 2.2 %collective-permute-start.3 = (bf16[512,256]{1,0:T(8,128)(2,1)S(1)}, bf16[512,256]{1,0:T(8,128)(2,1)S(1)}, u32[]{:S(2)}, u32[]{:S(2)}) collective-permute-start(bf16[512,256]{1,0:T(8,128)(2,1)S(1)} %get-tuple-element.36), channel_id=1, source_target_pairs={{0,24},{8,0},{16,8},{24,16},{32,56},{40,32},{48,40},{56,48},{64,88... | collective-permute-start | bytes 786440 | tf_op jit(solution)/shard_map/ppermute | solution.py:41
  28.4 3.2 %collective-permute-start.17 = (bf16[256,1408]{1,0:T(8,128)(2,1)S(1)}, bf16[256,1408]{1,0:T(8,128)(2,1)}, u32[]{:S(2)}, u32[]{:S(2)}) collective-permute-start(bf16[256,1408]{1,0:T(8,128)(2,1)S(1)} %pad_maximum_fusion.refs_0_), channel_id=1, source_target_pairs={{0,224},{8,232},{16,240},{24,248},{32,0},{40,8},{48,16},{56,24},{6... | collective-permute-start | bytes 2162696 | tf_op jit(solution)/shard_map/ppermute | solution.py:41
  31.6 4.4 %collective-permute-done.1.k1 = bf16[512,256]{1,0:T(8,128)(2,1)S(1)} collective-permute-done((bf16[512,256]{1,0:T(8,128)(2,1)S(1)}, bf16[512,256]{1,0:T(8,128)(2,1)S(1)}, u32[]{:S(2)}, u32[]{:S(2)}) %collective-permute-start.1) | collective-permute-done | bytes 262176 | tf_op jit(solution)/shard_map/ppermute | solution.py:41
  36.7 2.3 %collective-permute-done.2.k2 = bf16[512,256]{1,0:T(8,128)(2,1)S(1)} collective-permute-done((bf16[512,256]{1,0:T(8,128)(2,1)S(1)}, bf16[512,256]{1,0:T(8,128)(2,1)S(1)}, u32[]{:S(2)}, u32[]{:S(2)}) %collective-permute-start.2) | collective-permute-done | bytes 262176 | tf_op jit(solution)/shard_map/ppermute | solution.py:41
  39.7 2.2 %collective-permute-done.3.k3 = bf16[512,256]{1,0:T(8,128)(2,1)S(1)} collective-permute-done((bf16[512,256]{1,0:T(8,128)(2,1)S(1)}, bf16[512,256]{1,0:T(8,128)(2,1)S(1)}, u32[]{:S(2)}, u32[]{:S(2)}) %collective-permute-start.3) | collective-permute-done | bytes 262176 | tf_op jit(solution)/shard_map/ppermute | solution.py:41
  43.5 1.0 collective-permute-start.5
  44.5 2.2 %collective-permute-start.6 = (bf16[512,256]{1,0:T(8,128)(2,1)}, bf16[512,256]{1,0:T(8,128)(2,1)}, u32[]{:S(2)}, u32[]{:S(2)}) collective-permute-start(bf16[512,256]{1,0:T(8,128)(2,1)} %get-tuple-element.34), channel_id=1, source_target_pairs={{0,16},{8,24},{16,0},{24,8},{32,48},{40,56},{48,32},{56,40},{64,80... | collective-permute-start | bytes 786440 | tf_op jit(solution)/shard_map/ppermute | solution.py:41
  46.7 5.9 %collective-permute-done.5.v1 = bf16[512,256]{1,0:T(8,128)(2,1)S(1)} collective-permute-done((bf16[512,256]{1,0:T(8,128)(2,1)S(1)}, bf16[512,256]{1,0:T(8,128)(2,1)S(1)}, u32[]{:S(2)}, u32[]{:S(2)}) %collective-permute-start.5) | collective-permute-done | bytes 262176 | tf_op jit(solution)/shard_map/ppermute | solution.py:41
  53.3 7.8 %collective-permute-start.7 = (bf16[512,256]{1,0:T(8,128)(2,1)}, bf16[512,256]{1,0:T(8,128)(2,1)}, u32[]{:S(2)}, u32[]{:S(2)}) collective-permute-start(bf16[512,256]{1,0:T(8,128)(2,1)} %get-tuple-element.33), channel_id=1, source_target_pairs={{0,24},{8,0},{16,8},{24,16},{32,56},{40,32},{48,40},{56,48},{64,88... | collective-permute-start | bytes 786440 | tf_op jit(solution)/shard_map/ppermute | solution.py:41
  62.9 3.1 %collective-permute-start.19 = (bf16[256,1408]{1,0:T(8,128)(2,1)}, bf16[256,1408]{1,0:T(8,128)(2,1)}, u32[]{:S(2)}, u32[]{:S(2)}) collective-permute-start(bf16[256,1408]{1,0:T(8,128)(2,1)} %collective-permute-done.17.refs_2_), channel_id=1, source_target_pairs={{0,224},{8,232},{16,240},{24,248},{32,0},{40,8},{48,16},{56,24},{6... | collective-permute-start | bytes 2162696 | tf_op jit(solution)/shard_map/ppermute | solution.py:41
  67.9 1.0 copy-done.10
  68.9 1.0 copy-done.17
  69.9 1.0 copy-done.19
  70.9 0.9 copy-done.21
  71.8 0.9 copy-done.23
  73.7 6.9 %shard_map.139 = bf16[512,256]{1,0:T(8,128)(2,1)S(1)} custom-call(s32[3]{0:T(128)S(1)} %pad_add_fusion.where, bf16[512,256]{1,0:T(8,128)(2,1)S(1)} %copy-done.17, bf16[512,256]{1,0:T(8,128)(2,1)S(1)} %copy-done.6, bf16[512,256]{1,0:T(8,128)(2,1)S(1)} %copy-done.19, bf16[512,256]{1,0:T(8,128)(2,1)S(1)} %copy-done.21, bf16[512,256]{1,0:T(8,128)(2,1)S(1)} %copy-done.23, ...), custom_call_target="tpu_custom_call" | custom-call | flops 1342177280 | bytes 6291456 | tf_op jit(solution)/shard_map/pallas_call | solution.py:122
  82.0 1.2 shard_map.142
  83.2 4.4 %all-to-all-start.1 = ((bf16[8,24,2048]{2,1,0:T(8,128)(2,1)}), bf16[8,24,2048]{2,1,0:T(8,128)(2,1)S(1)}, u32[]{:S(2)}, u32[]{:S(2)}) async-start(bf16[8,24,2048]{2,1,0:T(8,128)(2,1)} %bitcast.14), calls=%async_computation.1 | async-start | bytes 1572864 | tf_op jit(solution)/shard_map/all_to_all | solution.py:378
  88.5 2.9 %shard_map.140 = bf16[4,64,2048]{2,1,0:T(8,128)(2,1)S(1)} custom-call(s32[1]{0:T(128)} %bitcast.where, bf16[4,64,256]{2,1,0:T(8,128)(2,1)S(1)} %copy-done.5, bf16[4,64,256]{2,1,0:T(8,128)(2,1)} %collective-permute-done.8.sib, bf16[256,2048]{1,0:T(8,128)(2,1)S(1)} %copy-done, bf16[256,2048]{1,0:T(8,128)(2,1)} %collective-permute-done.9.w_sib), custom_call_target="tpu_custom_call" | custom-call | flops 536870912 | bytes 6291456 | tf_op jit(solution)/shard_map/pallas_call | solution.py:154
  91.6 3.0 %collective-permute-done.19.refs_4_ = bf16[256,1408]{1,0:T(8,128)(2,1)} collective-permute-done((bf16[256,1408]{1,0:T(8,128)(2,1)}, bf16[256,1408]{1,0:T(8,128)(2,1)}, u32[]{:S(2)}, u32[]{:S(2)}) %collective-permute-start.19) | collective-permute-done | bytes 720928 | tf_op jit(solution)/shard_map/ppermute | solution.py:41
  94.7 3.7 %collective-permute-start.21 = (bf16[256,1408]{1,0:T(8,128)(2,1)}, bf16[256,1408]{1,0:T(8,128)(2,1)S(1)}, u32[]{:S(2)}, u32[]{:S(2)}) collective-permute-start(bf16[256,1408]{1,0:T(8,128)(2,1)} %collective-permute-done.19.refs_4_), channel_id=1, source_target_pairs={{0,224},{8,232},{16,240},{24,248},{32,0},{40,8},{48,16},{56,24},{6... | collective-permute-start | bytes 2162696 | tf_op jit(solution)/shard_map/ppermute | solution.py:41
  98.6 1.7 collective-permute-start.11
  100.3 1.5 collective-permute-start.12
  101.8 5.7 %collective-permute-done.10.p1 = bf16[64,2048]{1,0:T(8,128)(2,1)S(1)} collective-permute-done((bf16[64,2048]{1,0:T(8,128)(2,1)S(1)}, bf16[64,2048]{1,0:T(8,128)(2,1)S(1)}, u32[]{:S(2)}, u32[]{:S(2)}) %collective-permute-start.10) | collective-permute-done | bytes 262176 | tf_op jit(solution)/shard_map/ppermute | solution.py:53
  107.5 4.5 %collective-permute-done.11.p2 = bf16[64,2048]{1,0:T(8,128)(2,1)S(1)} collective-permute-done((bf16[64,2048]{1,0:T(8,128)(2,1)S(1)}, bf16[64,2048]{1,0:T(8,128)(2,1)S(1)}, u32[]{:S(2)}, u32[]{:S(2)}) %collective-permute-start.11) | collective-permute-done | bytes 262176 | tf_op jit(solution)/shard_map/ppermute | solution.py:53
  114.2 4.2 %all-to-all-start = ((bf16[8,24,2048]{2,1,0:T(8,128)(2,1)}), bf16[8,24,2048]{2,1,0:T(8,128)(2,1)}, u32[]{:S(2)}, u32[]{:S(2)}) async-start(bf16[8,24,2048]{2,1,0:T(8,128)(2,1)} %bitcast.37), calls=%async_computation | async-start | bytes 1572864 | tf_op jit(solution)/shard_map/all_to_all | solution.py:378
  118.4 8.9 %collective-permute-done.20.refs_5_ = bf16[256,1408]{1,0:T(8,128)(2,1)S(1)} collective-permute-done((bf16[256,1408]{1,0:T(8,128)(2,1)}, bf16[256,1408]{1,0:T(8,128)(2,1)S(1)}, u32[]{:S(2)}, u32[]{:S(2)}) %collective-permute-start.20) | collective-permute-done | bytes 720928 | tf_op jit(solution)/shard_map/ppermute | solution.py:41
  127.4 1.8 collective-permute-done.21.refs_6_
  129.2 3.9 %collective-permute-start.23 = (bf16[128,1408]{1,0:T(8,128)(2,1)S(1)}, bf16[128,1408]{1,0:T(8,128)(2,1)S(1)}, u32[]{:S(2)}, u32[]{:S(2)}) collective-permute-start(bf16[128,1408]{1,0:T(8,128)(2,1)S(1)} %slice.29), channel_id=1, source_target_pairs={{0,224},{8,232},{16,240},{24,248},{32,0},{40,8},{48,16},{56,24},{6... | collective-permute-start | bytes 1081352 | tf_op jit(solution)/shard_map/ppermute | solution.py:41
  133.1 14.1 %collective-permute-done.22.refs_7_ = bf16[128,1408]{1,0:T(8,128)(2,1)S(1)} collective-permute-done((bf16[128,1408]{1,0:T(8,128)(2,1)S(1)}, bf16[128,1408]{1,0:T(8,128)(2,1)S(1)}, u32[]{:S(2)}, u32[]{:S(2)}) %collective-permute-start.22) | collective-permute-done | bytes 360480 | tf_op jit(solution)/shard_map/ppermute | solution.py:41
  147.2 1.2 collective-permute-done.23.refs_8_
  148.4 7.3 %shard_map.143 = (bf16[2048,1408]{1,0:T(8,128)(2,1)S(1)}, f32[192,1408]{1,0:T(8,128)S(1)}) custom-call(s32[3]{0:T(128)S(1)} %pad_add_fusion.where, bf16[192,2048]{1,0:T(8,128)(2,1)S(1)} %bitcast.36, bf16[256,1408]{1,0:T(8,128)(2,1)S(1)} %pad_maximum_fusion.refs_0_, bf16[256,1408]{1,0:T(8,128)(2,1)S(1)} %copy-done.4, ...), custom_call_target="tpu_custom_call" | custom-call | flops 1107296256 | bytes 7340032 | tf_op jit(solution)/shard_map/pallas_call | solution.py:233
  155.6 2.4 %copy-done.14 = bf16[2048,1408]{1,0:T(8,128)(2,1)} copy-done((bf16[2048,1408]{1,0:T(8,128)(2,1)}, bf16[2048,1408]{1,0:T(8,128)(2,1)S(1)}, u32[]{:S(2)}) %copy-start.14) | copy-done | bytes 5767192
  158.1 1.0 copy-done.15
  159.9 1.2 copy-done.16
  161.1 16.2 %shard_map.144 = bf16[320,2048]{1,0:T(8,128)(2,1)} custom-call(bf16[192,2048]{1,0:T(8,128)(2,1)} %bitcast.13.rows_in, bf16[2048,1408]{1,0:T(8,128)(2,1)} %copy-done.14, f32[192,1408]{1,0:T(8,128)S(1)} %copy-done.16, bf16[32,128,1408]{2,1,0:T(8,128)(2,1)} %bitcast.47), custom_call_target="tpu_custom_call" | custom-call | flops 5536481280 | bytes 14680064 | tf_op jit(solution)/shard_map/pallas_call | solution.py:300
  177.3 3.7 %all-to-all-start.2 = ((bf16[8,40,2048]{2,1,0:T(8,128)(2,1)}), bf16[8,40,2048]{2,1,0:T(8,128)(2,1)S(1)}, u32[]{:S(2)}, u32[]{:S(2)}) async-start(bf16[8,40,2048]{2,1,0:T(8,128)(2,1)} %bitcast.22), calls=%async_computation.2 | async-start | bytes 2621440 | tf_op jit(solution)/shard_map/all_to_all | solution.py:378
  181.3 18.5 %all-to-all-done.2 = bf16[8,40,2048]{2,1,0:T(8,128)(2,1)S(1)} async-done(((bf16[8,40,2048]{2,1,0:T(8,128)(2,1)}), bf16[8,40,2048]{2,1,0:T(8,128)(2,1)S(1)}, u32[]{:S(2)}, u32[]{:S(2)}) %all-to-all-start.2) | async-done | bytes 1310752 | tf_op jit(solution)/shard_map/all_to_all | solution.py:378
  199.7 2.1 %shard_map.145 = (bf16[64,2048]{1,0:T(8,128)(2,1)}, bf16[64,2048]{1,0:T(8,128)(2,1)}, f32[64,2]{1,0:T(8,128)S(1)}) custom-call(bf16[64,2048]{1,0:T(8,128)(2,1)S(1)} %copy-done.12, bf16[64,2048]{1,0:T(8,128)(2,1)S(1)} %copy-done.1, bf16[320,2048]{1,0:T(8,128)(2,1)S(1)} %bitcast.35, s32[64,2]{1,0:T(8,128)S(1)} %add.31.target, f32[64,2]{1,0:T(8,128)S(1)} %copy.44.prob, ...), custom_call_target="tpu_custom_call" | custom-call | flops 268435456 | bytes 3145728 | tf_op jit(solution)/shard_map/pallas_call | solution.py:342
  (97 shorter events, 15.7 us)
Async XLA Ops:
  7.2 21.1 %copy-start.27 = (bf16[1,1408,64]{1,2,0:T(8,128)(2,1)S(1)}, bf16[1,1408,64]{1,2,0:T(8,128)(2,1)}, u32[]{:S(2)}) copy-start(bf16[1,1408,64]{1,2,0:T(8,128)(2,1)} %param.20) | copy-start | bytes 540676
  7.2 152.7 %all-gather.3.cloned.1.call-start = ((), (), s32[]{:S(2)}) async-start(), calls=%async_computation.3 | async-start | bytes 11894784 | tf_op jit(solution)/shard_map/all_gather | solution.py:359
  9.1 33.5 %copy-start = (bf16[256,2048]{1,0:T(8,128)(2,1)S(1)}, bf16[256,2048]{1,0:T(8,128)(2,1)}, u32[]{:S(2)}) copy-start(bf16[256,2048]{1,0:T(8,128)(2,1)} %w_own.1) | copy-start | bytes 3145732
  9.1 33.5 %copy-start.7 = (bf16[512,256]{1,0:T(8,128)(2,1)S(1)}, bf16[512,256]{1,0:T(8,128)(2,1)}, u32[]{:S(2)}) copy-start(bf16[512,256]{1,0:T(8,128)(2,1)} %v0.1) | copy-start | bytes 786436
  9.1 13.3 %collective-permute-start = (bf16[512,256]{1,0:T(8,128)(2,1)}, bf16[512,256]{1,0:T(8,128)(2,1)S(1)}, u32[]{:S(2)}, u32[]{:S(2)}) collective-permute-start(bf16[512,256]{1,0:T(8,128)(2,1)} %k0.1), channel_id=1, source_target_pairs={{0,32},{8,40},{16,48},{24,56},{32,64},{40,72},{48,80},{56,88},{64,... | collective-permute-start | bytes 786440 | tf_op jit(solution)/shard_map/ppermute | solution.py:41
  11.1 13.9 %collective-permute-start.15 = (bf16[64,1408]{1,0:T(8,128)(2,1)}, bf16[64,1408]{1,0:T(8,128)(2,1)S(1)}, u32[]{:S(2)}, u32[]{:S(2)}) collective-permute-start(bf16[64,1408]{1,0:T(8,128)(2,1)} %bitcast.43), channel_id=1, source_target_pairs={{0,24},{8,0},{16,8},{24,16},{32,56},{40,32},{48,40},{56,48},{64,88... | collective-permute-start | bytes 540680 | tf_op jit(solution)/shard_map/ppermute | solution.py:41
  11.6 14.5 %collective-permute-start.14 = (bf16[64,1408]{1,0:T(8,128)(2,1)}, bf16[64,1408]{1,0:T(8,128)(2,1)S(1)}, u32[]{:S(2)}, u32[]{:S(2)}) collective-permute-start(bf16[64,1408]{1,0:T(8,128)(2,1)} %bitcast.44), channel_id=1, source_target_pairs={{0,16},{8,24},{16,0},{24,8},{32,48},{40,56},{48,32},{56,40},{64,80... | collective-permute-start | bytes 540680 | tf_op jit(solution)/shard_map/ppermute | solution.py:41
  14.0 14.2 %collective-permute-start.13 = (bf16[64,1408]{1,0:T(8,128)(2,1)}, bf16[64,1408]{1,0:T(8,128)(2,1)S(1)}, u32[]{:S(2)}, u32[]{:S(2)}) collective-permute-start(bf16[64,1408]{1,0:T(8,128)(2,1)} %bitcast.45), channel_id=1, source_target_pairs={{0,8},{8,16},{16,24},{24,0},{32,40},{40,48},{48,56},{56,32},{64,72... | collective-permute-start | bytes 540680 | tf_op jit(solution)/shard_map/ppermute | solution.py:41
  15.8 12.5 %collective-permute-start.4 = (bf16[512,256]{1,0:T(8,128)(2,1)}, bf16[512,256]{1,0:T(8,128)(2,1)S(1)}, u32[]{:S(2)}, u32[]{:S(2)}) collective-permute-start(bf16[512,256]{1,0:T(8,128)(2,1)} %v0.1), channel_id=1, source_target_pairs={{0,32},{8,40},{16,48},{24,56},{32,64},{40,72},{48,80},{56,88},{64,... | collective-permute-start | bytes 786440 | tf_op jit(solution)/shard_map/ppermute | solution.py:41
  23.4 37.7 %copy-start.28 = (s32[64,2]{0,1:T(2,128)S(1)}, s32[64,2]{0,1:T(2,128)}, u32[]{:S(2)}) copy-start(s32[64,2]{0,1:T(2,128)} %param.21) | copy-start | bytes 1540
  23.4 12.7 %collective-permute-start.1 = (bf16[512,256]{1,0:T(8,128)(2,1)S(1)}, bf16[512,256]{1,0:T(8,128)(2,1)S(1)}, u32[]{:S(2)}, u32[]{:S(2)}) collective-permute-start(bf16[512,256]{1,0:T(8,128)(2,1)S(1)} %get-tuple-element.38), channel_id=1, source_target_pairs={{0,8},{8,16},{16,24},{24,0},{32,40},{40,48},{48,56},{56,32},{64,72... | collective-permute-start | bytes 786440 | tf_op jit(solution)/shard_map/ppermute | solution.py:41
  25.0 14.1 %collective-permute-start.2 = (bf16[512,256]{1,0:T(8,128)(2,1)S(1)}, bf16[512,256]{1,0:T(8,128)(2,1)S(1)}, u32[]{:S(2)}, u32[]{:S(2)}) collective-permute-start(bf16[512,256]{1,0:T(8,128)(2,1)S(1)} %get-tuple-element.37), channel_id=1, source_target_pairs={{0,16},{8,24},{16,0},{24,8},{32,48},{40,56},{48,32},{56,40},{64,80... | collective-permute-start | bytes 786440 | tf_op jit(solution)/shard_map/ppermute | solution.py:41
  26.1 41.8 %copy-start.6 = (bf16[512,256]{1,0:T(8,128)(2,1)S(1)}, bf16[512,256]{1,0:T(8,128)(2,1)}, u32[]{:S(2)}) copy-start(bf16[512,256]{1,0:T(8,128)(2,1)} %k0.1) | copy-start | bytes 786436
  26.1 15.8 %collective-permute-start.3 = (bf16[512,256]{1,0:T(8,128)(2,1)S(1)}, bf16[512,256]{1,0:T(8,128)(2,1)S(1)}, u32[]{:S(2)}, u32[]{:S(2)}) collective-permute-start(bf16[512,256]{1,0:T(8,128)(2,1)S(1)} %get-tuple-element.36), channel_id=1, source_target_pairs={{0,24},{8,0},{16,8},{24,16},{32,56},{40,32},{48,40},{56,48},{64,88... | collective-permute-start | bytes 786440 | tf_op jit(solution)/shard_map/ppermute | solution.py:41
  28.3 39.5 %copy-start.9 = (bf16[512,256]{1,0:T(8,128)(2,1)}, bf16[512,256]{1,0:T(8,128)(2,1)S(1)}, u32[]{:S(2)}) copy-start(bf16[512,256]{1,0:T(8,128)(2,1)S(1)} %collective-permute-done.4.v4) | copy-start | bytes 786436
  28.3 34.4 %collective-permute-start.16 = (bf16[256,1408]{1,0:T(8,128)(2,1)S(1)}, bf16[256,1408]{1,0:T(8,128)(2,1)S(1)}, u32[]{:S(2)}, u32[]{:S(2)}) collective-permute-start(bf16[256,1408]{1,0:T(8,128)(2,1)S(1)} %pad_maximum_fusion.refs_0_), channel_id=1, source_target_pairs={{0,32},{8,40},{16,48},{24,56},{32,64},{40,72},{48,80},{56,88},{64,... | collective-permute-start | bytes 2162696 | tf_op jit(solution)/shard_map/ppermute | solution.py:41
  28.4 34.5 %collective-permute-start.17 = (bf16[256,1408]{1,0:T(8,128)(2,1)S(1)}, bf16[256,1408]{1,0:T(8,128)(2,1)}, u32[]{:S(2)}, u32[]{:S(2)}) collective-permute-start(bf16[256,1408]{1,0:T(8,128)(2,1)S(1)} %pad_maximum_fusion.refs_0_), channel_id=1, source_target_pairs={{0,224},{8,232},{16,240},{24,248},{32,0},{40,8},{48,16},{56,24},{6... | collective-permute-start | bytes 2162696 | tf_op jit(solution)/shard_map/ppermute | solution.py:41
  42.6 45.0 %collective-permute-start.9 = (bf16[256,2048]{1,0:T(8,128)(2,1)S(1)}, bf16[256,2048]{1,0:T(8,128)(2,1)}, u32[]{:S(2)}, u32[]{:S(2)}) collective-permute-start(bf16[256,2048]{1,0:T(8,128)(2,1)S(1)} %copy-done), channel_id=1, source_target_pairs={{0,1},{1,0},{2,3},{3,2},{4,5},{5,4},{6,7},{7,6},{8,9},{9,8},{10,11... | collective-permute-start | bytes 3145736 | tf_op jit(solution)/shard_map/ppermute | solution.py:57
  43.5 9.1 %collective-permute-start.5 = (bf16[512,256]{1,0:T(8,128)(2,1)S(1)}, bf16[512,256]{1,0:T(8,128)(2,1)S(1)}, u32[]{:S(2)}, u32[]{:S(2)}) collective-permute-start(bf16[512,256]{1,0:T(8,128)(2,1)S(1)} %get-tuple-element.35), channel_id=1, source_target_pairs={{0,8},{8,16},{16,24},{24,0},{32,40},{40,48},{48,56},{56,32},{64,72... | collective-permute-start | bytes 786440 | tf_op jit(solution)/shard_map/ppermute | solution.py:41
  44.5 23.4 %collective-permute-start.6 = (bf16[512,256]{1,0:T(8,128)(2,1)}, bf16[512,256]{1,0:T(8,128)(2,1)}, u32[]{:S(2)}, u32[]{:S(2)}) collective-permute-start(bf16[512,256]{1,0:T(8,128)(2,1)} %get-tuple-element.34), channel_id=1, source_target_pairs={{0,16},{8,24},{16,0},{24,8},{32,48},{40,56},{48,32},{56,40},{64,80... | collective-permute-start | bytes 786440 | tf_op jit(solution)/shard_map/ppermute | solution.py:41
  53.3 14.6 %collective-permute-start.7 = (bf16[512,256]{1,0:T(8,128)(2,1)}, bf16[512,256]{1,0:T(8,128)(2,1)}, u32[]{:S(2)}, u32[]{:S(2)}) collective-permute-start(bf16[512,256]{1,0:T(8,128)(2,1)} %get-tuple-element.33), channel_id=1, source_target_pairs={{0,24},{8,0},{16,8},{24,16},{32,56},{40,32},{48,40},{56,48},{64,88... | collective-permute-start | bytes 786440 | tf_op jit(solution)/shard_map/ppermute | solution.py:41
  62.7 18.0 %copy-start.3 = (bf16[256,1408]{1,0:T(8,128)(2,1)}, bf16[256,1408]{1,0:T(8,128)(2,1)S(1)}, u32[]{:S(2)}) copy-start(bf16[256,1408]{1,0:T(8,128)(2,1)S(1)} %collective-permute-done.16.refs_1_) | copy-start | bytes 2162692
  62.7 28.9 %collective-permute-start.18 = (bf16[256,1408]{1,0:T(8,128)(2,1)S(1)}, bf16[256,1408]{1,0:T(8,128)(2,1)}, u32[]{:S(2)}, u32[]{:S(2)}) collective-permute-start(bf16[256,1408]{1,0:T(8,128)(2,1)S(1)} %collective-permute-done.16.refs_1_), channel_id=1, source_target_pairs={{0,32},{8,40},{16,48},{24,56},{32,64},{40,72},{48,80},{56,88},{64,... | collective-permute-start | bytes 2162696 | tf_op jit(solution)/shard_map/ppermute | solution.py:41
  62.9 31.7 %collective-permute-start.19 = (bf16[256,1408]{1,0:T(8,128)(2,1)}, bf16[256,1408]{1,0:T(8,128)(2,1)}, u32[]{:S(2)}, u32[]{:S(2)}) collective-permute-start(bf16[256,1408]{1,0:T(8,128)(2,1)} %collective-permute-done.17.refs_2_), channel_id=1, source_target_pairs={{0,224},{8,232},{16,240},{24,248},{32,0},{40,8},{48,16},{56,24},{6... | collective-permute-start | bytes 2162696 | tf_op jit(solution)/shard_map/ppermute | solution.py:41
  67.9 14.1 %copy-start.1 = (bf16[64,2048]{1,0:T(8,128)(2,1)S(1)}, bf16[64,2048]{1,0:T(8,128)(2,1)}, u32[]{:S(2)}) copy-start(bf16[64,2048]{1,0:T(8,128)(2,1)} %grad_out.1) | copy-start | bytes 786436
  67.9 1.0 copy-start.10
  68.9 1.0 copy-start.17
  81.4 6.2 %collective-permute-start.8 = (bf16[4,64,256]{2,1,0:T(8,128)(2,1)}, bf16[4,64,256]{2,1,0:T(8,128)(2,1)}, u32[]{:S(2)}, u32[]{:S(2)}) collective-permute-start(bf16[4,64,256]{2,1,0:T(8,128)(2,1)} %get-tuple-element.39), channel_id=1, source_target_pairs={{0,1},{1,0},{2,3},{3,2},{4,5},{5,4},{6,7},{7,6},{8,9},{9,8},{10,11... | collective-permute-start | bytes 393224 | tf_op jit(solution)/shard_map/ppermute | solution.py:57
  83.2 31.0 %all-to-all-start.1 = ((bf16[8,24,2048]{2,1,0:T(8,128)(2,1)}), bf16[8,24,2048]{2,1,0:T(8,128)(2,1)S(1)}, u32[]{:S(2)}, u32[]{:S(2)}) async-start(bf16[8,24,2048]{2,1,0:T(8,128)(2,1)} %bitcast.14), calls=%async_computation.1 | async-start | bytes 1572864 | tf_op jit(solution)/shard_map/all_to_all | solution.py:378
  91.4 20.6 %copy-start.8 = (bf16[64,2048]{1,0:T(8,128)(2,1)S(1)}, bf16[64,2048]{1,0:T(8,128)(2,1)}, u32[]{:S(2)}) copy-start(bf16[64,2048]{1,0:T(8,128)(2,1)} %x.1) | copy-start | bytes 786436
  91.4 20.6 %copy-start.13 = (f32[2048]{0:T(1024)S(1)}, f32[2048]{0:T(1024)}, u32[]{:S(2)}) copy-start(f32[2048]{0:T(1024)} %param.17) | copy-start | bytes 24580
  91.6 35.7 %collective-permute-start.20 = (bf16[256,1408]{1,0:T(8,128)(2,1)}, bf16[256,1408]{1,0:T(8,128)(2,1)S(1)}, u32[]{:S(2)}, u32[]{:S(2)}) collective-permute-start(bf16[256,1408]{1,0:T(8,128)(2,1)} %collective-permute-done.18.refs_3_), channel_id=1, source_target_pairs={{0,32},{8,40},{16,48},{24,56},{32,64},{40,72},{48,80},{56,88},{64,... | collective-permute-start | bytes 2162696 | tf_op jit(solution)/shard_map/ppermute | solution.py:41
  94.7 34.5 %collective-permute-start.21 = (bf16[256,1408]{1,0:T(8,128)(2,1)}, bf16[256,1408]{1,0:T(8,128)(2,1)S(1)}, u32[]{:S(2)}, u32[]{:S(2)}) collective-permute-start(bf16[256,1408]{1,0:T(8,128)(2,1)} %collective-permute-done.19.refs_4_), channel_id=1, source_target_pairs={{0,224},{8,232},{16,240},{24,248},{32,0},{40,8},{48,16},{56,24},{6... | collective-permute-start | bytes 2162696 | tf_op jit(solution)/shard_map/ppermute | solution.py:41
  98.5 9.0 %collective-permute-start.10 = (bf16[64,2048]{1,0:T(8,128)(2,1)S(1)}, bf16[64,2048]{1,0:T(8,128)(2,1)S(1)}, u32[]{:S(2)}, u32[]{:S(2)}) collective-permute-start(bf16[64,2048]{1,0:T(8,128)(2,1)S(1)} %get-tuple-element.31), channel_id=1, source_target_pairs={{0,2},{1,3},{2,4},{3,5},{4,6},{5,7},{6,0},{7,1},{8,10},{9,11},{10,... | collective-permute-start | bytes 786440 | tf_op jit(solution)/shard_map/ppermute | solution.py:53
  98.6 13.4 %collective-permute-start.11 = (bf16[64,2048]{1,0:T(8,128)(2,1)S(1)}, bf16[64,2048]{1,0:T(8,128)(2,1)S(1)}, u32[]{:S(2)}, u32[]{:S(2)}) collective-permute-start(bf16[64,2048]{1,0:T(8,128)(2,1)S(1)} %get-tuple-element.30), channel_id=1, source_target_pairs={{0,4},{1,5},{2,6},{3,7},{4,0},{5,1},{6,2},{7,3},{8,12},{9,13},{10,... | collective-permute-start | bytes 786440 | tf_op jit(solution)/shard_map/ppermute | solution.py:53
  100.3 11.7 %collective-permute-start.12 = (bf16[64,2048]{1,0:T(8,128)(2,1)S(1)}, bf16[64,2048]{1,0:T(8,128)(2,1)S(1)}, u32[]{:S(2)}, u32[]{:S(2)}) collective-permute-start(bf16[64,2048]{1,0:T(8,128)(2,1)S(1)} %get-tuple-element.29), channel_id=1, source_target_pairs={{0,6},{1,7},{2,0},{3,1},{4,2},{5,3},{6,4},{7,5},{8,14},{9,15},{10,... | collective-permute-start | bytes 786440 | tf_op jit(solution)/shard_map/ppermute | solution.py:53
  114.2 44.8 %all-to-all-start = ((bf16[8,24,2048]{2,1,0:T(8,128)(2,1)}), bf16[8,24,2048]{2,1,0:T(8,128)(2,1)}, u32[]{:S(2)}, u32[]{:S(2)}) async-start(bf16[8,24,2048]{2,1,0:T(8,128)(2,1)} %bitcast.37), calls=%async_computation | async-start | bytes 1572864 | tf_op jit(solution)/shard_map/all_to_all | solution.py:378
  118.4 29.9 %copy-start.4 = (bf16[256,1408]{1,0:T(8,128)(2,1)S(1)}, bf16[256,1408]{1,0:T(8,128)(2,1)}, u32[]{:S(2)}) copy-start(bf16[256,1408]{1,0:T(8,128)(2,1)} %copy-done.3) | copy-start | bytes 2162692
  127.3 19.8 %collective-permute-start.22 = (bf16[128,1408]{1,0:T(8,128)(2,1)S(1)}, bf16[128,1408]{1,0:T(8,128)(2,1)S(1)}, u32[]{:S(2)}, u32[]{:S(2)}) collective-permute-start(bf16[128,1408]{1,0:T(8,128)(2,1)S(1)} %slice.28), channel_id=1, source_target_pairs={{0,32},{8,40},{16,48},{24,56},{32,64},{40,72},{48,80},{56,88},{64,... | collective-permute-start | bytes 1081352 | tf_op jit(solution)/shard_map/ppermute | solution.py:41
  129.2 19.1 %collective-permute-start.23 = (bf16[128,1408]{1,0:T(8,128)(2,1)S(1)}, bf16[128,1408]{1,0:T(8,128)(2,1)S(1)}, u32[]{:S(2)}, u32[]{:S(2)}) collective-permute-start(bf16[128,1408]{1,0:T(8,128)(2,1)S(1)} %slice.29), channel_id=1, source_target_pairs={{0,224},{8,232},{16,240},{24,248},{32,0},{40,8},{48,16},{56,24},{6... | collective-permute-start | bytes 1081352 | tf_op jit(solution)/shard_map/ppermute | solution.py:41
  155.6 2.4 %copy-start.14 = (bf16[2048,1408]{1,0:T(8,128)(2,1)}, bf16[2048,1408]{1,0:T(8,128)(2,1)S(1)}, u32[]{:S(2)}) copy-start(bf16[2048,1408]{1,0:T(8,128)(2,1)S(1)} %get-tuple-element.15.down) | copy-start | bytes 17301508
  158.1 1.0 copy-start.15
  159.9 1.2 copy-start.16
  177.3 3.8 %copy-start.29 = (s32[64,2]{0,1:T(2,128)S(1)}, s32[64,2]{0,1:T(2,128)}, u32[]{:S(2)}) copy-start(s32[64,2]{0,1:T(2,128)} %get-tuple-element.41) | copy-start | bytes 1540
  177.3 3.9 %copy-start.26 = (s32[64,2]{1,0:T(8,128)S(1)}, s32[64,2]{1,0:T(8,128)}, u32[]{:S(2)}) copy-start(s32[64,2]{1,0:T(8,128)} %reduce_sum.12) | copy-start | bytes 1540
  177.3 3.9 %copy-start.30 = (f32[64,2]{0,1:T(2,128)S(1)}, f32[64,2]{0,1:T(2,128)}, u32[]{:S(2)}) copy-start(f32[64,2]{0,1:T(2,128)} %param.22) | copy-start | bytes 1540
  177.3 22.4 %copy-start.12 = (bf16[64,2048]{1,0:T(8,128)(2,1)S(1)}, bf16[64,2048]{1,0:T(8,128)(2,1)}, u32[]{:S(2)}) copy-start(bf16[64,2048]{1,0:T(8,128)(2,1)} %copy-done.11) | copy-start | bytes 786436
  177.3 22.4 %all-to-all-start.2 = ((bf16[8,40,2048]{2,1,0:T(8,128)(2,1)}), bf16[8,40,2048]{2,1,0:T(8,128)(2,1)S(1)}, u32[]{:S(2)}, u32[]{:S(2)}) async-start(bf16[8,40,2048]{2,1,0:T(8,128)(2,1)} %bitcast.22), calls=%async_computation.2 | async-start | bytes 2621440 | tf_op jit(solution)/shard_map/all_to_all | solution.py:378
  (11 other events, 9.1 us)
Sparse Core Ops, SparseCore 0:
  10.6 149.2 all-gather.2
where the time goes:
time: 212 us; the launch traced here: 209 us
  waiting for transfers between devices  78.1 us (37%)
  starting transfers between devices  54.5 us (26%)
  Pallas kernels  37.2 us (18%)
  local copies, waits for them, and re-layouts  20.7 us (10%)
  between operations  14.4 us (7%)
  other arithmetic  4.55 us (2%)
    ppermute x19, waiting for transfers between devices, shift_zx(): return lax.ppermute(block, 'seq', route)  48.6 us
    ppermute x19, starting transfers between devices, shift_zx(): return lax.ppermute(block, 'seq', route)  38.8 us
    all_to_all x3, waiting for transfers between devices, exchange(): return lax.all_to_all(split, 'exp', split_axis=0, concat_axis=0, tiled=True)  18.5 us
    unnamed x64, local copies, waits for them, and re-layouts  16.6 us
    pallas_call x1, Pallas kernels, experts(): pl.pallas_call(expert_kernel, out_shape=jax.ShapeDtypeStruct((2 * NY * BA...  16.2 us
    all_to_all x3, starting transfers between devices, exchange(): return lax.all_to_all(split, 'exp', split_axis=0, concat_axis=0, tiled=True)  12.3 us
    ppermute x3, waiting for transfers between devices, along_y(): lax.ppermute(block, 'exp', [(i, (i + 2 * d) % (2 * NY)) for i in range(2...  10.2 us
    pallas_call x1, Pallas kernels, down_part(): pl.pallas_call(functools.partial(down_kernel, runs), out_shape=(jax.Shape...  7.25 us
  transfers between devices with their start and end apart: 28, of which 15 were waited for; matrix products, arithmetic and copies ran while one was open for 3% of the time, Pallas kernels for 9%

commit v1 on v0

--- a/solution.py
+++ b/solution.py
@@ -129,19 +129,36 @@
     )(where, q, *keys, *vals)
 
 
-def gather_rows(rows, earlier):
-    count = rows.shape[0]
-    plane = jnp.concatenate([rows, along_x(rows, 1), along_x(rows, 2), along_x(rows, -1)], axis=0)
-    plane = after(plane, earlier)
+def round_z(block, cut, first=None):
+    ahead, behind = [along_z(block, 1)], [along_z(block, -1)]
+    for i in range(2):
+        a, b = ahead[-1], behind[-1]
+        if i == 0 and first is not None:
+            a, b = after(a, first), after(b, first)
+        ahead.append(along_z(a, 1))
+        behind.append(along_z(b, -1))
+    return ahead, behind, opposite(ahead[2], behind[2], cut, along_z)
+
+
+def gather_rows(rows, above, arrived):
+    half = rows.shape[0] // 2
+    a, b = rows[:half], rows[half:]
+    plane = jnp.concatenate([a, along_x(a, 1), along_x(a, 2), along_x(a, -1)], axis=0)
+    up, down, far = round_z(b, half // 2, above)
+    column = jnp.concatenate([b] + up + down + far, axis=0)
+    depths = (0, 1, 2, 3, 7, 6, 5, 4)
+    plane = after(plane, up[2], down[2])
+    ahead, behind, far = round_z(plane, NX // 2 * half)
     pieces = [(plane, 0)]
-    ahead, behind = plane, plane
-    for dz in (1, 2, 3):
-        ahead, behind = along_z(ahead, 1), along_z(behind, -1)
-        pieces += [(ahead, dz), (behind, NZ - dz)]
-    listed = [[(dx * count, dz, dx) for dx in range(NX)] for _, dz in pieces]
-    far = opposite(ahead, behind, NX // 2 * count, along_z)
-    listed += [[(dx % 2 * count, NZ // 2, dx) for dx in pair] for pair in ((0, 1), (2, 3))]
-    return [p for p, _ in pieces] + far, listed
+    for i in range(3):
+        pieces += [(ahead[i], i + 1), (behind[i], NZ - 1 - i)]
+    listed = [[(dx * half, 0, half, dz, dx) for dx in range(NX)] for _, dz in pieces]
+    listed += [[(dx % 2 * half, 0, half, NZ // 2, dx) for dx in pair] for pair in ((0, 1), (2, 3))]
+    pieces = [p for p, _ in pieces] + far
+    sent = after(column, arrived)
+    pieces += [column] + [along_x(sent, d) for d in (1, 2, -1)]
+    listed += [[(i * half, half, half, dz, dx) for i, dz in enumerate(depths)] for dx in range(NX)]
+    return pieces, listed
 
 
 def project_kernel(where, own, sib, w_own, w_sib, out):
@@ -215,10 +232,10 @@
     z, x = seq // NX, lax.rem(seq, NX)
     part = wd.shape[0] // (NZ * NX)
     for piece, listed in zip(pieces, runs):
-        for first, dz, dx in listed:
+        for first, offset, count, dz, dx in listed:
             source = lax.rem(z + NZ - dz, NZ) * NX + lax.rem(x + NX - dx, NX)
-            row = pl.multiple_of(source * part, part)
-            pltpu.make_async_copy(piece.at[pl.ds(first, part)], wd.at[pl.ds(row, part)], sem).start()
+            row = pl.multiple_of(source * part + offset, count)
+            pltpu.make_async_copy(piece.at[pl.ds(first, count)], wd.at[pl.ds(row, count)], sem).start()
     pltpu.make_async_copy(wd, wd, sem).wait()
     span = 256
     for k in range(wd.shape[0] // span):
@@ -360,7 +377,7 @@
     (k_above, k_loads), (v_above, v_loads) = to_earlier(key_proj), to_earlier(val_proj)
     keys = [key_proj] + earlier_shards(k_above, k_loads)
     vals = [val_proj] + earlier_shards(v_above, v_loads)
-    downs, runs = gather_rows(w_down[0].T, (k_above, v_above))
+    downs, runs = gather_rows(w_down[0].T, k_above, (keys, vals))
     w_sib = swap_core(after(w_out, keys))
 
     flat = routes.reshape(-1)

time: 212 us -> 209 us (0.986)
  local copies, waits for them, and re-layouts: 20.7 us -> 11.5 us
  starting transfers between devices: 54.5 us -> 60.3 us
  waiting for transfers between devices: 78.1 us -> 81.7 us
  other arithmetic: 4.55 us -> 2.27 us
    unnamed x64 -> x48, local copies, waits for them, and re-layouts: 16.6 us -> 8.36 us
    ppermute x19 -> x30, waiting for transfers between devices: 48.6 us -> 55.9 us  [shift_zx(): return lax.ppermute(block, 'seq', route)]
    ppermute x3, waiting for transfers between devices: 10.2 us -> 7.19 us  [along_y(): lax.ppermute(block, 'exp', [(i, (i + 2 * d) % (2 * NY)) for i in range(2...]
    ppermute x3, starting transfers between devices: 3.31 us -> 6.16 us  [along_y(): lax.ppermute(block, 'exp', [(i, (i + 2 * d) % (2 * NY)) for i in range(2...]
    ppermute x19 -> x30, starting transfers between devices: 38.8 us -> 40.1 us  [shift_zx(): return lax.ppermute(block, 'seq', route)]
  transfers between devices with their start and end apart: 28 -> 39, of which waited for: 15 -> 15; matrix products, arithmetic and copies ran while one was open for 3% -> 2% of each run, Pallas kernels for 9% -> 9%
where the time goes in v1:
time: 209 us; the launch traced here: 206 us
  waiting for transfers between devices  81.7 us (39%)
  starting transfers between devices  60.3 us (29%)
  Pallas kernels  36.4 us (17%)
  between operations  14.4 us (7%)
  local copies, waits for them, and re-layouts  11.5 us (6%)
  other arithmetic  2.27 us (1%)
    ppermute x30, waiting for transfers between devices, shift_zx(): return lax.ppermute(block, 'seq', route)  55.9 us
    ppermute x30, starting transfers between devices, shift_zx(): return lax.ppermute(block, 'seq', route)  40.1 us
    all_to_all x3, waiting for transfers between devices, exchange(): return lax.all_to_all(split, 'exp', split_axis=0, concat_axis=0, tiled=True)  18.6 us
    pallas_call x1, Pallas kernels, experts(): pl.pallas_call(expert_kernel, out_shape=jax.ShapeDtypeStruct((2 * NY * BA...  15 us
    all_to_all x3, starting transfers between devices, exchange(): return lax.all_to_all(split, 'exp', split_axis=0, concat_axis=0, tiled=True)  14 us
    unnamed x48, local copies, waits for them, and re-layouts  8.36 us
    pallas_call x1, Pallas kernels, down_part(): pl.pallas_call(functools.partial(down_kernel, runs), out_shape=(jax.Shape...  7.34 us
    ppermute x3, waiting for transfers between devices, along_y(): lax.ppermute(block, 'exp', [(i, (i + 2 * d) % (2 * NY)) for i in range(2...  7.19 us
  transfers between devices with their start and end apart: 39, of which 15 were waited for; matrix products, arithmetic and copies ran while one was open for 2% of the time, Pallas kernels for 9%

profile of v1, /device:TPU:2, one launch (start us, length us, event | category | flops | bytes accessed | tf_op | source)
XLA Modules:
  0.0 206.5 jit_solution(16981775730564339075)
XLA Ops:
  7.2 1.8 pad_maximum_fusion.1
  9.1 1.0 constant_dynamic-update-slice_fusion.8
  10.1 2.3 %collective-permute-start.15 = (bf16[32,1408]{1,0:T(8,128)(2,1)S(1)}, bf16[32,1408]{1,0:T(8,128)(2,1)S(1)}, u32[]{:S(2)}, u32[]{:S(2)}) collective-permute-start(bf16[32,1408]{1,0:T(8,128)(2,1)S(1)} %get-tuple-element.49), channel_id=1, source_target_pairs={{0,24},{8,0},{16,8},{24,16},{32,56},{40,32},{48,40},{56,48},{64,88... | collective-permute-start | bytes 270344 | tf_op jit(solution)/shard_map/ppermute | solution.py:41
  13.1 1.8 collective-permute-start.13
  14.9 1.9 collective-permute-start.16
  16.8 3.9 %collective-permute-start.19 = (bf16[32,1408]{1,0:T(8,128)(2,1)S(1)}, bf16[32,1408]{1,0:T(8,128)(2,1)S(1)}, u32[]{:S(2)}, u32[]{:S(2)}) collective-permute-start(bf16[32,1408]{1,0:T(8,128)(2,1)S(1)} %get-tuple-element.48), channel_id=1, source_target_pairs={{0,224},{8,232},{16,240},{24,248},{32,0},{40,8},{48,16},{56,24},{6... | collective-permute-start | bytes 270344 | tf_op jit(solution)/shard_map/ppermute | solution.py:41
  21.7 1.5 collective-permute-done.16
  23.3 9.7 %collective-permute-done.k4 = bf16[512,256]{1,0:T(8,128)(2,1)S(1)} collective-permute-done((bf16[512,256]{1,0:T(8,128)(2,1)S(1)}, bf16[512,256]{1,0:T(8,128)(2,1)S(1)}, u32[]{:S(2)}, u32[]{:S(2)}) %collective-permute-start) | collective-permute-done | bytes 262176 | tf_op jit(solution)/shard_map/ppermute | solution.py:41
  33.2 1.9 collective-permute-start.2
  35.2 1.4 collective-permute-start.3
  36.5 4.9 %collective-permute-done.4.v4 = bf16[512,256]{1,0:T(8,128)(2,1)S(1)} collective-permute-done((bf16[512,256]{1,0:T(8,128)(2,1)S(1)}, bf16[512,256]{1,0:T(8,128)(2,1)S(1)}, u32[]{:S(2)}, u32[]{:S(2)}) %collective-permute-start.4) | collective-permute-done | bytes 262176 | tf_op jit(solution)/shard_map/ppermute | solution.py:41
  41.5 1.1 collective-permute-start.20
  42.6 2.1 %collective-permute-done.17 = bf16[32,1408]{1,0:T(8,128)(2,1)S(1)} collective-permute-done((bf16[32,1408]{1,0:T(8,128)(2,1)S(1)}, bf16[32,1408]{1,0:T(8,128)(2,1)S(1)}, u32[]{:S(2)}, u32[]{:S(2)}) %collective-permute-start.17) | collective-permute-done | bytes 90144 | tf_op jit(solution)/shard_map/ppermute | solution.py:41
  44.7 2.3 %collective-permute-done.20 = bf16[32,1408]{1,0:T(8,128)(2,1)S(1)} collective-permute-done((bf16[32,1408]{1,0:T(8,128)(2,1)S(1)}, bf16[32,1408]{1,0:T(8,128)(2,1)S(1)}, u32[]{:S(2)}, u32[]{:S(2)}) %collective-permute-start.20) | collective-permute-done | bytes 90144 | tf_op jit(solution)/shard_map/ppermute | solution.py:41
  47.0 2.4 %collective-permute-start.21 = (bf16[32,1408]{1,0:T(8,128)(2,1)S(1)}, bf16[32,1408]{1,0:T(8,128)(2,1)S(1)}, u32[]{:S(2)}, u32[]{:S(2)}) collective-permute-start(bf16[32,1408]{1,0:T(8,128)(2,1)S(1)} %collective-permute-done.20), channel_id=1, source_target_pairs={{0,224},{8,232},{16,240},{24,248},{32,0},{40,8},{48,16},{56,24},{6... | collective-permute-start | bytes 270344 | tf_op jit(solution)/shard_map/ppermute | solution.py:41
  49.4 2.0 collective-permute-done.18
  51.4 1.3 collective-permute-done.21
  52.7 1.3 collective-permute-start.6
  54.0 1.1 collective-permute-start.7
  57.8 2.0 collective-permute-start.23
  61.3 1.9 collective-permute-done.7.v3
  63.2 6.6 %shard_map.139 = bf16[512,256]{1,0:T(8,128)(2,1)S(1)} custom-call(s32[3]{0:T(128)S(1)} %pad_add_fusion.where, bf16[512,256]{1,0:T(8,128)(2,1)S(1)} %copy-done.16, bf16[512,256]{1,0:T(8,128)(2,1)S(1)} %copy-done.6, bf16[512,256]{1,0:T(8,128)(2,1)S(1)} %collective-permute-done.1.k1, bf16[512,256]{1,0:T(8,128)(2,1)S(1)} %collective-permute-done.2.k2, ...), custom_call_target="tpu_custom_call" | custom-call | flops 1342177280 | bytes 6291456 | tf_op jit(solution)/shard_map/pallas_call | solution.py:122
  70.6 1.3 shard_map.142
  71.9 5.5 %all-to-all-start.1 = ((bf16[8,24,2048]{2,1,0:T(8,128)(2,1)}), bf16[8,24,2048]{2,1,0:T(8,128)(2,1)S(1)}, u32[]{:S(2)}, u32[]{:S(2)}) async-start(bf16[8,24,2048]{2,1,0:T(8,128)(2,1)} %bitcast.14), calls=%async_computation.1 | async-start | bytes 1572864 | tf_op jit(solution)/shard_map/all_to_all | solution.py:395
  77.4 2.3 %collective-permute-start.31 = (bf16[16,1408]{1,0:T(8,128)(2,1)}, bf16[16,1408]{1,0:T(8,128)(2,1)S(1)}, u32[]{:S(2)}, u32[]{:S(2)}) collective-permute-start(bf16[16,1408]{1,0:T(8,128)(2,1)} %slice.49), channel_id=1, source_target_pairs={{0,224},{8,232},{16,240},{24,248},{32,0},{40,8},{48,16},{56,24},{6... | collective-permute-start | bytes 135176 | tf_op jit(solution)/shard_map/ppermute | solution.py:41
  80.6 2.5 %shard_map.140 = bf16[4,64,2048]{2,1,0:T(8,128)(2,1)S(1)} custom-call(s32[1]{0:T(128)} %bitcast.where, bf16[4,64,256]{2,1,0:T(8,128)(2,1)S(1)} %copy-done.4, bf16[4,64,256]{2,1,0:T(8,128)(2,1)} %collective-permute-done.8.sib, bf16[256,2048]{1,0:T(8,128)(2,1)S(1)} %copy-done, bf16[256,2048]{1,0:T(8,128)(2,1)S(1)} %collective-permute-done.9.w_sib), custom_call_target="tpu_custom_call" | custom-call | flops 536870912 | bytes 6291456 | tf_op jit(solution)/shard_map/pallas_call | solution.py:171
  83.2 2.0 collective-permute-start.10
  85.2 2.7 %collective-permute-start.11 = (bf16[64,2048]{1,0:T(8,128)(2,1)S(1)}, bf16[64,2048]{1,0:T(8,128)(2,1)S(1)}, u32[]{:S(2)}, u32[]{:S(2)}) collective-permute-start(bf16[64,2048]{1,0:T(8,128)(2,1)S(1)} %get-tuple-element.36), channel_id=1, source_target_pairs={{0,4},{1,5},{2,6},{3,7},{4,0},{5,1},{6,2},{7,3},{8,12},{9,13},{10,... | collective-permute-start | bytes 786440 | tf_op jit(solution)/shard_map/ppermute | solution.py:53
  87.9 1.5 collective-permute-start.12
  90.2 3.2 %collective-permute-start.25 = (bf16[128,1408]{1,0:T(8,128)(2,1)}, bf16[128,1408]{1,0:T(8,128)(2,1)}, u32[]{:S(2)}, u32[]{:S(2)}) collective-permute-start(bf16[128,1408]{1,0:T(8,128)(2,1)} %collective-permute-done.23.refs_2_), channel_id=1, source_target_pairs={{0,224},{8,232},{16,240},{24,248},{32,0},{40,8},{48,16},{56,24},{6... | collective-permute-start | bytes 1081352 | tf_op jit(solution)/shard_map/ppermute | solution.py:41
  93.4 2.6 %collective-permute-done.10.p1 = bf16[64,2048]{1,0:T(8,128)(2,1)S(1)} collective-permute-done((bf16[64,2048]{1,0:T(8,128)(2,1)S(1)}, bf16[64,2048]{1,0:T(8,128)(2,1)S(1)}, u32[]{:S(2)}, u32[]{:S(2)}) %collective-permute-start.10) | collective-permute-done | bytes 262176 | tf_op jit(solution)/shard_map/ppermute | solution.py:53
  96.0 1.2 collective-permute-start.32
  97.2 4.6 %collective-permute-done.11.p2 = bf16[64,2048]{1,0:T(8,128)(2,1)S(1)} collective-permute-done((bf16[64,2048]{1,0:T(8,128)(2,1)S(1)}, bf16[64,2048]{1,0:T(8,128)(2,1)S(1)}, u32[]{:S(2)}, u32[]{:S(2)}) %collective-permute-start.11) | collective-permute-done | bytes 262176 | tf_op jit(solution)/shard_map/ppermute | solution.py:53
  101.8 1.8 collective-permute-start.33
  104.5 1.5 shard_map.141
  106.7 3.5 %all-to-all-start = ((bf16[8,24,2048]{2,1,0:T(8,128)(2,1)}), bf16[8,24,2048]{2,1,0:T(8,128)(2,1)S(1)}, u32[]{:S(2)}, u32[]{:S(2)}) async-start(bf16[8,24,2048]{2,1,0:T(8,128)(2,1)} %bitcast.12), calls=%async_computation | async-start | bytes 1572864 | tf_op jit(solution)/shard_map/all_to_all | solution.py:395
  110.8 3.4 %collective-permute-start.27 = (bf16[128,1408]{1,0:T(8,128)(2,1)}, bf16[128,1408]{1,0:T(8,128)(2,1)S(1)}, u32[]{:S(2)}, u32[]{:S(2)}) collective-permute-start(bf16[128,1408]{1,0:T(8,128)(2,1)} %collective-permute-done.25.refs_4_), channel_id=1, source_target_pairs={{0,224},{8,232},{16,240},{24,248},{32,0},{40,8},{48,16},{56,24},{6... | collective-permute-start | bytes 1081352 | tf_op jit(solution)/shard_map/ppermute | solution.py:41
  114.2 16.7 %collective-permute-done.26.refs_5_ = bf16[128,1408]{1,0:T(8,128)(2,1)S(1)} collective-permute-done((bf16[128,1408]{1,0:T(8,128)(2,1)S(1)}, bf16[128,1408]{1,0:T(8,128)(2,1)S(1)}, u32[]{:S(2)}, u32[]{:S(2)}) %collective-permute-start.26) | collective-permute-done | bytes 360480 | tf_op jit(solution)/shard_map/ppermute | solution.py:41
  131.0 3.3 %collective-permute-start.29 = (bf16[64,1408]{1,0:T(8,128)(2,1)S(1)}, bf16[64,1408]{1,0:T(8,128)(2,1)S(1)}, u32[]{:S(2)}, u32[]{:S(2)}) collective-permute-start(bf16[64,1408]{1,0:T(8,128)(2,1)S(1)} %slice.47), channel_id=1, source_target_pairs={{0,224},{8,232},{16,240},{24,248},{32,0},{40,8},{48,16},{56,24},{6... | collective-permute-start | bytes 540680 | tf_op jit(solution)/shard_map/ppermute | solution.py:41
  134.3 11.8 %collective-permute-done.34.refs_12_ = bf16[256,1408]{1,0:T(8,128)(2,1)} collective-permute-done((bf16[256,1408]{1,0:T(8,128)(2,1)S(1)}, bf16[256,1408]{1,0:T(8,128)(2,1)}, u32[]{:S(2)}, u32[]{:S(2)}) %collective-permute-start.34) | collective-permute-done | bytes 720928 | tf_op jit(solution)/shard_map/ppermute | solution.py:41
  146.1 7.3 %shard_map.143 = (bf16[2048,1408]{1,0:T(8,128)(2,1)S(1)}, f32[192,1408]{1,0:T(8,128)S(1)}) custom-call(s32[3]{0:T(128)S(1)} %pad_add_fusion.where, bf16[192,2048]{1,0:T(8,128)(2,1)S(1)} %bitcast.36, bf16[128,1408]{1,0:T(8,128)(2,1)S(1)} %pad_maximum_fusion.refs_0_, bf16[128,1408]{1,0:T(8,128)(2,1)} %collective-permute-done.22.refs_1_, ...), custom_call_target="tpu_custom_call" | custom-call | flops 1107296256 | bytes 7340032 | tf_op jit(solution)/shard_map/pallas_call | solution.py:250
  153.5 2.4 %copy-done.13 = bf16[2048,1408]{1,0:T(8,128)(2,1)} copy-done((bf16[2048,1408]{1,0:T(8,128)(2,1)}, bf16[2048,1408]{1,0:T(8,128)(2,1)S(1)}, u32[]{:S(2)}) %copy-start.13) | copy-done | bytes 5767192
  155.9 1.0 copy-done.14
  156.9 1.2 copy-done.15
  158.1 15.0 %shard_map.144 = bf16[320,2048]{1,0:T(8,128)(2,1)} custom-call(bf16[192,2048]{1,0:T(8,128)(2,1)S(1)} %bitcast.37, bf16[2048,1408]{1,0:T(8,128)(2,1)} %copy-done.13, f32[192,1408]{1,0:T(8,128)S(1)} %copy-done.15, bf16[32,128,1408]{2,1,0:T(8,128)(2,1)} %bitcast.44), custom_call_target="tpu_custom_call" | custom-call | flops 5536481280 | bytes 14680064 | tf_op jit(solution)/shard_map/pallas_call | solution.py:317
  173.2 4.9 %all-to-all-start.2 = ((bf16[8,40,2048]{2,1,0:T(8,128)(2,1)}), bf16[8,40,2048]{2,1,0:T(8,128)(2,1)S(1)}, u32[]{:S(2)}, u32[]{:S(2)}) async-start(bf16[8,40,2048]{2,1,0:T(8,128)(2,1)} %bitcast.22), calls=%async_computation.2 | async-start | bytes 2621440 | tf_op jit(solution)/shard_map/all_to_all | solution.py:395
  178.3 18.6 %all-to-all-done.2 = bf16[8,40,2048]{2,1,0:T(8,128)(2,1)S(1)} async-done(((bf16[8,40,2048]{2,1,0:T(8,128)(2,1)}), bf16[8,40,2048]{2,1,0:T(8,128)(2,1)S(1)}, u32[]{:S(2)}, u32[]{:S(2)}) %all-to-all-start.2) | async-done | bytes 1310752 | tf_op jit(solution)/shard_map/all_to_all | solution.py:395
  196.9 2.1 %shard_map.145 = (bf16[64,2048]{1,0:T(8,128)(2,1)}, bf16[64,2048]{1,0:T(8,128)(2,1)}, f32[64,2]{1,0:T(8,128)S(1)}) custom-call(bf16[64,2048]{1,0:T(8,128)(2,1)S(1)} %copy-done.11, bf16[64,2048]{1,0:T(8,128)(2,1)S(1)} %copy-done.1, bf16[320,2048]{1,0:T(8,128)(2,1)S(1)} %bitcast.35, s32[64,2]{1,0:T(8,128)S(1)} %add.31.target, f32[64,2]{1,0:T(8,128)S(1)} %copy.44.prob, ...), custom_call_target="tpu_custom_call" | custom-call | flops 268435456 | bytes 3145728 | tf_op jit(solution)/shard_map/pallas_call | solution.py:359
  (106 shorter events, 11.7 us)
Async XLA Ops:
  7.2 14.3 %copy-start.5 = (bf16[512,256]{1,0:T(8,128)(2,1)S(1)}, bf16[512,256]{1,0:T(8,128)(2,1)}, u32[]{:S(2)}) copy-start(bf16[512,256]{1,0:T(8,128)(2,1)} %k0.1) | copy-start | bytes 786436
  7.2 14.4 %copy-start.7 = (bf16[512,256]{1,0:T(8,128)(2,1)S(1)}, bf16[512,256]{1,0:T(8,128)(2,1)}, u32[]{:S(2)}) copy-start(bf16[512,256]{1,0:T(8,128)(2,1)} %v0.1) | copy-start | bytes 786436
  7.2 149.7 %all-gather.3.cloned.1.call-start = ((), (), s32[]{:S(2)}) async-start(), calls=%async_computation.3 | async-start | bytes 11894784 | tf_op jit(solution)/shard_map/all_gather | solution.py:376
  10.1 11.4 %collective-permute-start.15 = (bf16[32,1408]{1,0:T(8,128)(2,1)S(1)}, bf16[32,1408]{1,0:T(8,128)(2,1)S(1)}, u32[]{:S(2)}, u32[]{:S(2)}) collective-permute-start(bf16[32,1408]{1,0:T(8,128)(2,1)S(1)} %get-tuple-element.49), channel_id=1, source_target_pairs={{0,24},{8,0},{16,8},{24,16},{32,56},{40,32},{48,40},{56,48},{64,88... | collective-permute-start | bytes 270344 | tf_op jit(solution)/shard_map/ppermute | solution.py:41
  12.4 9.2 %collective-permute-start.14 = (bf16[32,1408]{1,0:T(8,128)(2,1)S(1)}, bf16[32,1408]{1,0:T(8,128)(2,1)S(1)}, u32[]{:S(2)}, u32[]{:S(2)}) collective-permute-start(bf16[32,1408]{1,0:T(8,128)(2,1)S(1)} %get-tuple-element.49), channel_id=1, source_target_pairs={{0,16},{8,24},{16,0},{24,8},{32,48},{40,56},{48,32},{56,40},{64,80... | collective-permute-start | bytes 270344 | tf_op jit(solution)/shard_map/ppermute | solution.py:41
  13.1 8.6 %collective-permute-start.13 = (bf16[32,1408]{1,0:T(8,128)(2,1)S(1)}, bf16[32,1408]{1,0:T(8,128)(2,1)S(1)}, u32[]{:S(2)}, u32[]{:S(2)}) collective-permute-start(bf16[32,1408]{1,0:T(8,128)(2,1)S(1)} %get-tuple-element.49), channel_id=1, source_target_pairs={{0,8},{8,16},{16,24},{24,0},{32,40},{40,48},{48,56},{56,32},{64,72... | collective-permute-start | bytes 270344 | tf_op jit(solution)/shard_map/ppermute | solution.py:41
  14.9 8.4 %collective-permute-start.16 = (bf16[32,1408]{1,0:T(8,128)(2,1)S(1)}, bf16[32,1408]{1,0:T(8,128)(2,1)S(1)}, u32[]{:S(2)}, u32[]{:S(2)}) collective-permute-start(bf16[32,1408]{1,0:T(8,128)(2,1)S(1)} %get-tuple-element.48), channel_id=1, source_target_pairs={{0,32},{8,40},{16,48},{24,56},{32,64},{40,72},{48,80},{56,88},{64,... | collective-permute-start | bytes 270344 | tf_op jit(solution)/shard_map/ppermute | solution.py:41
  16.8 19.7 %collective-permute-start.19 = (bf16[32,1408]{1,0:T(8,128)(2,1)S(1)}, bf16[32,1408]{1,0:T(8,128)(2,1)S(1)}, u32[]{:S(2)}, u32[]{:S(2)}) collective-permute-start(bf16[32,1408]{1,0:T(8,128)(2,1)S(1)} %get-tuple-element.48), channel_id=1, source_target_pairs={{0,224},{8,232},{16,240},{24,248},{32,0},{40,8},{48,16},{56,24},{6... | collective-permute-start | bytes 270344 | tf_op jit(solution)/shard_map/ppermute | solution.py:41
  21.5 11.5 %collective-permute-start = (bf16[512,256]{1,0:T(8,128)(2,1)S(1)}, bf16[512,256]{1,0:T(8,128)(2,1)S(1)}, u32[]{:S(2)}, u32[]{:S(2)}) collective-permute-start(bf16[512,256]{1,0:T(8,128)(2,1)S(1)} %copy-done.5), channel_id=1, source_target_pairs={{0,32},{8,40},{16,48},{24,56},{32,64},{40,72},{48,80},{56,88},{64,... | collective-permute-start | bytes 786440 | tf_op jit(solution)/shard_map/ppermute | solution.py:41
  21.6 19.9 %collective-permute-start.4 = (bf16[512,256]{1,0:T(8,128)(2,1)S(1)}, bf16[512,256]{1,0:T(8,128)(2,1)S(1)}, u32[]{:S(2)}, u32[]{:S(2)}) collective-permute-start(bf16[512,256]{1,0:T(8,128)(2,1)S(1)} %copy-done.7), channel_id=1, source_target_pairs={{0,32},{8,40},{16,48},{24,56},{32,64},{40,72},{48,80},{56,88},{64,... | collective-permute-start | bytes 786440 | tf_op jit(solution)/shard_map/ppermute | solution.py:41
  23.3 32.6 %copy-start = (bf16[256,2048]{1,0:T(8,128)(2,1)S(1)}, bf16[256,2048]{1,0:T(8,128)(2,1)}, u32[]{:S(2)}) copy-start(bf16[256,2048]{1,0:T(8,128)(2,1)} %w_own.1) | copy-start | bytes 3145732
  33.1 30.1 %copy-start.6 = (bf16[512,256]{1,0:T(8,128)(2,1)S(1)}, bf16[512,256]{1,0:T(8,128)(2,1)}, u32[]{:S(2)}) copy-start(bf16[512,256]{1,0:T(8,128)(2,1)} %k0.1) | copy-start | bytes 786436
  33.1 30.1 %copy-start.8 = (bf16[512,256]{1,0:T(8,128)(2,1)S(1)}, bf16[512,256]{1,0:T(8,128)(2,1)}, u32[]{:S(2)}) copy-start(bf16[512,256]{1,0:T(8,128)(2,1)} %v0.1) | copy-start | bytes 786436
  33.1 30.1 %copy-start.16 = (bf16[512,256]{1,0:T(8,128)(2,1)S(1)}, bf16[512,256]{1,0:T(8,128)(2,1)}, u32[]{:S(2)}) copy-start(bf16[512,256]{1,0:T(8,128)(2,1)} %q.1) | copy-start | bytes 786436
  33.1 20.9 %collective-permute-start.1 = (bf16[512,256]{1,0:T(8,128)(2,1)S(1)}, bf16[512,256]{1,0:T(8,128)(2,1)S(1)}, u32[]{:S(2)}, u32[]{:S(2)}) collective-permute-start(bf16[512,256]{1,0:T(8,128)(2,1)S(1)} %get-tuple-element.44), channel_id=1, source_target_pairs={{0,8},{8,16},{16,24},{24,0},{32,40},{40,48},{48,56},{56,32},{64,72... | collective-permute-start | bytes 786440 | tf_op jit(solution)/shard_map/ppermute | solution.py:41
  33.2 22.0 %collective-permute-start.2 = (bf16[512,256]{1,0:T(8,128)(2,1)S(1)}, bf16[512,256]{1,0:T(8,128)(2,1)S(1)}, u32[]{:S(2)}, u32[]{:S(2)}) collective-permute-start(bf16[512,256]{1,0:T(8,128)(2,1)S(1)} %get-tuple-element.43), channel_id=1, source_target_pairs={{0,16},{8,24},{16,0},{24,8},{32,48},{40,56},{48,32},{56,40},{64,80... | collective-permute-start | bytes 786440 | tf_op jit(solution)/shard_map/ppermute | solution.py:41
  35.2 20.7 %collective-permute-start.3 = (bf16[512,256]{1,0:T(8,128)(2,1)S(1)}, bf16[512,256]{1,0:T(8,128)(2,1)S(1)}, u32[]{:S(2)}, u32[]{:S(2)}) collective-permute-start(bf16[512,256]{1,0:T(8,128)(2,1)S(1)} %get-tuple-element.42), channel_id=1, source_target_pairs={{0,24},{8,0},{16,8},{24,16},{32,56},{40,32},{48,40},{56,48},{64,88... | collective-permute-start | bytes 786440 | tf_op jit(solution)/shard_map/ppermute | solution.py:41
  36.5 8.2 %collective-permute-start.17 = (bf16[32,1408]{1,0:T(8,128)(2,1)S(1)}, bf16[32,1408]{1,0:T(8,128)(2,1)S(1)}, u32[]{:S(2)}, u32[]{:S(2)}) collective-permute-start(bf16[32,1408]{1,0:T(8,128)(2,1)S(1)} %collective-permute-done.16), channel_id=1, source_target_pairs={{0,32},{8,40},{16,48},{24,56},{32,64},{40,72},{48,80},{56,88},{64,... | collective-permute-start | bytes 270344 | tf_op jit(solution)/shard_map/ppermute | solution.py:41
  41.5 5.5 %collective-permute-start.20 = (bf16[32,1408]{1,0:T(8,128)(2,1)S(1)}, bf16[32,1408]{1,0:T(8,128)(2,1)S(1)}, u32[]{:S(2)}, u32[]{:S(2)}) collective-permute-start(bf16[32,1408]{1,0:T(8,128)(2,1)S(1)} %collective-permute-done.19), channel_id=1, source_target_pairs={{0,224},{8,232},{16,240},{24,248},{32,0},{40,8},{48,16},{56,24},{6... | collective-permute-start | bytes 270344 | tf_op jit(solution)/shard_map/ppermute | solution.py:41
  44.7 6.7 %collective-permute-start.18 = (bf16[32,1408]{1,0:T(8,128)(2,1)S(1)}, bf16[32,1408]{1,0:T(8,128)(2,1)S(1)}, u32[]{:S(2)}, u32[]{:S(2)}) collective-permute-start(bf16[32,1408]{1,0:T(8,128)(2,1)S(1)} %collective-permute-done.17), channel_id=1, source_target_pairs={{0,32},{8,40},{16,48},{24,56},{32,64},{40,72},{48,80},{56,88},{64,... | collective-permute-start | bytes 270344 | tf_op jit(solution)/shard_map/ppermute | solution.py:41
  47.0 5.8 %collective-permute-start.21 = (bf16[32,1408]{1,0:T(8,128)(2,1)S(1)}, bf16[32,1408]{1,0:T(8,128)(2,1)S(1)}, u32[]{:S(2)}, u32[]{:S(2)}) collective-permute-start(bf16[32,1408]{1,0:T(8,128)(2,1)S(1)} %collective-permute-done.20), channel_id=1, source_target_pairs={{0,224},{8,232},{16,240},{24,248},{32,0},{40,8},{48,16},{56,24},{6... | collective-permute-start | bytes 270344 | tf_op jit(solution)/shard_map/ppermute | solution.py:41
  51.4 6.4 %collective-permute-start.5 = (bf16[512,256]{1,0:T(8,128)(2,1)S(1)}, bf16[512,256]{1,0:T(8,128)(2,1)S(1)}, u32[]{:S(2)}, u32[]{:S(2)}) collective-permute-start(bf16[512,256]{1,0:T(8,128)(2,1)S(1)} %get-tuple-element.41), channel_id=1, source_target_pairs={{0,8},{8,16},{16,24},{24,0},{32,40},{40,48},{48,56},{56,32},{64,72... | collective-permute-start | bytes 786440 | tf_op jit(solution)/shard_map/ppermute | solution.py:41
  52.7 8.0 %collective-permute-start.6 = (bf16[512,256]{1,0:T(8,128)(2,1)S(1)}, bf16[512,256]{1,0:T(8,128)(2,1)S(1)}, u32[]{:S(2)}, u32[]{:S(2)}) collective-permute-start(bf16[512,256]{1,0:T(8,128)(2,1)S(1)} %get-tuple-element.40), channel_id=1, source_target_pairs={{0,16},{8,24},{16,0},{24,8},{32,48},{40,56},{48,32},{56,40},{64,80... | collective-permute-start | bytes 786440 | tf_op jit(solution)/shard_map/ppermute | solution.py:41
  54.0 9.2 %collective-permute-start.7 = (bf16[512,256]{1,0:T(8,128)(2,1)S(1)}, bf16[512,256]{1,0:T(8,128)(2,1)S(1)}, u32[]{:S(2)}, u32[]{:S(2)}) collective-permute-start(bf16[512,256]{1,0:T(8,128)(2,1)S(1)} %get-tuple-element.39), channel_id=1, source_target_pairs={{0,24},{8,0},{16,8},{24,16},{32,56},{40,32},{48,40},{56,48},{64,88... | collective-permute-start | bytes 786440 | tf_op jit(solution)/shard_map/ppermute | solution.py:41
  55.2 35.0 %collective-permute-start.22 = (bf16[128,1408]{1,0:T(8,128)(2,1)S(1)}, bf16[128,1408]{1,0:T(8,128)(2,1)}, u32[]{:S(2)}, u32[]{:S(2)}) collective-permute-start(bf16[128,1408]{1,0:T(8,128)(2,1)S(1)} %pad_maximum_fusion.refs_0_), channel_id=1, source_target_pairs={{0,32},{8,40},{16,48},{24,56},{32,64},{40,72},{48,80},{56,88},{64,... | collective-permute-start | bytes 1081352 | tf_op jit(solution)/shard_map/ppermute | solution.py:41
  55.8 23.8 %collective-permute-start.9 = (bf16[256,2048]{1,0:T(8,128)(2,1)S(1)}, bf16[256,2048]{1,0:T(8,128)(2,1)S(1)}, u32[]{:S(2)}, u32[]{:S(2)}) collective-permute-start(bf16[256,2048]{1,0:T(8,128)(2,1)S(1)} %copy-done), channel_id=1, source_target_pairs={{0,1},{1,0},{2,3},{3,2},{4,5},{5,4},{6,7},{7,6},{8,9},{9,8},{10,11... | collective-permute-start | bytes 3145736 | tf_op jit(solution)/shard_map/ppermute | solution.py:57
  57.8 32.4 %collective-permute-start.23 = (bf16[128,1408]{1,0:T(8,128)(2,1)S(1)}, bf16[128,1408]{1,0:T(8,128)(2,1)}, u32[]{:S(2)}, u32[]{:S(2)}) collective-permute-start(bf16[128,1408]{1,0:T(8,128)(2,1)S(1)} %pad_maximum_fusion.refs_0_), channel_id=1, source_target_pairs={{0,224},{8,232},{16,240},{24,248},{32,0},{40,8},{48,16},{56,24},{6... | collective-permute-start | bytes 1081352 | tf_op jit(solution)/shard_map/ppermute | solution.py:41
  60.7 24.5 %collective-permute-start.30 = (bf16[16,1408]{1,0:T(8,128)(2,1)}, bf16[16,1408]{1,0:T(8,128)(2,1)}, u32[]{:S(2)}, u32[]{:S(2)}) collective-permute-start(bf16[16,1408]{1,0:T(8,128)(2,1)} %slice.48), channel_id=1, source_target_pairs={{0,32},{8,40},{16,48},{24,56},{32,64},{40,72},{48,80},{56,88},{64,... | collective-permute-start | bytes 135176 | tf_op jit(solution)/shard_map/ppermute | solution.py:41
  70.6 6.8 %collective-permute-start.8 = (bf16[4,64,256]{2,1,0:T(8,128)(2,1)}, bf16[4,64,256]{2,1,0:T(8,128)(2,1)}, u32[]{:S(2)}, u32[]{:S(2)}) collective-permute-start(bf16[4,64,256]{2,1,0:T(8,128)(2,1)} %get-tuple-element.45), channel_id=1, source_target_pairs={{0,1},{1,0},{2,3},{3,2},{4,5},{5,4},{6,7},{7,6},{8,9},{9,8},{10,11... | collective-permute-start | bytes 393224 | tf_op jit(solution)/shard_map/ppermute | solution.py:57
  71.9 34.8 %all-to-all-start.1 = ((bf16[8,24,2048]{2,1,0:T(8,128)(2,1)}), bf16[8,24,2048]{2,1,0:T(8,128)(2,1)S(1)}, u32[]{:S(2)}, u32[]{:S(2)}) async-start(bf16[8,24,2048]{2,1,0:T(8,128)(2,1)} %bitcast.14), calls=%async_computation.1 | async-start | bytes 1572864 | tf_op jit(solution)/shard_map/all_to_all | solution.py:395
  77.4 10.5 %collective-permute-start.31 = (bf16[16,1408]{1,0:T(8,128)(2,1)}, bf16[16,1408]{1,0:T(8,128)(2,1)S(1)}, u32[]{:S(2)}, u32[]{:S(2)}) collective-permute-start(bf16[16,1408]{1,0:T(8,128)(2,1)} %slice.49), channel_id=1, source_target_pairs={{0,224},{8,232},{16,240},{24,248},{32,0},{40,8},{48,16},{56,24},{6... | collective-permute-start | bytes 135176 | tf_op jit(solution)/shard_map/ppermute | solution.py:41
  83.1 21.4 %copy-start.9 = (bf16[64,2048]{1,0:T(8,128)(2,1)S(1)}, bf16[64,2048]{1,0:T(8,128)(2,1)}, u32[]{:S(2)}) copy-start(bf16[64,2048]{1,0:T(8,128)(2,1)} %x.1) | copy-start | bytes 786436
  83.1 21.4 %copy-start.12 = (f32[2048]{0:T(1024)S(1)}, f32[2048]{0:T(1024)}, u32[]{:S(2)}) copy-start(f32[2048]{0:T(1024)} %param.17) | copy-start | bytes 24580
  83.2 12.8 %collective-permute-start.10 = (bf16[64,2048]{1,0:T(8,128)(2,1)S(1)}, bf16[64,2048]{1,0:T(8,128)(2,1)S(1)}, u32[]{:S(2)}, u32[]{:S(2)}) collective-permute-start(bf16[64,2048]{1,0:T(8,128)(2,1)S(1)} %get-tuple-element.37), channel_id=1, source_target_pairs={{0,2},{1,3},{2,4},{3,5},{4,6},{5,7},{6,0},{7,1},{8,10},{9,11},{10,... | collective-permute-start | bytes 786440 | tf_op jit(solution)/shard_map/ppermute | solution.py:53
  85.2 16.6 %collective-permute-start.11 = (bf16[64,2048]{1,0:T(8,128)(2,1)S(1)}, bf16[64,2048]{1,0:T(8,128)(2,1)S(1)}, u32[]{:S(2)}, u32[]{:S(2)}) collective-permute-start(bf16[64,2048]{1,0:T(8,128)(2,1)S(1)} %get-tuple-element.36), channel_id=1, source_target_pairs={{0,4},{1,5},{2,6},{3,7},{4,0},{5,1},{6,2},{7,3},{8,12},{9,13},{10,... | collective-permute-start | bytes 786440 | tf_op jit(solution)/shard_map/ppermute | solution.py:53
  87.9 15.7 %collective-permute-start.12 = (bf16[64,2048]{1,0:T(8,128)(2,1)S(1)}, bf16[64,2048]{1,0:T(8,128)(2,1)S(1)}, u32[]{:S(2)}, u32[]{:S(2)}) collective-permute-start(bf16[64,2048]{1,0:T(8,128)(2,1)S(1)} %get-tuple-element.35), channel_id=1, source_target_pairs={{0,6},{1,7},{2,0},{3,1},{4,2},{5,3},{6,4},{7,5},{8,14},{9,15},{10,... | collective-permute-start | bytes 786440 | tf_op jit(solution)/shard_map/ppermute | solution.py:53
  90.2 20.1 %collective-permute-start.24 = (bf16[128,1408]{1,0:T(8,128)(2,1)}, bf16[128,1408]{1,0:T(8,128)(2,1)S(1)}, u32[]{:S(2)}, u32[]{:S(2)}) collective-permute-start(bf16[128,1408]{1,0:T(8,128)(2,1)} %collective-permute-done.22.refs_1_), channel_id=1, source_target_pairs={{0,32},{8,40},{16,48},{24,56},{32,64},{40,72},{48,80},{56,88},{64,... | collective-permute-start | bytes 1081352 | tf_op jit(solution)/shard_map/ppermute | solution.py:41
  90.2 20.6 %collective-permute-start.25 = (bf16[128,1408]{1,0:T(8,128)(2,1)}, bf16[128,1408]{1,0:T(8,128)(2,1)}, u32[]{:S(2)}, u32[]{:S(2)}) collective-permute-start(bf16[128,1408]{1,0:T(8,128)(2,1)} %collective-permute-done.23.refs_2_), channel_id=1, source_target_pairs={{0,224},{8,232},{16,240},{24,248},{32,0},{40,8},{48,16},{56,24},{6... | collective-permute-start | bytes 1081352 | tf_op jit(solution)/shard_map/ppermute | solution.py:41
  96.0 38.3 %collective-permute-start.32 = (bf16[256,1408]{1,0:T(8,128)(2,1)S(1)}, bf16[256,1408]{1,0:T(8,128)(2,1)}, u32[]{:S(2)}, u32[]{:S(2)}) collective-permute-start(bf16[256,1408]{1,0:T(8,128)(2,1)S(1)} %constant_dynamic-update-slice_fusion.refs_9_), channel_id=1, source_target_pairs={{0,8},{8,16},{16,24},{24,0},{32,40},{40,48},{48,56},{56,32},{64,72... | collective-permute-start | bytes 2162696 | tf_op jit(solution)/shard_map/ppermute | solution.py:41
  101.8 32.5 %collective-permute-start.33 = (bf16[256,1408]{1,0:T(8,128)(2,1)S(1)}, bf16[256,1408]{1,0:T(8,128)(2,1)}, u32[]{:S(2)}, u32[]{:S(2)}) collective-permute-start(bf16[256,1408]{1,0:T(8,128)(2,1)S(1)} %constant_dynamic-update-slice_fusion.refs_9_), channel_id=1, source_target_pairs={{0,16},{8,24},{16,0},{24,8},{32,48},{40,56},{48,32},{56,40},{64,80... | collective-permute-start | bytes 2162696 | tf_op jit(solution)/shard_map/ppermute | solution.py:41
  103.6 42.5 %collective-permute-start.34 = (bf16[256,1408]{1,0:T(8,128)(2,1)S(1)}, bf16[256,1408]{1,0:T(8,128)(2,1)}, u32[]{:S(2)}, u32[]{:S(2)}) collective-permute-start(bf16[256,1408]{1,0:T(8,128)(2,1)S(1)} %constant_dynamic-update-slice_fusion.refs_9_), channel_id=1, source_target_pairs={{0,24},{8,0},{16,8},{24,16},{32,56},{40,32},{48,40},{56,48},{64,88... | collective-permute-start | bytes 2162696 | tf_op jit(solution)/shard_map/ppermute | solution.py:41
  106.7 50.2 %all-to-all-start = ((bf16[8,24,2048]{2,1,0:T(8,128)(2,1)}), bf16[8,24,2048]{2,1,0:T(8,128)(2,1)S(1)}, u32[]{:S(2)}, u32[]{:S(2)}) async-start(bf16[8,24,2048]{2,1,0:T(8,128)(2,1)} %bitcast.12), calls=%async_computation | async-start | bytes 1572864 | tf_op jit(solution)/shard_map/all_to_all | solution.py:395
  110.2 20.7 %collective-permute-start.26 = (bf16[128,1408]{1,0:T(8,128)(2,1)S(1)}, bf16[128,1408]{1,0:T(8,128)(2,1)S(1)}, u32[]{:S(2)}, u32[]{:S(2)}) collective-permute-start(bf16[128,1408]{1,0:T(8,128)(2,1)S(1)} %collective-permute-done.24.refs_3_), channel_id=1, source_target_pairs={{0,32},{8,40},{16,48},{24,56},{32,64},{40,72},{48,80},{56,88},{64,... | collective-permute-start | bytes 1081352 | tf_op jit(solution)/shard_map/ppermute | solution.py:41
  110.8 20.2 %collective-permute-start.27 = (bf16[128,1408]{1,0:T(8,128)(2,1)}, bf16[128,1408]{1,0:T(8,128)(2,1)S(1)}, u32[]{:S(2)}, u32[]{:S(2)}) collective-permute-start(bf16[128,1408]{1,0:T(8,128)(2,1)} %collective-permute-done.25.refs_4_), channel_id=1, source_target_pairs={{0,224},{8,232},{16,240},{24,248},{32,0},{40,8},{48,16},{56,24},{6... | collective-permute-start | bytes 1081352 | tf_op jit(solution)/shard_map/ppermute | solution.py:41
  130.9 15.2 %collective-permute-start.28 = (bf16[64,1408]{1,0:T(8,128)(2,1)S(1)}, bf16[64,1408]{1,0:T(8,128)(2,1)S(1)}, u32[]{:S(2)}, u32[]{:S(2)}) collective-permute-start(bf16[64,1408]{1,0:T(8,128)(2,1)S(1)} %slice.46), channel_id=1, source_target_pairs={{0,32},{8,40},{16,48},{24,56},{32,64},{40,72},{48,80},{56,88},{64,... | collective-permute-start | bytes 540680 | tf_op jit(solution)/shard_map/ppermute | solution.py:41
  131.0 15.1 %collective-permute-start.29 = (bf16[64,1408]{1,0:T(8,128)(2,1)S(1)}, bf16[64,1408]{1,0:T(8,128)(2,1)S(1)}, u32[]{:S(2)}, u32[]{:S(2)}) collective-permute-start(bf16[64,1408]{1,0:T(8,128)(2,1)S(1)} %slice.47), channel_id=1, source_target_pairs={{0,224},{8,232},{16,240},{24,248},{32,0},{40,8},{48,16},{56,24},{6... | collective-permute-start | bytes 540680 | tf_op jit(solution)/shard_map/ppermute | solution.py:41
  173.1 23.7 %copy-start.11 = (bf16[64,2048]{1,0:T(8,128)(2,1)S(1)}, bf16[64,2048]{1,0:T(8,128)(2,1)}, u32[]{:S(2)}) copy-start(bf16[64,2048]{1,0:T(8,128)(2,1)} %copy-done.10) | copy-start | bytes 786436
  173.2 23.7 %all-to-all-start.2 = ((bf16[8,40,2048]{2,1,0:T(8,128)(2,1)}), bf16[8,40,2048]{2,1,0:T(8,128)(2,1)S(1)}, u32[]{:S(2)}, u32[]{:S(2)}) async-start(bf16[8,40,2048]{2,1,0:T(8,128)(2,1)} %bitcast.22), calls=%async_computation.2 | async-start | bytes 2621440 | tf_op jit(solution)/shard_map/all_to_all | solution.py:395
  (10 other events, 46.0 us)
Sparse Core Ops, SparseCore 0:
  10.6 142.8 all-gather.2

commit v2 on v1

--- a/solution.py
+++ b/solution.py
@@ -79,9 +79,9 @@
     return [along_x(loads[0], 1), along_x(loads[1], 2), along_x(loads[2], -1), above]
 
 
-def attention_kernel(where, q, k0, k1, k2, k3, k4, v0, v1, v2, v3, v4, out):
-    keys, vals = (k0, k1, k2, k3, k4), (v0, v1, v2, v3, v4)
-    rows, span = 128, k0.shape[0]
+def attention_kernel(where, q, *refs):
+    both, out = refs[:-1], refs[-1]
+    rows, span = 128, both[0].shape[0] // 2
     scale = 1.0 / math.sqrt(HD)
     seq = where[0]
 
@@ -94,7 +94,7 @@
             queries = q[pl.ds(at, rows), cols]
             scores = []
             for d in range(5):
-                s = nt(queries, keys[d][:, cols]) * scale
+                s = nt(queries, both[d][:span, cols]) * scale
                 if d == 0:
                     s = jnp.where(kpos <= qpos, s, -jnp.inf)
                 elif d == 4:
@@ -111,22 +111,22 @@
             for d in range(5):
                 e = jnp.exp(scores[d] - top)
                 total = total + e
-                mixed = mixed + nn(e.astype(BF16), vals[d][:, cols])
+                mixed = mixed + nn(e.astype(BF16), both[d][span:, cols])
             out[pl.ds(at, rows), cols] = (mixed / jnp.sum(total, axis=-1, keepdims=True)).astype(BF16)
         return 0
 
     lax.fori_loop(0, q.shape[0] // rows, block, 0)
 
 
-def attention(where, q, keys, vals):
+def attention(where, q, both):
     return pl.pallas_call(
         attention_kernel,
         out_shape=jax.ShapeDtypeStruct(q.shape, BF16),
-        in_specs=[SMEM] + [VMEM] * 11,
+        in_specs=[SMEM] + [VMEM] * (1 + len(both)),
         out_specs=VMEM,
         compiler_params=params(24),
         cost_estimate=pl.CostEstimate(flops=4 * 512 * 2560 * 256, bytes_accessed=6 * 2**20, transcendentals=512 * 2560 * 2),
-    )(where, q, *keys, *vals)
+    )(where, q, *both)
 
 
 def round_z(block, cut, first=None):
@@ -147,7 +147,7 @@
     up, down, far = round_z(b, half // 2, above)
     column = jnp.concatenate([b] + up + down + far, axis=0)
     depths = (0, 1, 2, 3, 7, 6, 5, 4)
-    plane = after(plane, up[2], down[2])
+    plane = after(plane, far)
     ahead, behind, far = round_z(plane, NX // 2 * half)
     pieces = [(plane, 0)]
     for i in range(3):
@@ -226,9 +226,7 @@
     )(rows, target_rows)
 
 
-def down_kernel(runs, where, rows_grad, *refs):
-    pieces, (wd, back, sem) = refs[: len(runs)], refs[len(runs) :]
-    seq = where[0]
+def fetch_rows(runs, seq, pieces, wd, sem):
     z, x = seq // NX, lax.rem(seq, NX)
     part = wd.shape[0] // (NZ * NX)
     for piece, listed in zip(pieces, runs):
@@ -236,6 +234,11 @@
             source = lax.rem(z + NZ - dz, NZ) * NX + lax.rem(x + NX - dx, NX)
             row = pl.multiple_of(source * part + offset, count)
             pltpu.make_async_copy(piece.at[pl.ds(first, count)], wd.at[pl.ds(row, count)], sem).start()
+
+
+def down_kernel(runs, where, rows_grad, *refs):
+    pieces, (back, wd, sem) = refs[: len(runs)], refs[len(runs) :]
+    fetch_rows(runs, where[0], pieces, wd, sem)
     pltpu.make_async_copy(wd, wd, sem).wait()
     span = 256
     for k in range(wd.shape[0] // span):
@@ -249,16 +252,17 @@
     hidden = pieces[0].shape[1]
     return pl.pallas_call(
         functools.partial(down_kernel, runs),
-        out_shape=(jax.ShapeDtypeStruct((width, hidden), BF16), jax.ShapeDtypeStruct((rows, hidden), F32)),
+        out_shape=jax.ShapeDtypeStruct((rows, hidden), F32),
         in_specs=[SMEM, VMEM] + [HBM] * len(pieces),
-        out_specs=(VMEM, VMEM),
-        scratch_shapes=[pltpu.SemaphoreType.DMA(())],
+        out_specs=VMEM,
+        scratch_shapes=[pltpu.VMEM((width, hidden), BF16), pltpu.SemaphoreType.DMA(())],
         compiler_params=params(16),
         cost_estimate=pl.CostEstimate(flops=2 * rows * width * hidden, bytes_accessed=7 * 2**20, transcendentals=0),
     )(where, rows_grad, *pieces)
 
 
-def expert_kernel(rows_in, down, ba, chunk, both, wg, wu, wd, ga, ua, hid, gpg, gpu, sems, down_sem):
+def expert_kernel(runs, where, rows_in, ba, chunk, *refs):
+    pieces, (both, wg, wu, wd, ga, ua, hid, gpg, gpu, sems, down_sem) = refs[: len(runs)], refs[len(runs) :]
     shards = chunk.shape[0]
     part = chunk.shape[1] // 2
     mats = (wg, wu)
@@ -275,8 +279,7 @@
         return 0
 
     lax.fori_loop(0, shards, start, 0)
-    fetch = pltpu.make_async_copy(down, wd, down_sem)
-    fetch.start()
+    fetch_rows(runs, where[0], pieces, wd, down_sem)
     for k in range(steps):
         cols = pl.ds(k * span, span)
         for m, acc in ((0, ga), (1, ua)):
@@ -296,7 +299,7 @@
         return 0
 
     lax.fori_loop(0, hid.shape[0] // 16, point, 0)
-    fetch.wait()
+    pltpu.make_async_copy(wd, wd, down_sem).wait()
     sources = 2 * NY
 
     def finish(k, _):
@@ -311,23 +314,23 @@
     lax.fori_loop(0, steps, finish, 0)
 
 
-def experts(rows_in, wd, back, chunk):
+def experts(where, rows_in, back, chunk, pieces, runs):
     rows, width = rows_in.shape
     shards, hidden = chunk.shape[0], chunk.shape[2]
     return pl.pallas_call(
-        expert_kernel,
+        functools.partial(expert_kernel, runs),
         out_shape=jax.ShapeDtypeStruct((2 * NY * BACK, width), BF16),
-        in_specs=[VMEM, HBM, VMEM, HBM],
+        in_specs=[SMEM, VMEM, VMEM, HBM] + [HBM] * len(pieces),
         out_specs=VMEM,
         scratch_shapes=[pltpu.VMEM((width, hidden), BF16)] * 3
         + [pltpu.VMEM((rows, hidden), F32)] * 2
         + [pltpu.VMEM((rows, hidden), BF16)] * 3
         + [pltpu.SemaphoreType.DMA((2, shards // 4)), pltpu.SemaphoreType.DMA(())],
-        compiler_params=params(50),
+        compiler_params=params(47),
         cost_estimate=pl.CostEstimate(
             flops=10 * rows * width * hidden, bytes_accessed=14 * 2**20, transcendentals=rows * hidden
         ),
-    )(rows_in, wd, back, chunk)
+    )(where, rows_in, back, chunk, *pieces)
 
 
 def combine_kernel(hidden, grad_out, rows, target, prob, gain, layer_out, grad_in, grad_gate):
@@ -374,11 +377,11 @@
     where = jnp.stack([me_seq, me_exp // 2, me_exp % 2]).astype(jnp.int32)
     core, y = me_exp % 2, me_exp // 2
     chunk = lax.all_gather(jnp.concatenate([w_gate[0], w_up[0]], axis=0), "seq", axis=0)
-    (k_above, k_loads), (v_above, v_loads) = to_earlier(key_proj), to_earlier(val_proj)
-    keys = [key_proj] + earlier_shards(k_above, k_loads)
-    vals = [val_proj] + earlier_shards(v_above, v_loads)
-    downs, runs = gather_rows(w_down[0].T, k_above, (keys, vals))
-    w_sib = swap_core(after(w_out, keys))
+    own = jnp.concatenate([key_proj, val_proj], axis=0)
+    above, loads = to_earlier(own)
+    both = [own] + earlier_shards(above, loads)
+    downs, runs = gather_rows(w_down[0].T, above, both)
+    w_sib = swap_core(after(w_out, above))
 
     flat = routes.reshape(-1)
     order = jnp.arange(flat.shape[0], dtype=jnp.int32)
@@ -394,17 +397,19 @@
         split = rows.reshape(sources, rows.shape[0] // sources, rows.shape[1])
         return lax.all_to_all(split, "exp", split_axis=0, concat_axis=0, tiled=True)
 
-    recv_grad = exchange(scatter_rows(after(grad_out, keys), target_rows, slots)).reshape(slots, width)
-    attn = attention(where, queries, keys, vals)
+    recv_grad = exchange(scatter_rows(after(grad_out, both), target_rows, slots)).reshape(slots, width)
+    attn = attention(where, queries, both)
     owners = attn.reshape(NY, 2, tok_dev, attn.shape[1])
     mine = lax.dynamic_index_in_dim(owners, core, 1, keepdims=False)
     theirs = swap_core(lax.dynamic_index_in_dim(owners, 1 - core, 1, keepdims=False))
     partial = project(y[None].astype(jnp.int32), mine, theirs, w_out, w_sib)
-    parts = [partial[0]] + [along_y(partial[d], d) for d in (1, 2, 3)]
+    sent = after(partial, *downs[-3:])
+    parts = [partial[0]] + [along_y(sent[d], d) for d in (1, 2, 3)]
     hidden, send_in = norm_dispatch(x_resid, parts, gain, target_rows, slots)
     recv_in = exchange(send_in).reshape(slots, width)
-    both = experts(recv_in, *down_part(where, recv_grad, downs, runs), chunk)
-    rows = exchange(both).reshape(sources * BACK, width)
+    back = down_part(where, recv_grad, downs, runs)
+    results = experts(where, recv_in, back, chunk, downs, runs)
+    rows = exchange(results).reshape(sources * BACK, width)
     return combine(hidden, grad_out, rows, returned, gate_prob, gain)
 
 

time: 209 us -> 235 us (1.12)
  waiting for transfers between devices: 81.7 us -> 93.4 us
  local copies, waits for them, and re-layouts: 11.5 us -> 21.3 us
  starting transfers between devices: 60.3 us -> 64.7 us
    ppermute x30 -> x26, waiting for transfers between devices: 55.9 us -> 65.9 us  [shift_zx(): return lax.ppermute(block, 'seq', route)]
    unnamed x48 -> x56, local copies, waits for them, and re-layouts: 8.36 us -> 16.6 us
    ppermute x30 -> x26, starting transfers between devices: 40.1 us -> 43.8 us  [shift_zx(): return lax.ppermute(block, 'seq', route)]
  transfers between devices with their start and end apart: 39 -> 35, of which waited for: 15 -> 12; matrix products, arithmetic and copies ran while one was open for 2% -> 4% of each run, Pallas kernels for 9% -> 7%
where the time goes in v2:
time: 235 us; the launch traced here: 232 us
  waiting for transfers between devices  93.4 us (40%)
  starting transfers between devices  64.7 us (28%)
  Pallas kernels  36.3 us (15%)
  local copies, waits for them, and re-layouts  21.3 us (9%)
  between operations  14.4 us (6%)
    ppermute x26, waiting for transfers between devices, shift_zx(): return lax.ppermute(block, 'seq', route)  65.9 us
    ppermute x26, starting transfers between devices, shift_zx(): return lax.ppermute(block, 'seq', route)  43.8 us
    all_to_all x3, waiting for transfers between devices, exchange(): return lax.all_to_all(split, 'exp', split_axis=0, concat_axis=0, tiled=True)  18.6 us
    pallas_call x1, Pallas kernels, experts(): pl.pallas_call(functools.partial(expert_kernel, runs), out_shape=jax.Shap...  17.4 us
    unnamed x56, local copies, waits for them, and re-layouts  16.6 us
    all_to_all x3, starting transfers between devices, exchange(): return lax.all_to_all(split, 'exp', split_axis=0, concat_axis=0, tiled=True)  14.9 us
    ppermute x3, waiting for transfers between devices, along_y(): lax.ppermute(block, 'exp', [(i, (i + 2 * d) % (2 * NY)) for i in range(2...  8.84 us
    pallas_call x1, Pallas kernels, attention(): pl.pallas_call(attention_kernel, out_shape=jax.ShapeDtypeStruct(q.shape,...  6.61 us
  transfers between devices with their start and end apart: 35, of which 12 were waited for; matrix products, arithmetic and copies ran while one was open for 4% of the time, Pallas kernels for 7%

profile of v2, /device:TPU:2, one launch (start us, length us, event | category | flops | bytes accessed | tf_op | source)
XLA Modules:
  0.0 232.3 jit_solution(9675594624188667735)
XLA Ops:
  7.2 1.8 pad_maximum_fusion.1
  9.1 1.6 fusion.1
  10.7 2.3 collective-permute-start.22
  13.6 1.8 collective-permute-start.20
  15.5 2.0 collective-permute-start
  17.5 1.9 collective-permute-start.6
  19.7 2.2 collective-permute-start.9
  21.9 16.1 %collective-permute-done.6 = bf16[32,1408]{1,0:T(8,128)(2,1)S(1)} collective-permute-done((bf16[32,1408]{1,0:T(8,128)(2,1)S(1)}, bf16[32,1408]{1,0:T(8,128)(2,1)S(1)}, u32[]{:S(2)}, u32[]{:S(2)}) %collective-permute-start.6) | collective-permute-done | bytes 90144 | tf_op jit(solution)/shard_map/ppermute | solution.py:41
  38.8 3.5 %collective-permute-start.10 = (bf16[32,1408]{1,0:T(8,128)(2,1)S(1)}, bf16[32,1408]{1,0:T(8,128)(2,1)S(1)}, u32[]{:S(2)}, u32[]{:S(2)}) collective-permute-start(bf16[32,1408]{1,0:T(8,128)(2,1)S(1)} %collective-permute-done.9), channel_id=1, source_target_pairs={{0,224},{8,232},{16,240},{24,248},{32,0},{40,8},{48,16},{56,24},{6... | collective-permute-start | bytes 270344 | tf_op jit(solution)/shard_map/ppermute | solution.py:41
  42.4 1.5 collective-permute-start.2
  44.0 1.9 collective-permute-start.3
  46.8 3.2 %collective-permute-start.11 = (bf16[32,1408]{1,0:T(8,128)(2,1)S(1)}, bf16[32,1408]{1,0:T(8,128)(2,1)S(1)}, u32[]{:S(2)}, u32[]{:S(2)}) collective-permute-start(bf16[32,1408]{1,0:T(8,128)(2,1)S(1)} %collective-permute-done.10), channel_id=1, source_target_pairs={{0,224},{8,232},{16,240},{24,248},{32,0},{40,8},{48,16},{56,24},{6... | collective-permute-start | bytes 270344 | tf_op jit(solution)/shard_map/ppermute | solution.py:41
  50.6 2.9 %collective-permute-done.8 = bf16[32,1408]{1,0:T(8,128)(2,1)S(1)} collective-permute-done((bf16[32,1408]{1,0:T(8,128)(2,1)S(1)}, bf16[32,1408]{1,0:T(8,128)(2,1)S(1)}, u32[]{:S(2)}, u32[]{:S(2)}) %collective-permute-start.8) | collective-permute-done | bytes 90144 | tf_op jit(solution)/shard_map/ppermute | solution.py:41
  53.5 3.3 %collective-permute-start.13 = (bf16[16,1408]{1,0:T(8,128)(2,1)S(1)}, bf16[16,1408]{1,0:T(8,128)(2,1)S(1)}, u32[]{:S(2)}, u32[]{:S(2)}) collective-permute-start(bf16[16,1408]{1,0:T(8,128)(2,1)S(1)} %slice.43), channel_id=1, source_target_pairs={{0,224},{8,232},{16,240},{24,248},{32,0},{40,8},{48,16},{56,24},{6... | collective-permute-start | bytes 135176 | tf_op jit(solution)/shard_map/ppermute | solution.py:41
  59.4 1.3 collective-permute-start.23
  62.8 2.0 collective-permute-start.24
  66.4 1.3 collective-permute-start.14
  67.7 2.4 %collective-permute-start.15 = (bf16[256,1408]{1,0:T(8,128)(2,1)}, bf16[256,1408]{1,0:T(8,128)(2,1)}, u32[]{:S(2)}, u32[]{:S(2)}) collective-permute-start(bf16[256,1408]{1,0:T(8,128)(2,1)} %constant_dynamic-update-slice_fusion.2.refs_9_), channel_id=1, source_target_pairs={{0,16},{8,24},{16,0},{24,8},{32,48},{40,56},{48,32},{56,40},{64,80... | collective-permute-start | bytes 2162696 | tf_op jit(solution)/shard_map/ppermute | solution.py:41
  70.2 1.4 collective-permute-done.23.refs_1_
  71.6 2.2 collective-permute-start.16
  74.8 1.1 copy-done.6
  75.8 1.0 copy-done.12
  76.9 1.0 copy-done.14
  77.9 1.0 copy-done.16
  79.0 1.0 copy-done.17
  79.9 6.6 %shard_map.139 = bf16[512,256]{1,0:T(8,128)(2,1)S(1)} custom-call(s32[3]{0:T(128)S(1)} %pad_add_fusion.where, bf16[512,256]{1,0:T(8,128)(2,1)S(1)} %copy-done.17, bf16[1024,256]{1,0:T(8,128)(2,1)S(1)} %constant_dynamic-update-slice_fusion.refs_0_, bf16[1024,256]{1,0:T(8,128)(2,1)S(1)} %copy-done.12, bf16[1024,256]{1,0:T(8,128)(2,1)S(1)} %copy-done.14, ...), custom_call_target="tpu_custom_call" | custom-call | flops 1342177280 | bytes 6291456 | tf_op jit(solution)/shard_map/pallas_call | solution.py:122
  87.3 1.2 shard_map.142
  88.5 5.3 %all-to-all-start.1 = ((bf16[8,24,2048]{2,1,0:T(8,128)(2,1)}), bf16[8,24,2048]{2,1,0:T(8,128)(2,1)S(1)}, u32[]{:S(2)}, u32[]{:S(2)}) async-start(bf16[8,24,2048]{2,1,0:T(8,128)(2,1)} %bitcast.16), calls=%async_computation.1 | async-start | bytes 1572864 | tf_op jit(solution)/shard_map/all_to_all | solution.py:398
  94.0 3.2 %collective-permute-start.26 = (bf16[128,1408]{1,0:T(8,128)(2,1)}, bf16[128,1408]{1,0:T(8,128)(2,1)}, u32[]{:S(2)}, u32[]{:S(2)}) collective-permute-start(bf16[128,1408]{1,0:T(8,128)(2,1)} %collective-permute-done.24.refs_2_), channel_id=1, source_target_pairs={{0,224},{8,232},{16,240},{24,248},{32,0},{40,8},{48,16},{56,24},{6... | collective-permute-start | bytes 1081352 | tf_op jit(solution)/shard_map/ppermute | solution.py:41
  98.1 2.5 %shard_map.140 = bf16[4,64,2048]{2,1,0:T(8,128)(2,1)S(1)} custom-call(s32[1]{0:T(128)} %bitcast.where, bf16[4,64,256]{2,1,0:T(8,128)(2,1)S(1)} %copy-done.4, bf16[4,64,256]{2,1,0:T(8,128)(2,1)} %collective-permute-done.4.sib, bf16[256,2048]{1,0:T(8,128)(2,1)S(1)} %copy-done.1, bf16[256,2048]{1,0:T(8,128)(2,1)S(1)} %collective-permute-done.5.w_sib), custom_call_target="tpu_custom_call" | custom-call | flops 536870912 | bytes 6291456 | tf_op jit(solution)/shard_map/pallas_call | solution.py:171
  100.8 3.1 %collective-permute-done.15.refs_11_ = bf16[256,1408]{1,0:T(8,128)(2,1)} collective-permute-done((bf16[256,1408]{1,0:T(8,128)(2,1)}, bf16[256,1408]{1,0:T(8,128)(2,1)}, u32[]{:S(2)}, u32[]{:S(2)}) %collective-permute-start.15) | collective-permute-done | bytes 720928 | tf_op jit(solution)/shard_map/ppermute | solution.py:41
  104.0 28.7 %collective-permute-done.16.refs_12_ = bf16[256,1408]{1,0:T(8,128)(2,1)} collective-permute-done((bf16[256,1408]{1,0:T(8,128)(2,1)}, bf16[256,1408]{1,0:T(8,128)(2,1)}, u32[]{:S(2)}, u32[]{:S(2)}) %collective-permute-start.16) | collective-permute-done | bytes 720928 | tf_op jit(solution)/shard_map/ppermute | solution.py:41
  132.7 1.8 collective-permute-start.17
  134.5 2.8 %collective-permute-start.18 = (bf16[64,2048]{1,0:T(8,128)(2,1)S(1)}, bf16[64,2048]{1,0:T(8,128)(2,1)S(1)}, u32[]{:S(2)}, u32[]{:S(2)}) collective-permute-start(bf16[64,2048]{1,0:T(8,128)(2,1)S(1)} %get-tuple-element.34), channel_id=1, source_target_pairs={{0,4},{1,5},{2,6},{3,7},{4,0},{5,1},{6,2},{7,3},{8,12},{9,13},{10,... | collective-permute-start | bytes 786440 | tf_op jit(solution)/shard_map/ppermute | solution.py:53
  137.4 1.3 collective-permute-start.19
  138.7 3.5 %collective-permute-done.17.p1 = bf16[64,2048]{1,0:T(8,128)(2,1)S(1)} collective-permute-done((bf16[64,2048]{1,0:T(8,128)(2,1)S(1)}, bf16[64,2048]{1,0:T(8,128)(2,1)S(1)}, u32[]{:S(2)}, u32[]{:S(2)}) %collective-permute-start.17) | collective-permute-done | bytes 262176 | tf_op jit(solution)/shard_map/ppermute | solution.py:53
  142.2 5.3 %collective-permute-done.18.p2 = bf16[64,2048]{1,0:T(8,128)(2,1)S(1)} collective-permute-done((bf16[64,2048]{1,0:T(8,128)(2,1)S(1)}, bf16[64,2048]{1,0:T(8,128)(2,1)S(1)}, u32[]{:S(2)}, u32[]{:S(2)}) %collective-permute-start.18) | collective-permute-done | bytes 262176 | tf_op jit(solution)/shard_map/ppermute | solution.py:53
  149.1 3.6 %all-to-all-start = ((bf16[8,24,2048]{2,1,0:T(8,128)(2,1)}), bf16[8,24,2048]{2,1,0:T(8,128)(2,1)S(1)}, u32[]{:S(2)}, u32[]{:S(2)}) async-start(bf16[8,24,2048]{2,1,0:T(8,128)(2,1)} %bitcast.38), calls=%async_computation | async-start | bytes 1572864 | tf_op jit(solution)/shard_map/all_to_all | solution.py:398
  153.0 3.2 %collective-permute-start.28 = (bf16[128,1408]{1,0:T(8,128)(2,1)}, bf16[128,1408]{1,0:T(8,128)(2,1)S(1)}, u32[]{:S(2)}, u32[]{:S(2)}) collective-permute-start(bf16[128,1408]{1,0:T(8,128)(2,1)} %collective-permute-done.26.refs_4_), channel_id=1, source_target_pairs={{0,224},{8,232},{16,240},{24,248},{32,0},{40,8},{48,16},{56,24},{6... | collective-permute-start | bytes 1081352 | tf_op jit(solution)/shard_map/ppermute | solution.py:41
  156.2 8.7 %collective-permute-done.27.refs_5_ = bf16[128,1408]{1,0:T(8,128)(2,1)S(1)} collective-permute-done((bf16[128,1408]{1,0:T(8,128)(2,1)}, bf16[128,1408]{1,0:T(8,128)(2,1)S(1)}, u32[]{:S(2)}, u32[]{:S(2)}) %collective-permute-start.27) | collective-permute-done | bytes 360480 | tf_op jit(solution)/shard_map/ppermute | solution.py:41
  165.6 2.8 %collective-permute-start.30 = (bf16[64,1408]{1,0:T(8,128)(2,1)S(1)}, bf16[64,1408]{1,0:T(8,128)(2,1)S(1)}, u32[]{:S(2)}, u32[]{:S(2)}) collective-permute-start(bf16[64,1408]{1,0:T(8,128)(2,1)S(1)} %slice.46), channel_id=1, source_target_pairs={{0,224},{8,232},{16,240},{24,248},{32,0},{40,8},{48,16},{56,24},{6... | collective-permute-start | bytes 540680 | tf_op jit(solution)/shard_map/ppermute | solution.py:41
  168.4 3.7 %collective-permute-done.29.refs_7_ = bf16[64,1408]{1,0:T(8,128)(2,1)S(1)} collective-permute-done((bf16[64,1408]{1,0:T(8,128)(2,1)S(1)}, bf16[64,1408]{1,0:T(8,128)(2,1)S(1)}, u32[]{:S(2)}, u32[]{:S(2)}) %collective-permute-start.29) | collective-permute-done | bytes 180256 | tf_op jit(solution)/shard_map/ppermute | solution.py:41
  172.1 5.8 %shard_map.143.ba = f32[192,1408]{1,0:T(8,128)S(1)} custom-call(s32[3]{0:T(128)S(1)} %pad_add_fusion.where, bf16[192,2048]{1,0:T(8,128)(2,1)S(1)} %bitcast.36, bf16[128,1408]{1,0:T(8,128)(2,1)S(1)} %pad_maximum_fusion.refs_0_, bf16[128,1408]{1,0:T(8,128)(2,1)} %collective-permute-done.23.refs_1_, bf16[128,1408]{1,0:T(8,128)(2,1)} %collective-permute-done.24.refs_2_, ...), custom_call_target="tpu_custom_call" | custom-call | flops 1107296256 | bytes 7340032 | tf_op jit(solution)/shard_map/pallas_call | solution.py:253
  178.0 1.0 copy-done
  180.5 17.4 %shard_map.144 = bf16[320,2048]{1,0:T(8,128)(2,1)} custom-call(s32[3]{0:T(128)S(1)} %pad_add_fusion.where, bf16[192,2048]{1,0:T(8,128)(2,1)S(1)} %bitcast.37, f32[192,1408]{1,0:T(8,128)} %copy-done, bf16[32,128,1408]{2,1,0:T(8,128)(2,1)} %bitcast.46, bf16[128,1408]{1,0:T(8,128)(2,1)S(1)} %pad_maximum_fusion.refs_0_, ...), custom_call_target="tpu_custom_call" | custom-call | flops 5536481280 | bytes 14680064 | tf_op jit(solution)/shard_map/pallas_call | solution.py:320
  198.0 5.9 %all-to-all-start.2 = ((bf16[8,40,2048]{2,1,0:T(8,128)(2,1)}), bf16[8,40,2048]{2,1,0:T(8,128)(2,1)S(1)}, u32[]{:S(2)}, u32[]{:S(2)}) async-start(bf16[8,40,2048]{2,1,0:T(8,128)(2,1)} %bitcast.42), calls=%async_computation.2 | async-start | bytes 2621440 | tf_op jit(solution)/shard_map/all_to_all | solution.py:398
  204.1 18.6 %all-to-all-done.2 = bf16[8,40,2048]{2,1,0:T(8,128)(2,1)S(1)} async-done(((bf16[8,40,2048]{2,1,0:T(8,128)(2,1)}), bf16[8,40,2048]{2,1,0:T(8,128)(2,1)S(1)}, u32[]{:S(2)}, u32[]{:S(2)}) %all-to-all-start.2) | async-done | bytes 1310752 | tf_op jit(solution)/shard_map/all_to_all | solution.py:398
  222.7 2.1 shard_map.145
  (108 shorter events, 17.6 us)
Async XLA Ops:
  7.2 8.3 %copy-start.18 = (bf16[512,256]{1,0:T(8,128)(2,1)S(1)}, bf16[512,256]{1,0:T(8,128)(2,1)}, u32[]{:S(2)}) copy-start(bf16[512,256]{1,0:T(8,128)(2,1)} %param.14) | copy-start | bytes 786436
  7.2 8.3 %copy-start.19 = (bf16[512,256]{1,0:T(8,128)(2,1)S(1)}, bf16[512,256]{1,0:T(8,128)(2,1)}, u32[]{:S(2)}) copy-start(bf16[512,256]{1,0:T(8,128)(2,1)} %param.15) | copy-start | bytes 786436
  7.2 172.4 %all-gather.3.cloned.1.call-start = ((), (), s32[]{:S(2)}) async-start(), calls=%async_computation.3 | async-start | bytes 11894784 | tf_op jit(solution)/shard_map/all_gather | solution.py:379
  7.2 12.2 %copy-start.20 = (s32[64,2]{0,1:T(2,128)S(1)}, s32[64,2]{0,1:T(2,128)}, u32[]{:S(2)}) copy-start(s32[64,2]{0,1:T(2,128)} %param.21) | copy-start | bytes 1540
  10.7 9.0 %collective-permute-start.22 = (bf16[32,1408]{1,0:T(8,128)(2,1)S(1)}, bf16[32,1408]{1,0:T(8,128)(2,1)S(1)}, u32[]{:S(2)}, u32[]{:S(2)}) collective-permute-start(bf16[32,1408]{1,0:T(8,128)(2,1)S(1)} %get-tuple-element.41), channel_id=1, source_target_pairs={{0,24},{8,0},{16,8},{24,16},{32,56},{40,32},{48,40},{56,48},{64,88... | collective-permute-start | bytes 270344 | tf_op jit(solution)/shard_map/ppermute | solution.py:41
  13.0 8.9 %collective-permute-start.21 = (bf16[32,1408]{1,0:T(8,128)(2,1)S(1)}, bf16[32,1408]{1,0:T(8,128)(2,1)S(1)}, u32[]{:S(2)}, u32[]{:S(2)}) collective-permute-start(bf16[32,1408]{1,0:T(8,128)(2,1)S(1)} %get-tuple-element.41), channel_id=1, source_target_pairs={{0,16},{8,24},{16,0},{24,8},{32,48},{40,56},{48,32},{56,40},{64,80... | collective-permute-start | bytes 270344 | tf_op jit(solution)/shard_map/ppermute | solution.py:41
  13.6 8.3 %collective-permute-start.20 = (bf16[32,1408]{1,0:T(8,128)(2,1)S(1)}, bf16[32,1408]{1,0:T(8,128)(2,1)S(1)}, u32[]{:S(2)}, u32[]{:S(2)}) collective-permute-start(bf16[32,1408]{1,0:T(8,128)(2,1)S(1)} %get-tuple-element.41), channel_id=1, source_target_pairs={{0,8},{8,16},{16,24},{24,0},{32,40},{40,48},{48,56},{56,32},{64,72... | collective-permute-start | bytes 270344 | tf_op jit(solution)/shard_map/ppermute | solution.py:41
  15.5 23.2 %collective-permute-start = (bf16[1024,256]{1,0:T(8,128)(2,1)S(1)}, bf16[1024,256]{1,0:T(8,128)(2,1)S(1)}, u32[]{:S(2)}, u32[]{:S(2)}) collective-permute-start(bf16[1024,256]{1,0:T(8,128)(2,1)S(1)} %constant_dynamic-update-slice_fusion.refs_0_), channel_id=1, source_target_pairs={{0,32},{8,40},{16,48},{24,56},{32,64},{40,72},{48,80},{56,88},{64,... | collective-permute-start | bytes 1572872 | tf_op jit(solution)/shard_map/ppermute | solution.py:41
  17.5 20.6 %collective-permute-start.6 = (bf16[32,1408]{1,0:T(8,128)(2,1)S(1)}, bf16[32,1408]{1,0:T(8,128)(2,1)S(1)}, u32[]{:S(2)}, u32[]{:S(2)}) collective-permute-start(bf16[32,1408]{1,0:T(8,128)(2,1)S(1)} %get-tuple-element.43), channel_id=1, source_target_pairs={{0,32},{8,40},{16,48},{24,56},{32,64},{40,72},{48,80},{56,88},{64,... | collective-permute-start | bytes 270344 | tf_op jit(solution)/shard_map/ppermute | solution.py:41
  19.7 19.1 %collective-permute-start.9 = (bf16[32,1408]{1,0:T(8,128)(2,1)S(1)}, bf16[32,1408]{1,0:T(8,128)(2,1)S(1)}, u32[]{:S(2)}, u32[]{:S(2)}) collective-permute-start(bf16[32,1408]{1,0:T(8,128)(2,1)S(1)} %get-tuple-element.43), channel_id=1, source_target_pairs={{0,224},{8,232},{16,240},{24,248},{32,0},{40,8},{48,16},{56,24},{6... | collective-permute-start | bytes 270344 | tf_op jit(solution)/shard_map/ppermute | solution.py:41
  38.7 20.7 %copy-start.1 = (bf16[256,2048]{1,0:T(8,128)(2,1)S(1)}, bf16[256,2048]{1,0:T(8,128)(2,1)}, u32[]{:S(2)}) copy-start(bf16[256,2048]{1,0:T(8,128)(2,1)} %w_own.1) | copy-start | bytes 3145732
  38.7 3.6 %copy-start.5 = (bf16[1024,256]{1,0:T(8,128)(2,1)}, bf16[1024,256]{1,0:T(8,128)(2,1)S(1)}, u32[]{:S(2)}) copy-start(bf16[1024,256]{1,0:T(8,128)(2,1)S(1)} %collective-permute-done.refs_4_) | copy-start | bytes 1572868
  38.7 8.0 %collective-permute-start.7 = (bf16[32,1408]{1,0:T(8,128)(2,1)S(1)}, bf16[32,1408]{1,0:T(8,128)(2,1)S(1)}, u32[]{:S(2)}, u32[]{:S(2)}) collective-permute-start(bf16[32,1408]{1,0:T(8,128)(2,1)S(1)} %collective-permute-done.6), channel_id=1, source_target_pairs={{0,32},{8,40},{16,48},{24,56},{32,64},{40,72},{48,80},{56,88},{64,... | collective-permute-start | bytes 270344 | tf_op jit(solution)/shard_map/ppermute | solution.py:41
  38.8 8.0 %collective-permute-start.10 = (bf16[32,1408]{1,0:T(8,128)(2,1)S(1)}, bf16[32,1408]{1,0:T(8,128)(2,1)S(1)}, u32[]{:S(2)}, u32[]{:S(2)}) collective-permute-start(bf16[32,1408]{1,0:T(8,128)(2,1)S(1)} %collective-permute-done.9), channel_id=1, source_target_pairs={{0,224},{8,232},{16,240},{24,248},{32,0},{40,8},{48,16},{56,24},{6... | collective-permute-start | bytes 270344 | tf_op jit(solution)/shard_map/ppermute | solution.py:41
  42.4 19.6 %collective-permute-start.1 = (bf16[1024,256]{1,0:T(8,128)(2,1)S(1)}, bf16[1024,256]{1,0:T(8,128)(2,1)S(1)}, u32[]{:S(2)}, u32[]{:S(2)}) collective-permute-start(bf16[1024,256]{1,0:T(8,128)(2,1)S(1)} %get-tuple-element.38), channel_id=1, source_target_pairs={{0,8},{8,16},{16,24},{24,0},{32,40},{40,48},{48,56},{56,32},{64,72... | collective-permute-start | bytes 1572872 | tf_op jit(solution)/shard_map/ppermute | solution.py:41
  42.4 22.4 %collective-permute-start.2 = (bf16[1024,256]{1,0:T(8,128)(2,1)S(1)}, bf16[1024,256]{1,0:T(8,128)(2,1)S(1)}, u32[]{:S(2)}, u32[]{:S(2)}) collective-permute-start(bf16[1024,256]{1,0:T(8,128)(2,1)S(1)} %get-tuple-element.37), channel_id=1, source_target_pairs={{0,16},{8,24},{16,0},{24,8},{32,48},{40,56},{48,32},{56,40},{64,80... | collective-permute-start | bytes 1572872 | tf_op jit(solution)/shard_map/ppermute | solution.py:41
  44.0 21.7 %collective-permute-start.3 = (bf16[1024,256]{1,0:T(8,128)(2,1)S(1)}, bf16[1024,256]{1,0:T(8,128)(2,1)S(1)}, u32[]{:S(2)}, u32[]{:S(2)}) collective-permute-start(bf16[1024,256]{1,0:T(8,128)(2,1)S(1)} %get-tuple-element.36), channel_id=1, source_target_pairs={{0,24},{8,0},{16,8},{24,16},{32,56},{40,32},{48,40},{56,48},{64,88... | collective-permute-start | bytes 1572872 | tf_op jit(solution)/shard_map/ppermute | solution.py:41
  46.8 6.7 %collective-permute-start.8 = (bf16[32,1408]{1,0:T(8,128)(2,1)S(1)}, bf16[32,1408]{1,0:T(8,128)(2,1)S(1)}, u32[]{:S(2)}, u32[]{:S(2)}) collective-permute-start(bf16[32,1408]{1,0:T(8,128)(2,1)S(1)} %collective-permute-done.7), channel_id=1, source_target_pairs={{0,32},{8,40},{16,48},{24,56},{32,64},{40,72},{48,80},{56,88},{64,... | collective-permute-start | bytes 270344 | tf_op jit(solution)/shard_map/ppermute | solution.py:41
  46.8 6.8 %collective-permute-start.11 = (bf16[32,1408]{1,0:T(8,128)(2,1)S(1)}, bf16[32,1408]{1,0:T(8,128)(2,1)S(1)}, u32[]{:S(2)}, u32[]{:S(2)}) collective-permute-start(bf16[32,1408]{1,0:T(8,128)(2,1)S(1)} %collective-permute-done.10), channel_id=1, source_target_pairs={{0,224},{8,232},{16,240},{24,248},{32,0},{40,8},{48,16},{56,24},{6... | collective-permute-start | bytes 270344 | tf_op jit(solution)/shard_map/ppermute | solution.py:41
  53.5 5.9 %collective-permute-start.12 = (bf16[16,1408]{1,0:T(8,128)(2,1)S(1)}, bf16[16,1408]{1,0:T(8,128)(2,1)S(1)}, u32[]{:S(2)}, u32[]{:S(2)}) collective-permute-start(bf16[16,1408]{1,0:T(8,128)(2,1)S(1)} %slice.42), channel_id=1, source_target_pairs={{0,32},{8,40},{16,48},{24,56},{32,64},{40,72},{48,80},{56,88},{64,... | collective-permute-start | bytes 135176 | tf_op jit(solution)/shard_map/ppermute | solution.py:41
  53.5 5.9 %collective-permute-start.13 = (bf16[16,1408]{1,0:T(8,128)(2,1)S(1)}, bf16[16,1408]{1,0:T(8,128)(2,1)S(1)}, u32[]{:S(2)}, u32[]{:S(2)}) collective-permute-start(bf16[16,1408]{1,0:T(8,128)(2,1)S(1)} %slice.43), channel_id=1, source_target_pairs={{0,224},{8,232},{16,240},{24,248},{32,0},{40,8},{48,16},{56,24},{6... | collective-permute-start | bytes 135176 | tf_op jit(solution)/shard_map/ppermute | solution.py:41
  59.4 34.6 %collective-permute-start.5 = (bf16[256,2048]{1,0:T(8,128)(2,1)S(1)}, bf16[256,2048]{1,0:T(8,128)(2,1)S(1)}, u32[]{:S(2)}, u32[]{:S(2)}) collective-permute-start(bf16[256,2048]{1,0:T(8,128)(2,1)S(1)} %copy-done.1), channel_id=1, source_target_pairs={{0,1},{1,0},{2,3},{3,2},{4,5},{5,4},{6,7},{7,6},{8,9},{9,8},{10,11... | collective-permute-start | bytes 3145736 | tf_op jit(solution)/shard_map/ppermute | solution.py:57
  59.4 12.1 %collective-permute-start.23 = (bf16[128,1408]{1,0:T(8,128)(2,1)S(1)}, bf16[128,1408]{1,0:T(8,128)(2,1)}, u32[]{:S(2)}, u32[]{:S(2)}) collective-permute-start(bf16[128,1408]{1,0:T(8,128)(2,1)S(1)} %pad_maximum_fusion.refs_0_), channel_id=1, source_target_pairs={{0,32},{8,40},{16,48},{24,56},{32,64},{40,72},{48,80},{56,88},{64,... | collective-permute-start | bytes 1081352 | tf_op jit(solution)/shard_map/ppermute | solution.py:41
  62.8 24.5 %collective-permute-start.24 = (bf16[128,1408]{1,0:T(8,128)(2,1)S(1)}, bf16[128,1408]{1,0:T(8,128)(2,1)}, u32[]{:S(2)}, u32[]{:S(2)}) collective-permute-start(bf16[128,1408]{1,0:T(8,128)(2,1)S(1)} %pad_maximum_fusion.refs_0_), channel_id=1, source_target_pairs={{0,224},{8,232},{16,240},{24,248},{32,0},{40,8},{48,16},{56,24},{6... | collective-permute-start | bytes 1081352 | tf_op jit(solution)/shard_map/ppermute | solution.py:41
  66.4 34.4 %collective-permute-start.14 = (bf16[256,1408]{1,0:T(8,128)(2,1)}, bf16[256,1408]{1,0:T(8,128)(2,1)}, u32[]{:S(2)}, u32[]{:S(2)}) collective-permute-start(bf16[256,1408]{1,0:T(8,128)(2,1)} %constant_dynamic-update-slice_fusion.2.refs_9_), channel_id=1, source_target_pairs={{0,8},{8,16},{16,24},{24,0},{32,40},{40,48},{48,56},{56,32},{64,72... | collective-permute-start | bytes 2162696 | tf_op jit(solution)/shard_map/ppermute | solution.py:41
  67.7 36.2 %collective-permute-start.15 = (bf16[256,1408]{1,0:T(8,128)(2,1)}, bf16[256,1408]{1,0:T(8,128)(2,1)}, u32[]{:S(2)}, u32[]{:S(2)}) collective-permute-start(bf16[256,1408]{1,0:T(8,128)(2,1)} %constant_dynamic-update-slice_fusion.2.refs_9_), channel_id=1, source_target_pairs={{0,16},{8,24},{16,0},{24,8},{32,48},{40,56},{48,32},{56,40},{64,80... | collective-permute-start | bytes 2162696 | tf_op jit(solution)/shard_map/ppermute | solution.py:41
  71.6 61.1 %collective-permute-start.16 = (bf16[256,1408]{1,0:T(8,128)(2,1)}, bf16[256,1408]{1,0:T(8,128)(2,1)}, u32[]{:S(2)}, u32[]{:S(2)}) collective-permute-start(bf16[256,1408]{1,0:T(8,128)(2,1)} %constant_dynamic-update-slice_fusion.2.refs_9_), channel_id=1, source_target_pairs={{0,24},{8,0},{16,8},{24,16},{32,56},{40,32},{48,40},{56,48},{64,88... | collective-permute-start | bytes 2162696 | tf_op jit(solution)/shard_map/ppermute | solution.py:41
  74.8 1.1 copy-start.6
  76.9 1.0 copy-start.14
  77.9 1.0 copy-start.16
  79.9 7.4 %copy-start.21 = (s32[64,2]{0,1:T(2,128)S(1)}, s32[64,2]{0,1:T(2,128)}, u32[]{:S(2)}) copy-start(s32[64,2]{0,1:T(2,128)} %copy.42) | copy-start | bytes 1540
  79.9 7.4 %copy-start.2 = (bf16[64,2048]{1,0:T(8,128)(2,1)S(1)}, bf16[64,2048]{1,0:T(8,128)(2,1)}, u32[]{:S(2)}) copy-start(bf16[64,2048]{1,0:T(8,128)(2,1)} %grad_out.1) | copy-start | bytes 786436
  87.3 6.6 %collective-permute-start.4 = (bf16[4,64,256]{2,1,0:T(8,128)(2,1)}, bf16[4,64,256]{2,1,0:T(8,128)(2,1)}, u32[]{:S(2)}, u32[]{:S(2)}) collective-permute-start(bf16[4,64,256]{2,1,0:T(8,128)(2,1)} %get-tuple-element.39), channel_id=1, source_target_pairs={{0,1},{1,0},{2,3},{3,2},{4,5},{5,4},{6,7},{7,6},{8,9},{9,8},{10,11... | collective-permute-start | bytes 393224 | tf_op jit(solution)/shard_map/ppermute | solution.py:57
  88.5 59.7 %all-to-all-start.1 = ((bf16[8,24,2048]{2,1,0:T(8,128)(2,1)}), bf16[8,24,2048]{2,1,0:T(8,128)(2,1)S(1)}, u32[]{:S(2)}, u32[]{:S(2)}) async-start(bf16[8,24,2048]{2,1,0:T(8,128)(2,1)} %bitcast.16), calls=%async_computation.1 | async-start | bytes 1572864 | tf_op jit(solution)/shard_map/all_to_all | solution.py:398
  93.9 58.8 %collective-permute-start.25 = (bf16[128,1408]{1,0:T(8,128)(2,1)}, bf16[128,1408]{1,0:T(8,128)(2,1)}, u32[]{:S(2)}, u32[]{:S(2)}) collective-permute-start(bf16[128,1408]{1,0:T(8,128)(2,1)} %collective-permute-done.23.refs_1_), channel_id=1, source_target_pairs={{0,32},{8,40},{16,48},{24,56},{32,64},{40,72},{48,80},{56,88},{64,... | collective-permute-start | bytes 1081352 | tf_op jit(solution)/shard_map/ppermute | solution.py:41
  94.0 59.0 %collective-permute-start.26 = (bf16[128,1408]{1,0:T(8,128)(2,1)}, bf16[128,1408]{1,0:T(8,128)(2,1)}, u32[]{:S(2)}, u32[]{:S(2)}) collective-permute-start(bf16[128,1408]{1,0:T(8,128)(2,1)} %collective-permute-done.24.refs_2_), channel_id=1, source_target_pairs={{0,224},{8,232},{16,240},{24,248},{32,0},{40,8},{48,16},{56,24},{6... | collective-permute-start | bytes 1081352 | tf_op jit(solution)/shard_map/ppermute | solution.py:41
  100.6 47.0 %copy-start.7 = (bf16[64,2048]{1,0:T(8,128)(2,1)S(1)}, bf16[64,2048]{1,0:T(8,128)(2,1)}, u32[]{:S(2)}) copy-start(bf16[64,2048]{1,0:T(8,128)(2,1)} %x.1) | copy-start | bytes 786436
  100.6 47.0 %copy-start.10 = (f32[2048]{0:T(1024)S(1)}, f32[2048]{0:T(1024)}, u32[]{:S(2)}) copy-start(f32[2048]{0:T(1024)} %param.17) | copy-start | bytes 24580
  132.7 9.5 %collective-permute-start.17 = (bf16[64,2048]{1,0:T(8,128)(2,1)S(1)}, bf16[64,2048]{1,0:T(8,128)(2,1)S(1)}, u32[]{:S(2)}, u32[]{:S(2)}) collective-permute-start(bf16[64,2048]{1,0:T(8,128)(2,1)S(1)} %get-tuple-element.35), channel_id=1, source_target_pairs={{0,2},{1,3},{2,4},{3,5},{4,6},{5,7},{6,0},{7,1},{8,10},{9,11},{10,... | collective-permute-start | bytes 786440 | tf_op jit(solution)/shard_map/ppermute | solution.py:53
  134.5 13.0 %collective-permute-start.18 = (bf16[64,2048]{1,0:T(8,128)(2,1)S(1)}, bf16[64,2048]{1,0:T(8,128)(2,1)S(1)}, u32[]{:S(2)}, u32[]{:S(2)}) collective-permute-start(bf16[64,2048]{1,0:T(8,128)(2,1)S(1)} %get-tuple-element.34), channel_id=1, source_target_pairs={{0,4},{1,5},{2,6},{3,7},{4,0},{5,1},{6,2},{7,3},{8,12},{9,13},{10,... | collective-permute-start | bytes 786440 | tf_op jit(solution)/shard_map/ppermute | solution.py:53
  137.4 10.2 %collective-permute-start.19 = (bf16[64,2048]{1,0:T(8,128)(2,1)S(1)}, bf16[64,2048]{1,0:T(8,128)(2,1)S(1)}, u32[]{:S(2)}, u32[]{:S(2)}) collective-permute-start(bf16[64,2048]{1,0:T(8,128)(2,1)S(1)} %get-tuple-element.33), channel_id=1, source_target_pairs={{0,6},{1,7},{2,0},{3,1},{4,2},{5,3},{6,4},{7,5},{8,14},{9,15},{10,... | collective-permute-start | bytes 786440 | tf_op jit(solution)/shard_map/ppermute | solution.py:53
  149.1 30.6 %all-to-all-start = ((bf16[8,24,2048]{2,1,0:T(8,128)(2,1)}), bf16[8,24,2048]{2,1,0:T(8,128)(2,1)S(1)}, u32[]{:S(2)}, u32[]{:S(2)}) async-start(bf16[8,24,2048]{2,1,0:T(8,128)(2,1)} %bitcast.38), calls=%async_computation | async-start | bytes 1572864 | tf_op jit(solution)/shard_map/all_to_all | solution.py:398
  152.7 12.3 %collective-permute-start.27 = (bf16[128,1408]{1,0:T(8,128)(2,1)}, bf16[128,1408]{1,0:T(8,128)(2,1)S(1)}, u32[]{:S(2)}, u32[]{:S(2)}) collective-permute-start(bf16[128,1408]{1,0:T(8,128)(2,1)} %collective-permute-done.25.refs_3_), channel_id=1, source_target_pairs={{0,32},{8,40},{16,48},{24,56},{32,64},{40,72},{48,80},{56,88},{64,... | collective-permute-start | bytes 1081352 | tf_op jit(solution)/shard_map/ppermute | solution.py:41
  153.0 12.5 %collective-permute-start.28 = (bf16[128,1408]{1,0:T(8,128)(2,1)}, bf16[128,1408]{1,0:T(8,128)(2,1)S(1)}, u32[]{:S(2)}, u32[]{:S(2)}) collective-permute-start(bf16[128,1408]{1,0:T(8,128)(2,1)} %collective-permute-done.26.refs_4_), channel_id=1, source_target_pairs={{0,224},{8,232},{16,240},{24,248},{32,0},{40,8},{48,16},{56,24},{6... | collective-permute-start | bytes 1081352 | tf_op jit(solution)/shard_map/ppermute | solution.py:41
  165.0 7.2 %collective-permute-start.29 = (bf16[64,1408]{1,0:T(8,128)(2,1)S(1)}, bf16[64,1408]{1,0:T(8,128)(2,1)S(1)}, u32[]{:S(2)}, u32[]{:S(2)}) collective-permute-start(bf16[64,1408]{1,0:T(8,128)(2,1)S(1)} %slice.45), channel_id=1, source_target_pairs={{0,32},{8,40},{16,48},{24,56},{32,64},{40,72},{48,80},{56,88},{64,... | collective-permute-start | bytes 540680 | tf_op jit(solution)/shard_map/ppermute | solution.py:41
  165.6 6.6 %collective-permute-start.30 = (bf16[64,1408]{1,0:T(8,128)(2,1)S(1)}, bf16[64,1408]{1,0:T(8,128)(2,1)S(1)}, u32[]{:S(2)}, u32[]{:S(2)}) collective-permute-start(bf16[64,1408]{1,0:T(8,128)(2,1)S(1)} %slice.46), channel_id=1, source_target_pairs={{0,224},{8,232},{16,240},{24,248},{32,0},{40,8},{48,16},{56,24},{6... | collective-permute-start | bytes 540680 | tf_op jit(solution)/shard_map/ppermute | solution.py:41
  198.0 6.1 %copy-start.22 = (f32[64,2]{0,1:T(2,128)S(1)}, f32[64,2]{0,1:T(2,128)}, u32[]{:S(2)}) copy-start(f32[64,2]{0,1:T(2,128)} %param.22) | copy-start | bytes 1540
  198.0 24.7 %all-to-all-start.2 = ((bf16[8,40,2048]{2,1,0:T(8,128)(2,1)}), bf16[8,40,2048]{2,1,0:T(8,128)(2,1)S(1)}, u32[]{:S(2)}, u32[]{:S(2)}) async-start(bf16[8,40,2048]{2,1,0:T(8,128)(2,1)} %bitcast.42), calls=%async_computation.2 | async-start | bytes 2621440 | tf_op jit(solution)/shard_map/all_to_all | solution.py:398
  (10 other events, 8.8 us)
Sparse Core Ops, SparseCore 0:
  10.6 147.4 all-gather.2

commit v3 on v1

--- a/solution.py
+++ b/solution.py
@@ -226,9 +226,7 @@
     )(rows, target_rows)
 
 
-def down_kernel(runs, where, rows_grad, *refs):
-    pieces, (wd, back, sem) = refs[: len(runs)], refs[len(runs) :]
-    seq = where[0]
+def fetch_rows(runs, seq, pieces, wd, sem):
     z, x = seq // NX, lax.rem(seq, NX)
     part = wd.shape[0] // (NZ * NX)
     for piece, listed in zip(pieces, runs):
@@ -236,29 +234,10 @@
             source = lax.rem(z + NZ - dz, NZ) * NX + lax.rem(x + NX - dx, NX)
             row = pl.multiple_of(source * part + offset, count)
             pltpu.make_async_copy(piece.at[pl.ds(first, count)], wd.at[pl.ds(row, count)], sem).start()
-    pltpu.make_async_copy(wd, wd, sem).wait()
-    span = 256
-    for k in range(wd.shape[0] // span):
-        cols = pl.ds(k * span, span)
-        term = nn(rows_grad[:, cols], wd[cols, :])
-        back[...] = term if k == 0 else back[...] + term
-
-
-def down_part(where, rows_grad, pieces, runs):
-    rows, width = rows_grad.shape
-    hidden = pieces[0].shape[1]
-    return pl.pallas_call(
-        functools.partial(down_kernel, runs),
-        out_shape=(jax.ShapeDtypeStruct((width, hidden), BF16), jax.ShapeDtypeStruct((rows, hidden), F32)),
-        in_specs=[SMEM, VMEM] + [HBM] * len(pieces),
-        out_specs=(VMEM, VMEM),
-        scratch_shapes=[pltpu.SemaphoreType.DMA(())],
-        compiler_params=params(16),
-        cost_estimate=pl.CostEstimate(flops=2 * rows * width * hidden, bytes_accessed=7 * 2**20, transcendentals=0),
-    )(where, rows_grad, *pieces)
-
-
-def expert_kernel(rows_in, down, ba, chunk, both, wg, wu, wd, ga, ua, hid, gpg, gpu, sems, down_sem):
+
+
+def expert_kernel(runs, where, rows_in, rows_grad, chunk, *refs):
+    pieces, (both, wg, wu, wd, ga, ua, ba, hid, gpg, gpu, sems, down_sem) = refs[: len(runs)], refs[len(runs) :]
     shards = chunk.shape[0]
     part = chunk.shape[1] // 2
     mats = (wg, wu)
@@ -275,8 +254,7 @@
         return 0
 
     lax.fori_loop(0, shards, start, 0)
-    fetch = pltpu.make_async_copy(down, wd, down_sem)
-    fetch.start()
+    fetch_rows(runs, where[0], pieces, wd, down_sem)
     for k in range(steps):
         cols = pl.ds(k * span, span)
         for m, acc in ((0, ga), (1, ua)):
@@ -284,6 +262,11 @@
             pltpu.make_async_copy(view, view, sems.at[m, k]).wait()
             term = nn(rows_in[:, cols], mats[m][cols, :])
             acc[...] = term if k == 0 else acc[...] + term
+    pltpu.make_async_copy(wd, wd, down_sem).wait()
+    for k in range(steps):
+        cols = pl.ds(k * span, span)
+        term = nn(rows_grad[:, cols], wd[cols, :])
+        ba[...] = term if k == 0 else ba[...] + term
 
     def point(i, _):
         r = pl.ds(pl.multiple_of(i * 16, 16), 16)
@@ -296,7 +279,6 @@
         return 0
 
     lax.fori_loop(0, hid.shape[0] // 16, point, 0)
-    fetch.wait()
     sources = 2 * NY
 
     def finish(k, _):
@@ -311,23 +293,23 @@
     lax.fori_loop(0, steps, finish, 0)
 
 
-def experts(rows_in, wd, back, chunk):
+def experts(where, rows_in, rows_grad, chunk, pieces, runs):
     rows, width = rows_in.shape
     shards, hidden = chunk.shape[0], chunk.shape[2]
     return pl.pallas_call(
-        expert_kernel,
+        functools.partial(expert_kernel, runs),
         out_shape=jax.ShapeDtypeStruct((2 * NY * BACK, width), BF16),
-        in_specs=[VMEM, HBM, VMEM, HBM],
+        in_specs=[SMEM, VMEM, VMEM, HBM] + [HBM] * len(pieces),
         out_specs=VMEM,
         scratch_shapes=[pltpu.VMEM((width, hidden), BF16)] * 3
-        + [pltpu.VMEM((rows, hidden), F32)] * 2
+        + [pltpu.VMEM((rows, hidden), F32)] * 3
         + [pltpu.VMEM((rows, hidden), BF16)] * 3
         + [pltpu.SemaphoreType.DMA((2, shards // 4)), pltpu.SemaphoreType.DMA(())],
-        compiler_params=params(50),
+        compiler_params=params(47),
         cost_estimate=pl.CostEstimate(
-            flops=10 * rows * width * hidden, bytes_accessed=14 * 2**20, transcendentals=rows * hidden
+            flops=12 * rows * width * hidden, bytes_accessed=20 * 2**20, transcendentals=rows * hidden
         ),
-    )(rows_in, wd, back, chunk)
+    )(where, rows_in, rows_grad, chunk, *pieces)
 
 
 def combine_kernel(hidden, grad_out, rows, target, prob, gain, layer_out, grad_in, grad_gate):
@@ -403,7 +385,7 @@
     parts = [partial[0]] + [along_y(partial[d], d) for d in (1, 2, 3)]
     hidden, send_in = norm_dispatch(x_resid, parts, gain, target_rows, slots)
     recv_in = exchange(send_in).reshape(slots, width)
-    both = experts(recv_in, *down_part(where, recv_grad, downs, runs), chunk)
+    both = experts(where, recv_in, recv_grad, chunk, downs, runs)
     rows = exchange(both).reshape(sources * BACK, width)
     return combine(hidden, grad_out, rows, returned, gate_prob, gain)
 

time: 209 us -> 211 us (level); the launches traced: 206 us -> 211 us
  starting transfers between devices: 60.3 us -> 66.4 us
  Pallas kernels: 36.4 us -> 32.4 us
  waiting for transfers between devices: 81.7 us -> 84.3 us
    all_gather x1, waiting for transfers between devices: 0.01 us -> 5.34 us  [per_device(): lax.all_gather(jnp.concatenate([w_gate[0], w_up[0]], axis=0), 'seq', axis=0)]
    ppermute x30, waiting for transfers between devices: 55.9 us -> 51.7 us  [shift_zx(): return lax.ppermute(block, 'seq', route)]
    all_to_all x3, starting transfers between devices: 14 us -> 17.2 us  [exchange(): return lax.all_to_all(split, 'exp', split_axis=0, concat_axis=0, tiled=True)]
    pallas_call x2 -> x1, Pallas kernels: 22.4 us -> 19.3 us  [experts(): pl.pallas_call(functools.partial(expert_kernel, runs), out_shape=jax.Shap...]
    ppermute x30, starting transfers between devices: 40.1 us -> 42.9 us  [shift_zx(): return lax.ppermute(block, 'seq', route)]
    unnamed x48 -> x36, local copies, waits for them, and re-layouts: 8.36 us -> 9.48 us
  transfers between devices with their start and end apart: 39 -> 39, of which waited for: 15 -> 15; matrix products, arithmetic and copies ran while one was open for 2% -> 4% of each run, Pallas kernels for 9% -> 5%
where the time goes in v3:
time: 211 us
  waiting for transfers between devices  84.3 us (40%)
  starting transfers between devices  66.4 us (31%)
  Pallas kernels  32.4 us (15%)
  between operations  14.3 us (7%)
  local copies, waits for them, and re-layouts  11.3 us (5%)
  other arithmetic  2.28 us (1%)
    ppermute x30, waiting for transfers between devices, shift_zx(): return lax.ppermute(block, 'seq', route)  51.7 us
    ppermute x30, starting transfers between devices, shift_zx(): return lax.ppermute(block, 'seq', route)  42.9 us
    pallas_call x1, Pallas kernels, experts(): pl.pallas_call(functools.partial(expert_kernel, runs), out_shape=jax.Shap...  19.3 us
    all_to_all x3, waiting for transfers between devices, exchange(): return lax.all_to_all(split, 'exp', split_axis=0, concat_axis=0, tiled=True)  18.6 us
    all_to_all x3, starting transfers between devices, exchange(): return lax.all_to_all(split, 'exp', split_axis=0, concat_axis=0, tiled=True)  17.2 us
    unnamed x36, local copies, waits for them, and re-layouts  9.48 us
    ppermute x3, waiting for transfers between devices, along_y(): lax.ppermute(block, 'exp', [(i, (i + 2 * d) % (2 * NY)) for i in range(2...  8.69 us
    pallas_call x1, Pallas kernels, attention(): pl.pallas_call(attention_kernel, out_shape=jax.ShapeDtypeStruct(q.shape,...  6.6 us
  transfers between devices with their start and end apart: 39, of which 15 were waited for; matrix products, arithmetic and copies ran while one was open for 4% of the time, Pallas kernels for 5%

profile of v3, /device:TPU:2, one launch (start us, length us, event | category | flops | bytes accessed | tf_op | source)
XLA Modules:
  0.0 211.0 jit_solution(4081151953056844220)
XLA Ops:
  7.2 1.8 pad_maximum_fusion
  9.1 1.6 constant_dynamic-update-slice_fusion.8
  10.7 2.3 %collective-permute-start.15 = (bf16[32,1408]{1,0:T(8,128)(2,1)S(1)}, bf16[32,1408]{1,0:T(8,128)(2,1)S(1)}, u32[]{:S(2)}, u32[]{:S(2)}) collective-permute-start(bf16[32,1408]{1,0:T(8,128)(2,1)S(1)} %get-tuple-element.45), channel_id=1, source_target_pairs={{0,24},{8,0},{16,8},{24,16},{32,56},{40,32},{48,40},{56,48},{64,88... | collective-permute-start | bytes 270344 | tf_op jit(solution)/shard_map/ppermute | solution.py:41
  13.7 1.8 collective-permute-start.13
  15.5 1.9 collective-permute-start.16
  17.4 3.9 %collective-permute-start.19 = (bf16[32,1408]{1,0:T(8,128)(2,1)S(1)}, bf16[32,1408]{1,0:T(8,128)(2,1)S(1)}, u32[]{:S(2)}, u32[]{:S(2)}) collective-permute-start(bf16[32,1408]{1,0:T(8,128)(2,1)S(1)} %get-tuple-element.44), channel_id=1, source_target_pairs={{0,224},{8,232},{16,240},{24,248},{32,0},{40,8},{48,16},{56,24},{6... | collective-permute-start | bytes 270344 | tf_op jit(solution)/shard_map/ppermute | solution.py:41
  22.3 1.5 collective-permute-done.16
  24.5 9.7 %collective-permute-done.k4 = bf16[512,256]{1,0:T(8,128)(2,1)S(1)} collective-permute-done((bf16[512,256]{1,0:T(8,128)(2,1)S(1)}, bf16[512,256]{1,0:T(8,128)(2,1)S(1)}, u32[]{:S(2)}, u32[]{:S(2)}) %collective-permute-start) | collective-permute-done | bytes 262176 | tf_op jit(solution)/shard_map/ppermute | solution.py:41
  34.4 1.9 collective-permute-start.2
  36.3 1.4 collective-permute-start.3
  37.7 5.0 %collective-permute-done.4.v4 = bf16[512,256]{1,0:T(8,128)(2,1)S(1)} collective-permute-done((bf16[512,256]{1,0:T(8,128)(2,1)S(1)}, bf16[512,256]{1,0:T(8,128)(2,1)S(1)}, u32[]{:S(2)}, u32[]{:S(2)}) %collective-permute-start.4) | collective-permute-done | bytes 262176 | tf_op jit(solution)/shard_map/ppermute | solution.py:41
  42.8 0.9 collective-permute-start.20
  43.7 2.1 %collective-permute-done.17 = bf16[32,1408]{1,0:T(8,128)(2,1)S(1)} collective-permute-done((bf16[32,1408]{1,0:T(8,128)(2,1)S(1)}, bf16[32,1408]{1,0:T(8,128)(2,1)S(1)}, u32[]{:S(2)}, u32[]{:S(2)}) %collective-permute-start.17) | collective-permute-done | bytes 90144 | tf_op jit(solution)/shard_map/ppermute | solution.py:41
  45.9 2.3 %collective-permute-done.20 = bf16[32,1408]{1,0:T(8,128)(2,1)S(1)} collective-permute-done((bf16[32,1408]{1,0:T(8,128)(2,1)S(1)}, bf16[32,1408]{1,0:T(8,128)(2,1)S(1)}, u32[]{:S(2)}, u32[]{:S(2)}) %collective-permute-start.20) | collective-permute-done | bytes 90144 | tf_op jit(solution)/shard_map/ppermute | solution.py:41
  48.1 3.1 %collective-permute-start.21 = (bf16[32,1408]{1,0:T(8,128)(2,1)S(1)}, bf16[32,1408]{1,0:T(8,128)(2,1)S(1)}, u32[]{:S(2)}, u32[]{:S(2)}) collective-permute-start(bf16[32,1408]{1,0:T(8,128)(2,1)S(1)} %collective-permute-done.20), channel_id=1, source_target_pairs={{0,224},{8,232},{16,240},{24,248},{32,0},{40,8},{48,16},{56,24},{6... | collective-permute-start | bytes 270344 | tf_op jit(solution)/shard_map/ppermute | solution.py:41
  52.8 1.0 collective-permute-done.21
  53.8 2.5 %collective-permute-start.6 = (bf16[512,256]{1,0:T(8,128)(2,1)S(1)}, bf16[512,256]{1,0:T(8,128)(2,1)S(1)}, u32[]{:S(2)}, u32[]{:S(2)}) collective-permute-start(bf16[512,256]{1,0:T(8,128)(2,1)S(1)} %get-tuple-element.36), channel_id=1, source_target_pairs={{0,16},{8,24},{16,0},{24,8},{32,48},{40,56},{48,32},{56,40},{64,80... | collective-permute-start | bytes 786440 | tf_op jit(solution)/shard_map/ppermute | solution.py:41
  59.0 2.6 %collective-permute-start.23 = (bf16[128,1408]{1,0:T(8,128)(2,1)S(1)}, bf16[128,1408]{1,0:T(8,128)(2,1)}, u32[]{:S(2)}, u32[]{:S(2)}) collective-permute-start(bf16[128,1408]{1,0:T(8,128)(2,1)S(1)} %pad_maximum_fusion.1.refs_0_), channel_id=1, source_target_pairs={{0,224},{8,232},{16,240},{24,248},{32,0},{40,8},{48,16},{56,24},{6... | collective-permute-start | bytes 1081352 | tf_op jit(solution)/shard_map/ppermute | solution.py:41
  61.8 1.9 collective-permute-start.30
  63.7 0.8 collective-permute-done.7.v3
  64.5 6.6 %shard_map.139 = bf16[512,256]{1,0:T(8,128)(2,1)S(1)} custom-call(s32[3]{0:T(128)S(1)} %pad_add_fusion.where, bf16[512,256]{1,0:T(8,128)(2,1)S(1)} %copy-done.6, bf16[512,256]{1,0:T(8,128)(2,1)S(1)} %copy-done.2, bf16[512,256]{1,0:T(8,128)(2,1)S(1)} %collective-permute-done.1.k1, bf16[512,256]{1,0:T(8,128)(2,1)S(1)} %collective-permute-done.2.k2, ...), custom_call_target="tpu_custom_call" | custom-call | flops 1342177280 | bytes 6291456 | tf_op jit(solution)/shard_map/pallas_call | solution.py:122
  71.8 1.2 shard_map.142
  73.1 5.2 %all-to-all-start.1 = ((bf16[8,24,2048]{2,1,0:T(8,128)(2,1)}), bf16[8,24,2048]{2,1,0:T(8,128)(2,1)}, u32[]{:S(2)}, u32[]{:S(2)}) async-start(bf16[8,24,2048]{2,1,0:T(8,128)(2,1)} %bitcast.14), calls=%async_computation.1 | async-start | bytes 1572864 | tf_op jit(solution)/shard_map/all_to_all | solution.py:377
  78.3 2.5 %collective-permute-start.31 = (bf16[16,1408]{1,0:T(8,128)(2,1)S(1)}, bf16[16,1408]{1,0:T(8,128)(2,1)S(1)}, u32[]{:S(2)}, u32[]{:S(2)}) collective-permute-start(bf16[16,1408]{1,0:T(8,128)(2,1)S(1)} %slice.49), channel_id=1, source_target_pairs={{0,224},{8,232},{16,240},{24,248},{32,0},{40,8},{48,16},{56,24},{6... | collective-permute-start | bytes 135176 | tf_op jit(solution)/shard_map/ppermute | solution.py:41
  80.8 1.6 shard_map.140
  82.5 2.0 collective-permute-start.10
  84.5 2.7 %collective-permute-start.11 = (bf16[64,2048]{1,0:T(8,128)(2,1)S(1)}, bf16[64,2048]{1,0:T(8,128)(2,1)S(1)}, u32[]{:S(2)}, u32[]{:S(2)}) collective-permute-start(bf16[64,2048]{1,0:T(8,128)(2,1)S(1)} %get-tuple-element.32), channel_id=1, source_target_pairs={{0,4},{1,5},{2,6},{3,7},{4,0},{5,1},{6,2},{7,3},{8,12},{9,13},{10,... | collective-permute-start | bytes 786440 | tf_op jit(solution)/shard_map/ppermute | solution.py:53
  87.2 1.5 collective-permute-start.12
  89.3 3.2 %collective-permute-start.25 = (bf16[128,1408]{1,0:T(8,128)(2,1)}, bf16[128,1408]{1,0:T(8,128)(2,1)}, u32[]{:S(2)}, u32[]{:S(2)}) collective-permute-start(bf16[128,1408]{1,0:T(8,128)(2,1)} %collective-permute-done.23.refs_2_), channel_id=1, source_target_pairs={{0,224},{8,232},{16,240},{24,248},{32,0},{40,8},{48,16},{56,24},{6... | collective-permute-start | bytes 1081352 | tf_op jit(solution)/shard_map/ppermute | solution.py:41
  93.1 3.8 %collective-permute-done.10.p1 = bf16[64,2048]{1,0:T(8,128)(2,1)S(1)} collective-permute-done((bf16[64,2048]{1,0:T(8,128)(2,1)S(1)}, bf16[64,2048]{1,0:T(8,128)(2,1)S(1)}, u32[]{:S(2)}, u32[]{:S(2)}) %collective-permute-start.10) | collective-permute-done | bytes 262176 | tf_op jit(solution)/shard_map/ppermute | solution.py:53
  96.9 0.9 collective-permute-start.32
  97.8 4.9 %collective-permute-done.11.p2 = bf16[64,2048]{1,0:T(8,128)(2,1)S(1)} collective-permute-done((bf16[64,2048]{1,0:T(8,128)(2,1)S(1)}, bf16[64,2048]{1,0:T(8,128)(2,1)S(1)}, u32[]{:S(2)}, u32[]{:S(2)}) %collective-permute-start.11) | collective-permute-done | bytes 262176 | tf_op jit(solution)/shard_map/ppermute | solution.py:53
  102.7 1.9 collective-permute-start.33
  104.6 1.1 collective-permute-start.34
  105.7 1.5 shard_map.141
  107.2 3.5 %all-to-all-start = ((bf16[8,24,2048]{2,1,0:T(8,128)(2,1)}), bf16[8,24,2048]{2,1,0:T(8,128)(2,1)S(1)}, u32[]{:S(2)}, u32[]{:S(2)}) async-start(bf16[8,24,2048]{2,1,0:T(8,128)(2,1)} %bitcast.12), calls=%async_computation | async-start | bytes 1572864 | tf_op jit(solution)/shard_map/all_to_all | solution.py:377
  110.8 0.7 collective-permute-start.26
  111.5 2.6 %collective-permute-start.27 = (bf16[128,1408]{1,0:T(8,128)(2,1)}, bf16[128,1408]{1,0:T(8,128)(2,1)S(1)}, u32[]{:S(2)}, u32[]{:S(2)}) collective-permute-start(bf16[128,1408]{1,0:T(8,128)(2,1)} %collective-permute-done.25.refs_4_), channel_id=1, source_target_pairs={{0,224},{8,232},{16,240},{24,248},{32,0},{40,8},{48,16},{56,24},{6... | collective-permute-start | bytes 1081352 | tf_op jit(solution)/shard_map/ppermute | solution.py:41
  114.1 16.7 %collective-permute-done.26.refs_5_ = bf16[128,1408]{1,0:T(8,128)(2,1)S(1)} collective-permute-done((bf16[128,1408]{1,0:T(8,128)(2,1)S(1)}, bf16[128,1408]{1,0:T(8,128)(2,1)S(1)}, u32[]{:S(2)}, u32[]{:S(2)}) %collective-permute-start.26) | collective-permute-done | bytes 360480 | tf_op jit(solution)/shard_map/ppermute | solution.py:41
  131.0 3.3 %collective-permute-start.29 = (bf16[64,1408]{1,0:T(8,128)(2,1)S(1)}, bf16[64,1408]{1,0:T(8,128)(2,1)S(1)}, u32[]{:S(2)}, u32[]{:S(2)}) collective-permute-start(bf16[64,1408]{1,0:T(8,128)(2,1)S(1)} %slice.47), channel_id=1, source_target_pairs={{0,224},{8,232},{16,240},{24,248},{32,0},{40,8},{48,16},{56,24},{6... | collective-permute-start | bytes 540680 | tf_op jit(solution)/shard_map/ppermute | solution.py:41
  134.3 12.0 %collective-permute-done.34.refs_12_ = bf16[256,1408]{1,0:T(8,128)(2,1)} collective-permute-done((bf16[256,1408]{1,0:T(8,128)(2,1)}, bf16[256,1408]{1,0:T(8,128)(2,1)}, u32[]{:S(2)}, u32[]{:S(2)}) %collective-permute-start.34) | collective-permute-done | bytes 720928 | tf_op jit(solution)/shard_map/ppermute | solution.py:41
  147.7 5.3 %all-gather.3.cloned.1.call-done = bf16[4096,1408]{1,0:T(8,128)(2,1)} async-done(((bf16[128,1408]{1,0:T(8,128)(2,1)}), bf16[4096,1408]{1,0:T(8,128)(2,1)}) %all-gather.3.cloned.1.call-update) | async-done | bytes 11534352 | tf_op jit(solution)/shard_map/all_gather | solution.py:358
  153.0 0.9 copy-done.8
  154.0 0.9 copy-done.10
  154.9 19.3 %shard_map.143 = bf16[320,2048]{1,0:T(8,128)(2,1)} custom-call(s32[3]{0:T(128)S(1)} %pad_add_fusion.where, bf16[192,2048]{1,0:T(8,128)(2,1)S(1)} %bitcast.36, bf16[192,2048]{1,0:T(8,128)(2,1)} %bitcast.15.rows_grad, bf16[32,128,1408]{2,1,0:T(8,128)(2,1)} %bitcast.44, bf16[128,1408]{1,0:T(8,128)(2,1)S(1)} %pad_maximum_fusion.1.refs_0_, ...), custom_call_target="tpu_custom_call" | custom-call | flops 6643777536 | bytes 20971520 | tf_op jit(solution)/shard_map/pallas_call | solution.py:299
  174.2 8.4 %all-to-all-start.2 = ((bf16[8,40,2048]{2,1,0:T(8,128)(2,1)}), bf16[8,40,2048]{2,1,0:T(8,128)(2,1)S(1)}, u32[]{:S(2)}, u32[]{:S(2)}) async-start(bf16[8,40,2048]{2,1,0:T(8,128)(2,1)} %bitcast.40), calls=%async_computation.2 | async-start | bytes 2621440 | tf_op jit(solution)/shard_map/all_to_all | solution.py:377
  182.8 18.6 %all-to-all-done.2 = bf16[8,40,2048]{2,1,0:T(8,128)(2,1)S(1)} async-done(((bf16[8,40,2048]{2,1,0:T(8,128)(2,1)}), bf16[8,40,2048]{2,1,0:T(8,128)(2,1)S(1)}, u32[]{:S(2)}, u32[]{:S(2)}) %all-to-all-start.2) | async-done | bytes 1310752 | tf_op jit(solution)/shard_map/all_to_all | solution.py:377
  201.4 2.2 %shard_map.144 = (bf16[64,2048]{1,0:T(8,128)(2,1)}, bf16[64,2048]{1,0:T(8,128)(2,1)}, f32[64,2]{1,0:T(8,128)S(1)}) custom-call(bf16[64,2048]{1,0:T(8,128)(2,1)S(1)} %get-tuple-element.12.hidden, bf16[64,2048]{1,0:T(8,128)(2,1)S(1)} %copy-done.1, bf16[320,2048]{1,0:T(8,128)(2,1)S(1)} %bitcast.35, s32[64,2]{1,0:T(8,128)S(1)} %add.31.target, ...), custom_call_target="tpu_custom_call" | custom-call | flops 268435456 | bytes 3145728 | tf_op jit(solution)/shard_map/pallas_call | solution.py:341
  (93 shorter events, 11.4 us)
Async XLA Ops:
  7.2 14.2 %copy-start.11 = (s32[64,2]{0,1:T(2,128)S(1)}, s32[64,2]{0,1:T(2,128)}, u32[]{:S(2)}) copy-start(s32[64,2]{0,1:T(2,128)} %param.21) | copy-start | bytes 1540
  7.2 14.9 %copy-start.2 = (bf16[512,256]{1,0:T(8,128)(2,1)S(1)}, bf16[512,256]{1,0:T(8,128)(2,1)}, u32[]{:S(2)}) copy-start(bf16[512,256]{1,0:T(8,128)(2,1)} %k0.1) | copy-start | bytes 786436
  7.2 15.0 %copy-start.3 = (bf16[512,256]{1,0:T(8,128)(2,1)S(1)}, bf16[512,256]{1,0:T(8,128)(2,1)}, u32[]{:S(2)}) copy-start(bf16[512,256]{1,0:T(8,128)(2,1)} %v0.1) | copy-start | bytes 786436
  7.2 145.8 %all-gather.3.cloned.1.call-start = ((), (), s32[]{:S(2)}) async-start(), calls=%async_computation.3 | async-start | bytes 11894784 | tf_op jit(solution)/shard_map/all_gather | solution.py:358
  10.7 11.3 %collective-permute-start.15 = (bf16[32,1408]{1,0:T(8,128)(2,1)S(1)}, bf16[32,1408]{1,0:T(8,128)(2,1)S(1)}, u32[]{:S(2)}, u32[]{:S(2)}) collective-permute-start(bf16[32,1408]{1,0:T(8,128)(2,1)S(1)} %get-tuple-element.45), channel_id=1, source_target_pairs={{0,24},{8,0},{16,8},{24,16},{32,56},{40,32},{48,40},{56,48},{64,88... | collective-permute-start | bytes 270344 | tf_op jit(solution)/shard_map/ppermute | solution.py:41
  13.0 9.2 %collective-permute-start.14 = (bf16[32,1408]{1,0:T(8,128)(2,1)S(1)}, bf16[32,1408]{1,0:T(8,128)(2,1)S(1)}, u32[]{:S(2)}, u32[]{:S(2)}) collective-permute-start(bf16[32,1408]{1,0:T(8,128)(2,1)S(1)} %get-tuple-element.45), channel_id=1, source_target_pairs={{0,16},{8,24},{16,0},{24,8},{32,48},{40,56},{48,32},{56,40},{64,80... | collective-permute-start | bytes 270344 | tf_op jit(solution)/shard_map/ppermute | solution.py:41
  13.7 8.6 %collective-permute-start.13 = (bf16[32,1408]{1,0:T(8,128)(2,1)S(1)}, bf16[32,1408]{1,0:T(8,128)(2,1)S(1)}, u32[]{:S(2)}, u32[]{:S(2)}) collective-permute-start(bf16[32,1408]{1,0:T(8,128)(2,1)S(1)} %get-tuple-element.45), channel_id=1, source_target_pairs={{0,8},{8,16},{16,24},{24,0},{32,40},{40,48},{48,56},{56,32},{64,72... | collective-permute-start | bytes 270344 | tf_op jit(solution)/shard_map/ppermute | solution.py:41
  15.5 8.4 %collective-permute-start.16 = (bf16[32,1408]{1,0:T(8,128)(2,1)S(1)}, bf16[32,1408]{1,0:T(8,128)(2,1)S(1)}, u32[]{:S(2)}, u32[]{:S(2)}) collective-permute-start(bf16[32,1408]{1,0:T(8,128)(2,1)S(1)} %get-tuple-element.44), channel_id=1, source_target_pairs={{0,32},{8,40},{16,48},{24,56},{32,64},{40,72},{48,80},{56,88},{64,... | collective-permute-start | bytes 270344 | tf_op jit(solution)/shard_map/ppermute | solution.py:41
  17.4 20.3 %collective-permute-start.19 = (bf16[32,1408]{1,0:T(8,128)(2,1)S(1)}, bf16[32,1408]{1,0:T(8,128)(2,1)S(1)}, u32[]{:S(2)}, u32[]{:S(2)}) collective-permute-start(bf16[32,1408]{1,0:T(8,128)(2,1)S(1)} %get-tuple-element.44), channel_id=1, source_target_pairs={{0,224},{8,232},{16,240},{24,248},{32,0},{40,8},{48,16},{56,24},{6... | collective-permute-start | bytes 270344 | tf_op jit(solution)/shard_map/ppermute | solution.py:41
  22.1 12.1 %collective-permute-start = (bf16[512,256]{1,0:T(8,128)(2,1)S(1)}, bf16[512,256]{1,0:T(8,128)(2,1)S(1)}, u32[]{:S(2)}, u32[]{:S(2)}) collective-permute-start(bf16[512,256]{1,0:T(8,128)(2,1)S(1)} %copy-done.2), channel_id=1, source_target_pairs={{0,32},{8,40},{16,48},{24,56},{32,64},{40,72},{48,80},{56,88},{64,... | collective-permute-start | bytes 786440 | tf_op jit(solution)/shard_map/ppermute | solution.py:41
  22.2 20.6 %collective-permute-start.4 = (bf16[512,256]{1,0:T(8,128)(2,1)S(1)}, bf16[512,256]{1,0:T(8,128)(2,1)S(1)}, u32[]{:S(2)}, u32[]{:S(2)}) collective-permute-start(bf16[512,256]{1,0:T(8,128)(2,1)S(1)} %copy-done.3), channel_id=1, source_target_pairs={{0,32},{8,40},{16,48},{24,56},{32,64},{40,72},{48,80},{56,88},{64,... | collective-permute-start | bytes 786440 | tf_op jit(solution)/shard_map/ppermute | solution.py:41
  24.5 32.6 %copy-start = (bf16[256,2048]{1,0:T(8,128)(2,1)S(1)}, bf16[256,2048]{1,0:T(8,128)(2,1)}, u32[]{:S(2)}) copy-start(bf16[256,2048]{1,0:T(8,128)(2,1)} %w_own.1) | copy-start | bytes 3145732
  34.3 30.2 %copy-start.6 = (bf16[512,256]{1,0:T(8,128)(2,1)S(1)}, bf16[512,256]{1,0:T(8,128)(2,1)}, u32[]{:S(2)}) copy-start(bf16[512,256]{1,0:T(8,128)(2,1)} %q.1) | copy-start | bytes 786436
  34.3 22.0 %collective-permute-start.1 = (bf16[512,256]{1,0:T(8,128)(2,1)S(1)}, bf16[512,256]{1,0:T(8,128)(2,1)S(1)}, u32[]{:S(2)}, u32[]{:S(2)}) collective-permute-start(bf16[512,256]{1,0:T(8,128)(2,1)S(1)} %get-tuple-element.40), channel_id=1, source_target_pairs={{0,8},{8,16},{16,24},{24,0},{32,40},{40,48},{48,56},{56,32},{64,72... | collective-permute-start | bytes 786440 | tf_op jit(solution)/shard_map/ppermute | solution.py:41
  34.4 22.0 %collective-permute-start.2 = (bf16[512,256]{1,0:T(8,128)(2,1)S(1)}, bf16[512,256]{1,0:T(8,128)(2,1)S(1)}, u32[]{:S(2)}, u32[]{:S(2)}) collective-permute-start(bf16[512,256]{1,0:T(8,128)(2,1)S(1)} %get-tuple-element.39), channel_id=1, source_target_pairs={{0,16},{8,24},{16,0},{24,8},{32,48},{40,56},{48,32},{56,40},{64,80... | collective-permute-start | bytes 786440 | tf_op jit(solution)/shard_map/ppermute | solution.py:41
  36.3 20.7 %collective-permute-start.3 = (bf16[512,256]{1,0:T(8,128)(2,1)S(1)}, bf16[512,256]{1,0:T(8,128)(2,1)S(1)}, u32[]{:S(2)}, u32[]{:S(2)}) collective-permute-start(bf16[512,256]{1,0:T(8,128)(2,1)S(1)} %get-tuple-element.38), channel_id=1, source_target_pairs={{0,24},{8,0},{16,8},{24,16},{32,56},{40,32},{48,40},{56,48},{64,88... | collective-permute-start | bytes 786440 | tf_op jit(solution)/shard_map/ppermute | solution.py:41
  37.7 8.1 %collective-permute-start.17 = (bf16[32,1408]{1,0:T(8,128)(2,1)S(1)}, bf16[32,1408]{1,0:T(8,128)(2,1)S(1)}, u32[]{:S(2)}, u32[]{:S(2)}) collective-permute-start(bf16[32,1408]{1,0:T(8,128)(2,1)S(1)} %collective-permute-done.16), channel_id=1, source_target_pairs={{0,32},{8,40},{16,48},{24,56},{32,64},{40,72},{48,80},{56,88},{64,... | collective-permute-start | bytes 270344 | tf_op jit(solution)/shard_map/ppermute | solution.py:41
  42.8 5.4 %collective-permute-start.20 = (bf16[32,1408]{1,0:T(8,128)(2,1)S(1)}, bf16[32,1408]{1,0:T(8,128)(2,1)S(1)}, u32[]{:S(2)}, u32[]{:S(2)}) collective-permute-start(bf16[32,1408]{1,0:T(8,128)(2,1)S(1)} %collective-permute-done.19), channel_id=1, source_target_pairs={{0,224},{8,232},{16,240},{24,248},{32,0},{40,8},{48,16},{56,24},{6... | collective-permute-start | bytes 270344 | tf_op jit(solution)/shard_map/ppermute | solution.py:41
  45.9 6.3 %collective-permute-start.18 = (bf16[32,1408]{1,0:T(8,128)(2,1)S(1)}, bf16[32,1408]{1,0:T(8,128)(2,1)S(1)}, u32[]{:S(2)}, u32[]{:S(2)}) collective-permute-start(bf16[32,1408]{1,0:T(8,128)(2,1)S(1)} %collective-permute-done.17), channel_id=1, source_target_pairs={{0,32},{8,40},{16,48},{24,56},{32,64},{40,72},{48,80},{56,88},{64,... | collective-permute-start | bytes 270344 | tf_op jit(solution)/shard_map/ppermute | solution.py:41
  48.1 5.7 %collective-permute-start.21 = (bf16[32,1408]{1,0:T(8,128)(2,1)S(1)}, bf16[32,1408]{1,0:T(8,128)(2,1)S(1)}, u32[]{:S(2)}, u32[]{:S(2)}) collective-permute-start(bf16[32,1408]{1,0:T(8,128)(2,1)S(1)} %collective-permute-done.20), channel_id=1, source_target_pairs={{0,224},{8,232},{16,240},{24,248},{32,0},{40,8},{48,16},{56,24},{6... | collective-permute-start | bytes 270344 | tf_op jit(solution)/shard_map/ppermute | solution.py:41
  52.1 6.9 %collective-permute-start.5 = (bf16[512,256]{1,0:T(8,128)(2,1)S(1)}, bf16[512,256]{1,0:T(8,128)(2,1)S(1)}, u32[]{:S(2)}, u32[]{:S(2)}) collective-permute-start(bf16[512,256]{1,0:T(8,128)(2,1)S(1)} %get-tuple-element.37), channel_id=1, source_target_pairs={{0,8},{8,16},{16,24},{24,0},{32,40},{40,48},{48,56},{56,32},{64,72... | collective-permute-start | bytes 786440 | tf_op jit(solution)/shard_map/ppermute | solution.py:41
  53.8 8.0 %collective-permute-start.6 = (bf16[512,256]{1,0:T(8,128)(2,1)S(1)}, bf16[512,256]{1,0:T(8,128)(2,1)S(1)}, u32[]{:S(2)}, u32[]{:S(2)}) collective-permute-start(bf16[512,256]{1,0:T(8,128)(2,1)S(1)} %get-tuple-element.36), channel_id=1, source_target_pairs={{0,16},{8,24},{16,0},{24,8},{32,48},{40,56},{48,32},{56,40},{64,80... | collective-permute-start | bytes 786440 | tf_op jit(solution)/shard_map/ppermute | solution.py:41
  56.3 8.1 %collective-permute-start.7 = (bf16[512,256]{1,0:T(8,128)(2,1)S(1)}, bf16[512,256]{1,0:T(8,128)(2,1)S(1)}, u32[]{:S(2)}, u32[]{:S(2)}) collective-permute-start(bf16[512,256]{1,0:T(8,128)(2,1)S(1)} %get-tuple-element.35), channel_id=1, source_target_pairs={{0,24},{8,0},{16,8},{24,16},{32,56},{40,32},{48,40},{56,48},{64,88... | collective-permute-start | bytes 786440 | tf_op jit(solution)/shard_map/ppermute | solution.py:41
  56.4 32.9 %collective-permute-start.22 = (bf16[128,1408]{1,0:T(8,128)(2,1)S(1)}, bf16[128,1408]{1,0:T(8,128)(2,1)}, u32[]{:S(2)}, u32[]{:S(2)}) collective-permute-start(bf16[128,1408]{1,0:T(8,128)(2,1)S(1)} %pad_maximum_fusion.1.refs_0_), channel_id=1, source_target_pairs={{0,32},{8,40},{16,48},{24,56},{32,64},{40,72},{48,80},{56,88},{64,... | collective-permute-start | bytes 1081352 | tf_op jit(solution)/shard_map/ppermute | solution.py:41
  57.1 23.7 %collective-permute-start.9 = (bf16[256,2048]{1,0:T(8,128)(2,1)S(1)}, bf16[256,2048]{1,0:T(8,128)(2,1)S(1)}, u32[]{:S(2)}, u32[]{:S(2)}) collective-permute-start(bf16[256,2048]{1,0:T(8,128)(2,1)S(1)} %copy-done), channel_id=1, source_target_pairs={{0,1},{1,0},{2,3},{3,2},{4,5},{5,4},{6,7},{7,6},{8,9},{9,8},{10,11... | collective-permute-start | bytes 3145736 | tf_op jit(solution)/shard_map/ppermute | solution.py:57
  59.0 12.9 %copy-start.1 = (bf16[64,2048]{1,0:T(8,128)(2,1)S(1)}, bf16[64,2048]{1,0:T(8,128)(2,1)}, u32[]{:S(2)}) copy-start(bf16[64,2048]{1,0:T(8,128)(2,1)} %grad_out.1) | copy-start | bytes 786436
  59.0 30.3 %collective-permute-start.23 = (bf16[128,1408]{1,0:T(8,128)(2,1)S(1)}, bf16[128,1408]{1,0:T(8,128)(2,1)}, u32[]{:S(2)}, u32[]{:S(2)}) collective-permute-start(bf16[128,1408]{1,0:T(8,128)(2,1)S(1)} %pad_maximum_fusion.1.refs_0_), channel_id=1, source_target_pairs={{0,224},{8,232},{16,240},{24,248},{32,0},{40,8},{48,16},{56,24},{6... | collective-permute-start | bytes 1081352 | tf_op jit(solution)/shard_map/ppermute | solution.py:41
  61.8 22.8 %collective-permute-start.30 = (bf16[16,1408]{1,0:T(8,128)(2,1)S(1)}, bf16[16,1408]{1,0:T(8,128)(2,1)S(1)}, u32[]{:S(2)}, u32[]{:S(2)}) collective-permute-start(bf16[16,1408]{1,0:T(8,128)(2,1)S(1)} %slice.48), channel_id=1, source_target_pairs={{0,32},{8,40},{16,48},{24,56},{32,64},{40,72},{48,80},{56,88},{64,... | collective-permute-start | bytes 135176 | tf_op jit(solution)/shard_map/ppermute | solution.py:41
  71.1 7.2 %collective-permute-start.8 = (bf16[4,64,256]{2,1,0:T(8,128)(2,1)S(1)}, bf16[4,64,256]{2,1,0:T(8,128)(2,1)S(1)}, u32[]{:S(2)}, u32[]{:S(2)}) collective-permute-start(bf16[4,64,256]{2,1,0:T(8,128)(2,1)S(1)} %get-tuple-element.41), channel_id=1, source_target_pairs={{0,1},{1,0},{2,3},{3,2},{4,5},{5,4},{6,7},{7,6},{8,9},{9,8},{10,11... | collective-permute-start | bytes 393224 | tf_op jit(solution)/shard_map/ppermute | solution.py:57
  73.1 34.1 %all-to-all-start.1 = ((bf16[8,24,2048]{2,1,0:T(8,128)(2,1)}), bf16[8,24,2048]{2,1,0:T(8,128)(2,1)}, u32[]{:S(2)}, u32[]{:S(2)}) async-start(bf16[8,24,2048]{2,1,0:T(8,128)(2,1)} %bitcast.14), calls=%async_computation.1 | async-start | bytes 1572864 | tf_op jit(solution)/shard_map/all_to_all | solution.py:377
  78.3 8.9 %collective-permute-start.31 = (bf16[16,1408]{1,0:T(8,128)(2,1)S(1)}, bf16[16,1408]{1,0:T(8,128)(2,1)S(1)}, u32[]{:S(2)}, u32[]{:S(2)}) collective-permute-start(bf16[16,1408]{1,0:T(8,128)(2,1)S(1)} %slice.49), channel_id=1, source_target_pairs={{0,224},{8,232},{16,240},{24,248},{32,0},{40,8},{48,16},{56,24},{6... | collective-permute-start | bytes 135176 | tf_op jit(solution)/shard_map/ppermute | solution.py:41
  82.4 23.3 %copy-start.4 = (bf16[64,2048]{1,0:T(8,128)(2,1)S(1)}, bf16[64,2048]{1,0:T(8,128)(2,1)}, u32[]{:S(2)}) copy-start(bf16[64,2048]{1,0:T(8,128)(2,1)} %x.1) | copy-start | bytes 786436
  82.4 23.3 %copy-start.5 = (f32[2048]{0:T(1024)S(1)}, f32[2048]{0:T(1024)}, u32[]{:S(2)}) copy-start(f32[2048]{0:T(1024)} %param.17) | copy-start | bytes 24580
  82.5 14.4 %collective-permute-start.10 = (bf16[64,2048]{1,0:T(8,128)(2,1)S(1)}, bf16[64,2048]{1,0:T(8,128)(2,1)S(1)}, u32[]{:S(2)}, u32[]{:S(2)}) collective-permute-start(bf16[64,2048]{1,0:T(8,128)(2,1)S(1)} %get-tuple-element.33), channel_id=1, source_target_pairs={{0,2},{1,3},{2,4},{3,5},{4,6},{5,7},{6,0},{7,1},{8,10},{9,11},{10,... | collective-permute-start | bytes 786440 | tf_op jit(solution)/shard_map/ppermute | solution.py:53
  84.5 18.2 %collective-permute-start.11 = (bf16[64,2048]{1,0:T(8,128)(2,1)S(1)}, bf16[64,2048]{1,0:T(8,128)(2,1)S(1)}, u32[]{:S(2)}, u32[]{:S(2)}) collective-permute-start(bf16[64,2048]{1,0:T(8,128)(2,1)S(1)} %get-tuple-element.32), channel_id=1, source_target_pairs={{0,4},{1,5},{2,6},{3,7},{4,0},{5,1},{6,2},{7,3},{8,12},{9,13},{10,... | collective-permute-start | bytes 786440 | tf_op jit(solution)/shard_map/ppermute | solution.py:53
  87.2 17.4 %collective-permute-start.12 = (bf16[64,2048]{1,0:T(8,128)(2,1)S(1)}, bf16[64,2048]{1,0:T(8,128)(2,1)S(1)}, u32[]{:S(2)}, u32[]{:S(2)}) collective-permute-start(bf16[64,2048]{1,0:T(8,128)(2,1)S(1)} %get-tuple-element.31), channel_id=1, source_target_pairs={{0,6},{1,7},{2,0},{3,1},{4,2},{5,3},{6,4},{7,5},{8,14},{9,15},{10,... | collective-permute-start | bytes 786440 | tf_op jit(solution)/shard_map/ppermute | solution.py:53
  89.3 21.5 %collective-permute-start.24 = (bf16[128,1408]{1,0:T(8,128)(2,1)}, bf16[128,1408]{1,0:T(8,128)(2,1)S(1)}, u32[]{:S(2)}, u32[]{:S(2)}) collective-permute-start(bf16[128,1408]{1,0:T(8,128)(2,1)} %collective-permute-done.22.refs_1_), channel_id=1, source_target_pairs={{0,32},{8,40},{16,48},{24,56},{32,64},{40,72},{48,80},{56,88},{64,... | collective-permute-start | bytes 1081352 | tf_op jit(solution)/shard_map/ppermute | solution.py:41
  89.3 22.2 %collective-permute-start.25 = (bf16[128,1408]{1,0:T(8,128)(2,1)}, bf16[128,1408]{1,0:T(8,128)(2,1)}, u32[]{:S(2)}, u32[]{:S(2)}) collective-permute-start(bf16[128,1408]{1,0:T(8,128)(2,1)} %collective-permute-done.23.refs_2_), channel_id=1, source_target_pairs={{0,224},{8,232},{16,240},{24,248},{32,0},{40,8},{48,16},{56,24},{6... | collective-permute-start | bytes 1081352 | tf_op jit(solution)/shard_map/ppermute | solution.py:41
  96.9 37.4 %collective-permute-start.32 = (bf16[256,1408]{1,0:T(8,128)(2,1)}, bf16[256,1408]{1,0:T(8,128)(2,1)}, u32[]{:S(2)}, u32[]{:S(2)}) collective-permute-start(bf16[256,1408]{1,0:T(8,128)(2,1)} %constant_dynamic-update-slice_fusion.refs_9_), channel_id=1, source_target_pairs={{0,8},{8,16},{16,24},{24,0},{32,40},{40,48},{48,56},{56,32},{64,72... | collective-permute-start | bytes 2162696 | tf_op jit(solution)/shard_map/ppermute | solution.py:41
  102.7 31.6 %collective-permute-start.33 = (bf16[256,1408]{1,0:T(8,128)(2,1)}, bf16[256,1408]{1,0:T(8,128)(2,1)}, u32[]{:S(2)}, u32[]{:S(2)}) collective-permute-start(bf16[256,1408]{1,0:T(8,128)(2,1)} %constant_dynamic-update-slice_fusion.refs_9_), channel_id=1, source_target_pairs={{0,16},{8,24},{16,0},{24,8},{32,48},{40,56},{48,32},{56,40},{64,80... | collective-permute-start | bytes 2162696 | tf_op jit(solution)/shard_map/ppermute | solution.py:41
  104.6 41.7 %collective-permute-start.34 = (bf16[256,1408]{1,0:T(8,128)(2,1)}, bf16[256,1408]{1,0:T(8,128)(2,1)}, u32[]{:S(2)}, u32[]{:S(2)}) collective-permute-start(bf16[256,1408]{1,0:T(8,128)(2,1)} %constant_dynamic-update-slice_fusion.refs_9_), channel_id=1, source_target_pairs={{0,24},{8,0},{16,8},{24,16},{32,56},{40,32},{48,40},{56,48},{64,88... | collective-permute-start | bytes 2162696 | tf_op jit(solution)/shard_map/ppermute | solution.py:41
  107.2 40.5 %all-to-all-start = ((bf16[8,24,2048]{2,1,0:T(8,128)(2,1)}), bf16[8,24,2048]{2,1,0:T(8,128)(2,1)S(1)}, u32[]{:S(2)}, u32[]{:S(2)}) async-start(bf16[8,24,2048]{2,1,0:T(8,128)(2,1)} %bitcast.12), calls=%async_computation | async-start | bytes 1572864 | tf_op jit(solution)/shard_map/all_to_all | solution.py:377
  110.8 20.0 %collective-permute-start.26 = (bf16[128,1408]{1,0:T(8,128)(2,1)S(1)}, bf16[128,1408]{1,0:T(8,128)(2,1)S(1)}, u32[]{:S(2)}, u32[]{:S(2)}) collective-permute-start(bf16[128,1408]{1,0:T(8,128)(2,1)S(1)} %collective-permute-done.24.refs_3_), channel_id=1, source_target_pairs={{0,32},{8,40},{16,48},{24,56},{32,64},{40,72},{48,80},{56,88},{64,... | collective-permute-start | bytes 1081352 | tf_op jit(solution)/shard_map/ppermute | solution.py:41
  111.5 19.5 %collective-permute-start.27 = (bf16[128,1408]{1,0:T(8,128)(2,1)}, bf16[128,1408]{1,0:T(8,128)(2,1)S(1)}, u32[]{:S(2)}, u32[]{:S(2)}) collective-permute-start(bf16[128,1408]{1,0:T(8,128)(2,1)} %collective-permute-done.25.refs_4_), channel_id=1, source_target_pairs={{0,224},{8,232},{16,240},{24,248},{32,0},{40,8},{48,16},{56,24},{6... | collective-permute-start | bytes 1081352 | tf_op jit(solution)/shard_map/ppermute | solution.py:41
  130.9 15.5 %collective-permute-start.28 = (bf16[64,1408]{1,0:T(8,128)(2,1)S(1)}, bf16[64,1408]{1,0:T(8,128)(2,1)S(1)}, u32[]{:S(2)}, u32[]{:S(2)}) collective-permute-start(bf16[64,1408]{1,0:T(8,128)(2,1)S(1)} %slice.46), channel_id=1, source_target_pairs={{0,32},{8,40},{16,48},{24,56},{32,64},{40,72},{48,80},{56,88},{64,... | collective-permute-start | bytes 540680 | tf_op jit(solution)/shard_map/ppermute | solution.py:41
  131.0 16.0 %collective-permute-start.29 = (bf16[64,1408]{1,0:T(8,128)(2,1)S(1)}, bf16[64,1408]{1,0:T(8,128)(2,1)S(1)}, u32[]{:S(2)}, u32[]{:S(2)}) collective-permute-start(bf16[64,1408]{1,0:T(8,128)(2,1)S(1)} %slice.47), channel_id=1, source_target_pairs={{0,224},{8,232},{16,240},{24,248},{32,0},{40,8},{48,16},{56,24},{6... | collective-permute-start | bytes 540680 | tf_op jit(solution)/shard_map/ppermute | solution.py:41
  174.2 8.5 %copy-start.12 = (f32[64,2]{0,1:T(2,128)S(1)}, f32[64,2]{0,1:T(2,128)}, u32[]{:S(2)}) copy-start(f32[64,2]{0,1:T(2,128)} %param.22) | copy-start | bytes 1540
  174.2 27.2 %all-to-all-start.2 = ((bf16[8,40,2048]{2,1,0:T(8,128)(2,1)}), bf16[8,40,2048]{2,1,0:T(8,128)(2,1)S(1)}, u32[]{:S(2)}, u32[]{:S(2)}) async-start(bf16[8,40,2048]{2,1,0:T(8,128)(2,1)} %bitcast.40), calls=%async_computation.2 | async-start | bytes 2621440 | tf_op jit(solution)/shard_map/all_to_all | solution.py:377
  (4 other events, 3.2 us)
Sparse Core Ops, SparseCore 0:
  10.6 142.3 all-gather.2
